TPU v7x, 32 devices: a whole 2x2x4 slice. The times are simulated.
32 devices in a mesh: seq: 8 (over z, x), chan: 4 (over y, core).
Axes of the slice: x: 2, y: 2, z: 4, core: 2. Of those that a mesh axis runs over, the one named last changes fastest.
Arguments:
- block_input: bfloat16 [8, 1024, 1024], P(None, 'seq', 'chan'), may hold values from -6 to 6
- lengths: int32 [8], replicated, may hold values from 128 to 1024, as said below
- norm1_gain: float32 [1024], P('chan'), may hold values from 0.25 to 1.75
- norm1_bias: float32 [1024], P('chan'), may hold values from -3 to 3
- a_decay: float32 [64, 1024], P(None, 'chan'), may hold values from 0.01953125 to 1
- a_freq: float32 [64, 1024], P(None, 'chan'), may hold values from 0 to 10
- b_state: float32 [2, 64, 1024], P(None, None, 'chan'), may hold values from -6 to 6
- c_state: float32 [2, 64, 1024], P(None, None, 'chan'), may hold values from -0.24 to 0.24
- step_size: float32 [1024], P('chan'), may hold values from 0.01 to 0.1
- skip_gain: float32 [1024], P('chan'), may hold values from -4 to 4
- w_value: bfloat16 [1024, 1024], P(None, 'chan'), may hold values from -0.1875 to 0.1875
- b_value: float32 [1024], P('chan'), may hold values from -3 to 3
- w_gate: bfloat16 [1024, 1024], P(None, 'chan'), may hold values from -0.1875 to 0.1875
- b_gate: float32 [1024], P('chan'), may hold values from -3 to 3
- norm2_gain: float32 [1024], P('chan'), may hold values from 0.25 to 1.75
- norm2_bias: float32 [1024], P('chan'), may hold values from -3 to 3
- w_up: bfloat16 [1024, 4096], P(None, 'chan'), may hold values from -0.1875 to 0.1875
- b_up: float32 [4096], P('chan'), may hold values from -3 to 3
- w_down: bfloat16 [4096, 1024], P('chan'), may hold values from -0.1875 to 0.1875
- b_down: float32 [1024], P('chan'), may hold values from -3 to 3
- out_grad: bfloat16 [8, 1024, 1024], P(None, 'seq', 'chan'), may hold values from -6 to 6
Outputs:
- output: bfloat16 [8, 1024, 1024], P(None, 'seq', 'chan')
- grad_input: float32 [8, 1024, 1024], P(None, 'seq', 'chan')
- grad_norm1_gain: float32 [1024], P('chan')
- grad_norm1_bias: float32 [1024], P('chan')
- grad_a_decay: float32 [64, 1024], P(None, 'chan')
- grad_a_freq: float32 [64, 1024], P(None, 'chan')
- grad_b_state: float32 [2, 64, 1024], P(None, None, 'chan')
- grad_c_state: float32 [2, 64, 1024], P(None, None, 'chan')
- grad_step_size: float32 [1024], P('chan')
- grad_skip_gain: float32 [1024], P('chan')
- grad_w_value: float32 [1024, 1024], P(None, 'chan')
- grad_b_value: float32 [1024], P('chan')
- grad_w_gate: float32 [1024, 1024], P(None, 'chan')
- grad_b_gate: float32 [1024], P('chan')
- grad_norm2_gain: float32 [1024], P('chan')
- grad_norm2_bias: float32 [1024], P('chan')
- grad_w_up: float32 [1024, 4096], P(None, 'chan')
- grad_b_up: float32 [4096], P('chan')
- grad_w_down: float32 [4096, 1024], P('chan')
- grad_b_down: float32 [1024], P('chan')
Inputs may be any that keep to these rules, and one draw needn't show every extreme that they name: One sequence, chosen by the seed, has length 1024; lengths have a heavy tail toward 128.
All inputs are finite; a program needn't handle non-finite values.
Results may differ from a plain program's by a relative error of at most 0.008.
Values may be sent and summed in bfloat16 or wider, within the bound.
No kernel may reach another device: no remote copies, remote signals or barrier semaphores. Data moves between devices by JAX's collectives and lax.ppermute only.
A program may use at most 512 MiB of HBM per device.

v0:
```python
import math

import jax
import jax.numpy as jnp
from jax import lax
from jax.sharding import PartitionSpec as P

D = 1024


EPSILON = 1e-05


def s4_tables(decay, freq, b_state, c_state, step_size, length):
    rate = step_size * decay
    turn = step_size * freq
    half_turn = jnp.sin(0.5 * turn)
    less_re = jnp.expm1(-rate) * jnp.cos(turn) - 2.0 * half_turn * half_turn
    less_im = jnp.exp(-rate) * jnp.sin(turn)
    modulus = decay * decay + freq * freq
    ratio_re = (freq * less_im - decay * less_re) / modulus
    ratio_im = -(decay * less_im + freq * less_re) / modulus
    input_re = ratio_re * b_state[0] - ratio_im * b_state[1]
    input_im = ratio_re * b_state[1] + ratio_im * b_state[0]
    counts = jnp.arange(length + 1, dtype=jnp.float32)[:, None, None]
    damping = jnp.exp(-rate * counts)
    power_re = damping * jnp.cos(turn * counts)
    power_im = damping * jnp.sin(turn * counts)
    return (input_re, input_im, power_re, power_im, c_state[0], c_state[1])


def s4_out(signal, state_re, state_im, tables, skip_gain):
    input_re, input_im, power_re, power_im, out_re, out_im = tables
    length = signal.shape[1]
    weight_re = out_re * input_re - out_im * input_im
    weight_im = out_re * input_im + out_im * input_re
    kernel = 2.0 * jnp.sum(weight_re * power_re[:length] - weight_im * power_im[:length], axis=1)
    places = jnp.arange(length, dtype=jnp.int32)
    lags = places[:, None] - places[None, :]
    toeplitz = jnp.where((lags >= 0)[:, :, None], kernel[jnp.maximum(lags, 0)], 0.0)
    local = jnp.einsum("tsh,bsh->bth", toeplitz, signal, precision=lax.Precision.HIGHEST)
    read_re = out_re * power_re[1:] - out_im * power_im[1:]
    read_im = out_re * power_im[1:] + out_im * power_re[1:]
    carried = jnp.einsum("tnh,bnh->bth", read_re, state_re, precision=lax.Precision.HIGHEST)
    carried = carried - jnp.einsum(
        "tnh,bnh->bth", read_im, state_im, precision=lax.Precision.HIGHEST
    )
    return local + 2.0 * carried + skip_gain * signal


def s4_end(signal, tables):
    input_re, input_im, power_re, power_im, out_re, out_im = tables
    length = signal.shape[1]
    flip_re = power_re[:length][::-1]
    flip_im = power_im[:length][::-1]
    write_re = input_re * flip_re - input_im * flip_im
    write_im = input_re * flip_im + input_im * flip_re
    end_re = jnp.einsum("snh,bsh->bnh", write_re, signal, precision=lax.Precision.HIGHEST)
    end_im = jnp.einsum("snh,bsh->bnh", write_im, signal, precision=lax.Precision.HIGHEST)
    return (end_re, end_im, power_re[length], power_im[length])


def s4_block(signal, state_re, state_im, decay, freq, b_state, c_state, step_size, skip_gain):
    tables = s4_tables(decay, freq, b_state, c_state, step_size, signal.shape[1])
    end_re, end_im, carry_re, carry_im = s4_end(signal, tables)
    return (
        s4_out(signal, state_re, state_im, tables, skip_gain),
        end_re,
        end_im,
        carry_re,
        carry_im,
    )


def power_rows(offsets, tables, bits):
    power_re, power_im = (tables[2], tables[3])
    length = power_re.shape[0] - 1
    remainder = offsets % length
    multiple = offsets // length
    result_re = power_re[remainder]
    result_im = power_im[remainder]
    stride_re = power_re[length]
    stride_im = power_im[length]
    for level in range(bits):
        chosen = (multiple // 2**level % 2 == 1)[:, None, None]
        moved_re = result_re * stride_re - result_im * stride_im
        moved_im = result_re * stride_im + result_im * stride_re
        result_re = jnp.where(chosen, moved_re, result_re)
        result_im = jnp.where(chosen, moved_im, result_im)
        stride_re, stride_im = (
            stride_re * stride_re - stride_im * stride_im,
            2.0 * stride_re * stride_im,
        )
    return (result_re, result_im)


def fold_blocks(piece, block, begin, tables, bits, mirror):
    batch, rows, width_h = piece.shape
    width = math.gcd(rows, block)
    count = rows // width
    parts = piece.reshape(batch, count, width, width_h).astype(jnp.float32)
    power_re, power_im = (tables[2], tables[3])
    firsts = width * jnp.arange(count, dtype=jnp.int32)
    if mirror:
        read_re = tables[4] * power_re[1 : width + 1] - tables[5] * power_im[1 : width + 1]
        read_im = tables[4] * power_im[1 : width + 1] + tables[5] * power_re[1 : width + 1]
        sum_re = 2.0 * jnp.einsum("pnh,bkph->bknh", read_re, parts, precision=lax.Precision.HIGHEST)
        sum_im = -2.0 * jnp.einsum(
            "pnh,bkph->bknh", read_im, parts, precision=lax.Precision.HIGHEST
        )
        gaps = firsts - begin - block
    else:
        flip_re = power_re[:width][::-1]
        flip_im = power_im[:width][::-1]
        write_re = tables[0] * flip_re - tables[1] * flip_im
        write_im = tables[0] * flip_im + tables[1] * flip_re
        sum_re = jnp.einsum("pnh,bkph->bknh", write_re, parts, precision=lax.Precision.HIGHEST)
        sum_im = jnp.einsum("pnh,bkph->bknh", write_im, parts, precision=lax.Precision.HIGHEST)
        gaps = begin - firsts - width
    live = (gaps >= 0).astype(jnp.float32)[:, None, None]
    move_re, move_im = power_rows(jnp.maximum(gaps, 0), tables, bits)
    move_re = live * move_re
    move_im = live * move_im
    if mirror:
        new_re = sum_re * move_re + sum_im * move_im
        new_im = sum_im * move_re - sum_re * move_im
    else:
        new_re = sum_re * move_re - sum_im * move_im
        new_im = sum_re * move_im + sum_im * move_re
    return (jnp.sum(new_re, axis=1), jnp.sum(new_im, axis=1))


def layer_forward(values, gain, bias):
    totals, squares = lax.psum(
        (jnp.sum(values, axis=-1), jnp.sum(values * values, axis=-1)), "chan"
    )
    center = totals / D
    spread_var = squares / D - center * center
    inverse = lax.rsqrt(spread_var + EPSILON)[..., None]
    normed = (values - center[..., None]) * inverse
    return (normed * gain + bias, normed, inverse)


def layer_backward(grad_out, normed, inverse, gain):
    scaled = grad_out * gain
    totals, crossed = lax.psum(
        (jnp.sum(scaled, axis=-1), jnp.sum(scaled * normed, axis=-1)), "chan"
    )
    grad_in = inverse * (scaled - totals[..., None] / D - normed * crossed[..., None] / D)
    return (grad_in, jnp.sum(grad_out * normed, axis=(0, 1)), jnp.sum(grad_out, axis=(0, 1)))


def project(acts, weight):
    return jnp.einsum("bld,de->ble", acts, weight, preferred_element_type=jnp.float32)


def project_back(grads, weight):
    return jnp.einsum("ble,de->bld", grads, weight, preferred_element_type=jnp.float32)


def weight_grad(acts, grads):
    return jnp.einsum("bld,ble->de", acts, grads, preferred_element_type=jnp.float32)


def body(
    block_input,
    lengths,
    norm1_gain,
    norm1_bias,
    a_decay,
    a_freq,
    b_state,
    c_state,
    step_size,
    skip_gain,
    w_value,
    b_value,
    w_gate,
    b_gate,
    norm2_gain,
    norm2_bias,
    w_up,
    b_up,
    w_down,
    b_down,
    out_grad,
):
    batch, block, local_width = block_input.shape
    begin = lax.axis_index("seq") * block
    places = begin + jnp.arange(block, dtype=jnp.int32)
    mask = (places[None, :] < lengths[:, None]).astype(jnp.float32)[..., None]
    bits = max((lax.axis_size("seq") - 1).bit_length(), 1)
    inputs = block_input.astype(jnp.float32)
    norm_one, normed_one, inverse_one = layer_forward(inputs, norm1_gain, norm1_bias)
    signal_low = (mask * norm_one).astype(jnp.bfloat16)
    signal = signal_low.astype(jnp.float32)
    tables = s4_tables(a_decay, a_freq, b_state, c_state, step_size, block)
    state_re, state_im = fold_blocks(
        lax.all_gather(signal_low, "seq", axis=1, tiled=True), block, begin, tables, bits, False
    )
    mixed = s4_out(signal, state_re, state_im, tables, skip_gain)
    activ_low = jax.nn.gelu(mixed).astype(jnp.bfloat16)
    activ_full = lax.all_gather(activ_low, "chan", axis=2, tiled=True)
    value = project(activ_full, w_value) + b_value
    gate = project(activ_full, w_gate) + b_gate
    opened = jax.nn.sigmoid(gate)
    resid = inputs + value * opened
    norm_two, normed_two, inverse_two = layer_forward(resid, norm2_gain, norm2_bias)
    norm_full = lax.all_gather(norm_two.astype(jnp.bfloat16), "chan", axis=2, tiled=True)
    hidden = project(norm_full, w_up) + b_up
    spread_low = jax.nn.gelu(hidden).astype(jnp.bfloat16)
    down_terms = project(spread_low, w_down)
    output = (
        resid + lax.psum_scatter(down_terms, "chan", scatter_dimension=2, tiled=True) + b_down
    ).astype(jnp.bfloat16)
    grad_out = out_grad.astype(jnp.float32)
    grad_full = lax.all_gather(out_grad, "chan", axis=2, tiled=True)
    grad_spread = project_back(grad_full, w_down)
    grad_w_down = weight_grad(spread_low, grad_full)
    grad_b_down = jnp.sum(grad_out, axis=(0, 1))
    _, gelu_pull = jax.vjp(jax.nn.gelu, hidden)
    grad_hidden = gelu_pull(grad_spread)[0].astype(jnp.bfloat16)
    grad_w_up = weight_grad(norm_full, grad_hidden)
    grad_b_up = jnp.sum(grad_hidden.astype(jnp.float32), axis=(0, 1))
    grad_norm_two = lax.psum_scatter(
        project_back(grad_hidden, w_up), "chan", scatter_dimension=2, tiled=True
    )
    grad_resid_norm, grad_norm2_gain, grad_norm2_bias = layer_backward(
        grad_norm_two, normed_two, inverse_two, norm2_gain
    )
    grad_resid = grad_out + grad_resid_norm
    grad_value = (grad_resid * opened).astype(jnp.bfloat16)
    grad_gate = (grad_resid * value * opened * (1.0 - opened)).astype(jnp.bfloat16)
    grad_w_value = weight_grad(activ_full, grad_value)
    grad_b_value = jnp.sum(grad_value.astype(jnp.float32), axis=(0, 1))
    grad_w_gate = weight_grad(activ_full, grad_gate)
    grad_b_gate = jnp.sum(grad_gate.astype(jnp.float32), axis=(0, 1))
    activ_terms = project_back(grad_value, w_value) + project_back(grad_gate, w_gate)
    grad_activ = lax.psum_scatter(activ_terms, "chan", scatter_dimension=2, tiled=True)
    _, mixed_pull = jax.vjp(jax.nn.gelu, mixed)
    grad_mixed_low = mixed_pull(grad_activ)[0].astype(jnp.bfloat16)
    grad_mixed = grad_mixed_low.astype(jnp.float32)
    later_re, later_im = fold_blocks(
        lax.all_gather(grad_mixed_low, "seq", axis=1, tiled=True), block, begin, tables, bits, True
    )
    grad_carry_re = jnp.sum(later_re * state_re + later_im * state_im, axis=0)
    grad_carry_im = jnp.sum(later_im * state_re - later_re * state_im, axis=0)
    _, s4_pull = jax.vjp(
        s4_block,
        signal,
        state_re,
        state_im,
        a_decay,
        a_freq,
        b_state,
        c_state,
        step_size,
        skip_gain,
    )
    pulled = s4_pull((grad_mixed, later_re, later_im, grad_carry_re, grad_carry_im))
    grad_signal = pulled[0]
    grad_input_norm, grad_norm1_gain, grad_norm1_bias = layer_backward(
        grad_signal * mask, normed_one, inverse_one, norm1_gain
    )
    grad_input = grad_resid + grad_input_norm
    summed = lax.psum(
        (
            grad_norm1_gain,
            grad_norm1_bias,
            pulled[3],
            pulled[4],
            pulled[5],
            pulled[6],
            pulled[7],
            pulled[8],
            grad_w_value,
            grad_b_value,
            grad_w_gate,
            grad_b_gate,
            grad_norm2_gain,
            grad_norm2_bias,
            grad_w_up,
            grad_b_up,
            grad_w_down,
            grad_b_down,
        ),
        "seq",
    )
    return (
        output,
        grad_input,
        summed[0],
        summed[1],
        summed[2],
        summed[3],
        summed[4],
        summed[5],
        summed[6],
        summed[7],
        summed[8],
        summed[9],
        summed[10],
        summed[11],
        summed[12],
        summed[13],
        summed[14],
        summed[15],
        summed[16],
        summed[17],
    )


def solution(mesh):
    in_specs = (
        P(None, "seq", "chan"),
        P(),
        P("chan"),
        P("chan"),
        P(None, "chan"),
        P(None, "chan"),
        P(None, None, "chan"),
        P(None, None, "chan"),
        P("chan"),
        P("chan"),
        P(None, "chan"),
        P("chan"),
        P(None, "chan"),
        P("chan"),
        P("chan"),
        P("chan"),
        P(None, "chan"),
        P("chan"),
        P("chan", None),
        P("chan"),
        P(None, "seq", "chan"),
    )
    out_specs = (
        P(None, "seq", "chan"),
        P(None, "seq", "chan"),
        P("chan"),
        P("chan"),
        P(None, "chan"),
        P(None, "chan"),
        P(None, None, "chan"),
        P(None, None, "chan"),
        P("chan"),
        P("chan"),
        P(None, "chan"),
        P("chan"),
        P(None, "chan"),
        P("chan"),
        P("chan"),
        P("chan"),
        P(None, "chan"),
        P("chan"),
        P("chan", None),
        P("chan"),
    )
    return jax.shard_map(body, mesh=mesh, in_specs=in_specs, out_specs=out_specs, check_vma=False)
```

profile of v0, /device:TPU:0, one launch (start us, length us, event | category | flops | bytes accessed | tf_op | source)
XLA Modules:
  0.0 1373.3 jit_solution(16042081612488545159)
XLA Ops:
  9.1 8.5 all-reduce.21
  23.6 32.1 %fusion.6 = (f32[129,64,256]{2,1,0:T(8,128)}, f32[129,64,256]{2,1,0:T(8,128)}) fusion(f32[64,256]{1,0:T(8,128)S(1)} %get-tuple-element.233, f32[64,256]{1,0:T(8,128)S(1)} %get-tuple-element.232), kind=kLoop, calls=%fused_computation.19 | loop fusion | flops 8454144 | bytes 17039360 | tf_op jit(solution)/shard_map/mul | solution.py:27
  75.4 24.6 %multiply_add_fusion = (f32[128,64,256]{2,1,0:T(8,128)}, f32[128,64,256]{2,1,0:T(8,128)}, f32[128,256]{1,0:T(8,128)S(1)}, f32[128,64,256]{2,1,0:T(8,128)}, f32[128,64,256]{2,1,0:T(8,128)}) fusion(f32[129,64,256]{2,1,0:T(8,128)} %get-tuple-element.231, f32[129,64,256]{2,1,0:T(8,128)} %get-tuple-element.230, f32[64,256]{1,0:T(8,128)S(1)} %get-tuple-element.229, ...), kind=kLoop, calls=%fused_computation.64 | loop fusion | flops 20938752 | bytes 67502080 | tf_op jit(solution)/shard_map/add | solution.py:43
  100.0 62.0 %gather_fusion = f32[16384,256]{1,0:T(8,128)} fusion(f32[128,256]{1,0:T(8,128)S(1)} %broadcast_multiply_fusion.7, s32[16384]{0:T(1024)S(1)} %broadcast_clamp_fusion), kind=kCustom, calls=%fused_computation | custom fusion | bytes 33619968 | tf_op jit(solution)/shard_map/gather | solution.py:40
  162.0 18.1 %copy.218 = f32[128,128,256]{1,0,2:T(8,128)} copy(f32[128,128,256]{2,1,0:T(8,128)} %bitcast.281) | data formatting | bytes 33554432 | tf_op jit(solution)/shard_map/gather | solution.py:40
  180.1 11.4 multiply_subtract_fusion.1
  191.5 8.8 copy.295
  208.3 8.9 copy.296
  217.2 8.9 copy.225
  226.1 8.9 copy.226
  235.0 17.0 %fusion.2 = f32[256,8,128]{2,1,0:T(8,128)} fusion(bf16[8,128,256]{1,0,2:T(8,128)(2,1)S(1)} %copy-done.5, f32[128,128,256]{1,0,2:T(8,128)} %copy.218, pred[128,128]{1,0:T(8,128)(4,1)S(1)} %subtract_compare_fusion), kind=kOutput, calls=%fused_computation.9 | convolution fusion | flops 406847488 | bytes 18366464 | tf_op jit(solution)/shard_map/tsh,bsh->bth/dot_general | solution.py:41
  252.0 14.7 %fusion.42 = f32[256,8,8,64]{3,2,1,0:T(8,128)} fusion(f32[128,64,256,1]{0,1,3,2:T(8,128)} %copy.295, bf16[8,8,128,256]{2,0,1,3:T(8,128)(2,1)} %bitcast.283), kind=kOutput, calls=%fused_computation.93 | convolution fusion | flops 1610612736 | bytes 16777216 | tf_op jit(solution)/shard_map/pnh,bkph->bknh/dot_general | solution.py:117
  266.8 17.0 %fusion.23 = (f32[8,64,256]{1,0,2:T(8,128)S(1)}, f32[8,64,256]{1,0,2:T(8,128)S(1)}) fusion(f32[256,8,8,64]{3,2,1,0:T(8,128)} %fusion.42, f32[8,64,256]{1,0,2:T(8,128)} %copy.224, f32[8,64,256]{1,0,2:T(8,128)} %copy.221, f32[128,64,256,1]{0,1,3,2:T(8,128)} %copy.296, bf16[8,8,128,256]{2,0,1,3:T(8,128)(2,1)S(1)} %bitcast.284), kind=kOutput, calls=%fused_computation.57 | convolution fusion | flops 1618739200 | bytes 18874368 | tf_op jit(solution)/shard_map/pnh,bkph->bknh/dot_general | solution.py:118
  283.8 10.3 fusion.160
  294.1 10.9 multiply_convert_fusion.3
  305.1 23.0 %all-gather.8.cloned.1.call-done = bf16[8,128,1024]{1,0,2:T(8,128)(2,1)} async-done(((bf16[8,128,256]{1,0,2:T(8,128)(2,1)}), bf16[8,128,1024]{1,0,2:T(8,128)(2,1)}) %all-gather.8.cloned.1.call-update) | async-done | bytes 2097168 | tf_op jit(solution)/shard_map/all_gather | solution.py:203
  352.4 23.2 %all-gather.10.cloned.1.call-done = bf16[8,128,1024]{1,0,2:T(8,128)(2,1)} async-done(((bf16[8,128,256]{1,0,2:T(8,128)(2,1)}), bf16[8,128,1024]{1,0,2:T(8,128)(2,1)}) %all-gather.10.cloned.1.call-update) | async-done | bytes 2097168 | tf_op jit(solution)/shard_map/all_gather | solution.py:209
  382.2 17.7 %all-gather.12.cloned.1.call-done = bf16[8,128,1024]{2,1,0:T(8,128)(2,1)} async-done(((bf16[8,128,256]{2,1,0:T(8,128)(2,1)}), bf16[8,128,1024]{2,1,0:T(8,128)(2,1)}) %all-gather.12.cloned.1.call-update) | async-done | bytes 2097168 | tf_op jit(solution)/shard_map/all_gather | solution.py:217
  399.9 8.2 convert_reduce_fusion
  435.0 28.9 %reduce-scatter.6.cloned.1.call-done = f32[8,128,256]{1,0,2:T(8,128)} async-done(((f32[8,128,1024]{1,0,2:T(8,128)}), f32[8,128,256]{1,0,2:T(8,128)}) %reduce-scatter.6.cloned.1.call-update) | async-done | bytes 1048592 | tf_op jit(solution)/shard_map/reduce_scatter | solution.py:225
  473.6 37.3 %reduce-scatter.4.cloned.1.call-done = f32[8,128,256]{1,0,2:T(8,128)} async-done(((f32[8,128,1024]{1,0,2:T(8,128)}), f32[8,128,256]{1,0,2:T(8,128)}) %reduce-scatter.4.cloned.1.call-update) | async-done | bytes 1048592 | tf_op jit(solution)/shard_map/reduce_scatter | solution.py:214
  511.0 10.6 convert_reduce_fusion.3
  550.1 44.6 %reduce-scatter.8.cloned.1.call-done = f32[8,128,256]{1,0,2:T(8,128)} async-done(((f32[8,128,1024]{1,0,2:T(8,128)}), f32[8,128,256]{1,0,2:T(8,128)}) %reduce-scatter.8.cloned.1.call-update) | async-done | bytes 1048592 | tf_op jit(solution)/shard_map/reduce_scatter | solution.py:239
  601.3 9.3 copy.297
  618.2 9.1 copy.298
  642.2 15.8 %fusion.75 = f32[256,128,64]{1,2,0:T(8,128)} fusion(f32[8,64,256]{1,0,2:T(8,128)S(1)} %copy-done.13, bf16[8,128,256]{1,0,2:T(8,128)(2,1)S(1)} %copy-done.6), kind=kOutput, calls=%fused_computation.141 | convolution fusion | flops 202113024 | bytes 9437184 | tf_op jit(solution)/shard_map/transpose(jvp(tnh,bnh->bth))/dot_general | solution.py:45
  658.0 9.3 copy.266
  674.4 17.8 %copy.308 = f32[128,128,256]{2,1,0:T(8,128)} copy(f32[128,128,256]{1,0,2:T(8,128)} %select_bitcast_fusion) | data formatting | bytes 33554432 | tf_op jit(solution)/shard_map/transpose(jvp(jit(_where)))/select_n | solution.py:40
  692.2 15.5 %fusion.77 = f32[256,128,64]{1,2,0:T(8,128)} fusion(f32[8,64,256]{1,0,2:T(8,128)S(1)} %copy-done.8, bf16[8,128,256]{1,0,2:T(8,128)(2,1)S(1)} %copy-done.6), kind=kOutput, calls=%fused_computation.142 | convolution fusion | flops 201850880 | bytes 9437184 | tf_op jit(solution)/shard_map/transpose(jvp(tnh,bnh->bth))/dot_general | solution.py:44
  707.8 9.3 copy.267
  717.1 98.6 %scatter_custom_fusion = f32[128,256]{1,0:T(8,128)S(1)} fusion(s32[16384]{0:T(1024)} %maximum_bitcast_fusion, f32[16384,256]{1,0:T(8,128)} %bitcast.282, f32[]{:T(128)} %constant.180.clone.1), kind=kCustom, calls=%fused_computation.254 | custom fusion | flops 4194304 | bytes 131584 | tf_op jit(solution)/shard_map/transpose(jvp())/scatter-add | solution.py:40
  815.8 35.2 %fusion.9 = (f32[64,256]{1,0:T(8,128)S(1)}, f32[64,256]{1,0:T(8,128)S(1)}, f32[64,256]{1,0:T(8,128)}, f32[64,256]{1,0:T(8,128)}, f32[64,256]{1,0:T(8,128)}, /*in...) fusion(f32[256,128,64]{0,2,1:T(8,128)} %copy.266, ...), kind=kLoop, calls=%fused_computation.30 | loop fusion | flops 39747584 | bytes 101580800 | tf_op jit(solution)/shard_map/transpose(jvp())/reduce_sum | solution.py:43
  851.1 14.6 %fusion.38 = f32[256,8,8,64]{3,2,1,0:T(8,128)} fusion(f32[128,64,256,1]{0,1,3,2:T(8,128)} %copy.297, bf16[8,8,128,256]{2,0,1,3:T(8,128)(2,1)} %bitcast.285), kind=kOutput, calls=%fused_computation.89 | convolution fusion | flops 1610612736 | bytes 16777216 | tf_op jit(solution)/shard_map/pnh,bkph->bknh/dot_general | solution.py:108
  865.6 17.9 %fusion.17 = (f32[8,64,256]{1,0,2:T(8,128)S(1)}, f32[8,64,256]{1,0,2:T(8,128)S(1)}) fusion(f32[256,8,8,64]{3,2,1,0:T(8,128)} %fusion.38, f32[8,64,256]{1,0,2:T(8,128)S(1)} %copy-done.24, f32[8,64,256]{1,0,2:T(8,128)} %copy.241, f32[8,64,256]{1,0,2:T(8,128)} %copy.247, f32[8,64,256]{1,0,2:T(8,128)} %copy.246, f32[128,64,256,1]{0,1,3,2:T(8,128)} %copy.298, ...), kind=kOutput, calls=%fused_computation.47 | convolution fusion | flops 1618739200 | bytes 19922944 | tf_op jit(solution)/shard_map/pnh,bkph->bknh/dot_general | solution.py:107
  883.6 9.0 fusion.105
  892.6 9.1 fusion.102
  902.5 9.3 copy.254
  911.7 9.3 copy.257
  921.1 18.7 %fusion.14 = (f32[64,256]{1,0:T(8,128)S(1)}, f32[64,256]{1,0:T(8,128)S(1)}, f32[64,256]{1,0:T(8,128)S(1)}, f32[64,256]{1,0:T(8,128)S(1)}, f32[128,64,256]{2,1,0:T(8,128)}, /*index=5*/f32[128,64,256]{2,1,0:T(8,128)}) fusion(f32[256,64,128]{0,1,2:T(8,128)} %copy.254, f32[128,64,256]{2,1,0:T(8,128)} %get-tuple-element.199, f32[256,64,128]{0,1,2:T(8,128)} %copy.257, ...), kind=kLoop, calls=%fused_computation.42 | loop fusion | flops 31391744 | bytes 50724864 | tf_op jit(solution)/shard_map/transpose(jvp())/reduce_sum | solution.py:57
  947.6 7.9 rev.16
  956.4 45.4 %multiply_reduce_fusion = (f32[64,256]{1,0:T(8,128)S(1)}, f32[64,256]{1,0:T(8,128)S(1)}, f32[64,256]{1,0:T(8,128)S(1)}) fusion(f32[64,256]{1,0:T(8,128)S(1)} %copy-done.47, f32[64,256]{1,0:T(8,128)S(1)} %copy-done.45, f32[128,64,256]{2,1,0:T(8,128)} %rev.17, f32[1,64,256]{2,1,0:T(8,128)S(1)} %bitcast.287, f32[128,64,256]{2,1,0:T(8,128)} %get-tuple-element.225, ...), kind=kLoop, calls=%fused_computation.11 | loop fusion | flops 52789248 | bytes 67567616 | tf_op jit(solution)/shard_map/transpose(jvp())/reduce_sum | solution.py:27
  1005.1 9.5 copy.248
  1014.6 8.9 copy.245
  1024.7 11.3 fusion.69
  1036.1 9.9 convolution_bitcast_fusion.4
  1046.2 8.8 fusion.100
  1064.2 39.1 %all-reduce.16 = (f32[256]{0:T(256)}, f32[256]{0:T(256)}, f32[256]{0:T(256)}, f32[256]{0:T(256)}, f32[256]{0:T(256)}, /*index=5*/f32[256]{0:T(256)}, f32[256]{0:...) all-reduce(f32[256]{0:T(256)S(1)} %get-tuple-element.124, ...), channel_id=1, replica_groups=mesh['seq'=8,'chan'=4] {'seq'}, use_global_device_ids=true, to_apply=%region_25.26 | all-reduce | flops 3328 | bytes 26624 | tf_op jit(solution)/shard_map/psum | solution.py:266
  1103.3 245.3 %all-reduce.24.cloned.1.call-done = (f32[64,256]{1,0:T(8,128)}, f32[64,256]{1,0:T(8,128)}, f32[2,64,256]{2,1,0:T(8,128)}, f32[2,64,256]{2,1,0:T(8,128)}, f32[102...) async-done(((f32[64,256]{1,0:T(8,128)}, f32[64,256]{1,0:T(8,128)}, f32[2,64,256]{2,1,0:T(8,128)}, f32[2,64,256]{2,1,0:T(8,128)}, ...) | async-done | bytes 10878992 | tf_op jit(solution)/shard_map/psum | solution.py:266
  (298 shorter events, 208.2 us)
Async XLA Ops:
  7.2 392.7 %copy-start = (bf16[1024,1024]{1,0:T(8,128)(2,1)S(1)}, bf16[1024,1024]{1,0:T(8,128)(2,1)}, u32[]{:S(2)}) copy-start(bf16[1024,1024]{1,0:T(8,128)(2,1)} %param.39) | copy-start | bytes 6291460
  7.2 244.8 %all-gather.6.cloned.1.call-start = ((), (), s32[]{:S(2)}) async-start(), calls=%async_computation.3 | async-start | bytes 4718592 | tf_op jit(solution)/shard_map/all_gather | solution.py:199
  8.8 585.9 %copy-start.3 = (bf16[8,128,256]{1,0,2:T(8,128)(2,1)}, bf16[8,128,256]{1,0,2:T(8,128)(2,1)S(1)}, u32[]{:S(2)}) copy-start(bf16[8,128,256]{1,0,2:T(8,128)(2,1)S(1)} %copy.215) | copy-start | bytes 1572868
  21.3 306.8 %all-gather.8.cloned.1.call-start = ((), (), s32[]{:S(2)}) async-start(), calls=%async_computation.4 | async-start | bytes 2621440 | tf_op jit(solution)/shard_map/all_gather | solution.py:203
  23.5 32.2 %copy-start.44 = (f32[64,256]{1,0:T(8,128)}, f32[64,256]{1,0:T(8,128)S(1)}, u32[]{:S(2)}) copy-start(f32[64,256]{1,0:T(8,128)S(1)} %get-tuple-element.232) | copy-start | bytes 196612
  23.5 32.2 %copy-start.46 = (f32[64,256]{1,0:T(8,128)}, f32[64,256]{1,0:T(8,128)S(1)}, u32[]{:S(2)}) copy-start(f32[64,256]{1,0:T(8,128)S(1)} %get-tuple-element.233) | copy-start | bytes 196612
  23.5 51.8 %copy-start.56 = (f32[64,256]{1,0:T(8,128)}, f32[64,256]{1,0:T(8,128)S(1)}, u32[]{:S(2)}) copy-start(f32[64,256]{1,0:T(8,128)S(1)} %get-tuple-element.180) | copy-start | bytes 196612
  23.5 156.6 %copy-start.40 = (f32[64,256]{1,0:T(8,128)}, f32[64,256]{1,0:T(8,128)S(1)}, u32[]{:S(2)}) copy-start(f32[64,256]{1,0:T(8,128)S(1)} %get-tuple-element.181) | copy-start | bytes 196612
  23.6 156.6 %copy-start.42 = (f32[64,256]{1,0:T(8,128)}, f32[64,256]{1,0:T(8,128)S(1)}, u32[]{:S(2)}) copy-start(f32[64,256]{1,0:T(8,128)S(1)} %get-tuple-element.182) | copy-start | bytes 196612
  23.6 51.7 %copy-start.38 = (f32[2,64,256]{2,1,0:T(8,128)S(1)}, f32[2,64,256]{2,1,0:T(8,128)}, u32[]{:S(2)}) copy-start(f32[2,64,256]{2,1,0:T(8,128)} %param.28) | copy-start | bytes 393220
  75.3 24.6 %copy-start.52 = (f32[64,256]{1,0:T(8,128)}, f32[64,256]{1,0:T(8,128)S(1)}, u32[]{:S(2)}) copy-start(f32[64,256]{1,0:T(8,128)S(1)} %get-tuple-element.228) | copy-start | bytes 196612
  75.3 24.6 %copy-start.54 = (f32[64,256]{1,0:T(8,128)}, f32[64,256]{1,0:T(8,128)S(1)}, u32[]{:S(2)}) copy-start(f32[64,256]{1,0:T(8,128)S(1)} %get-tuple-element.229) | copy-start | bytes 196612
  75.4 24.6 %copy-start.50 = (f32[64,256]{1,0:T(8,128)}, f32[64,256]{1,0:T(8,128)S(1)}, u32[]{:S(2)}) copy-start(f32[64,256]{1,0:T(8,128)S(1)} %multiply_add_fusion.4) | copy-start | bytes 196612
  283.8 21.2 %copy-start.7 = (f32[8,64,256]{1,0,2:T(8,128)}, f32[8,64,256]{1,0,2:T(8,128)S(1)}, u32[]{:S(2)}) copy-start(f32[8,64,256]{1,0,2:T(8,128)S(1)} %get-tuple-element.101) | copy-start | bytes 1572868
  283.8 21.2 %copy-start.12 = (f32[8,64,256]{1,0,2:T(8,128)}, f32[8,64,256]{1,0,2:T(8,128)S(1)}, u32[]{:S(2)}) copy-start(f32[8,64,256]{1,0,2:T(8,128)S(1)} %get-tuple-element.100) | copy-start | bytes 1572868
  304.9 35.0 %copy-start.77 = (f32[256]{0:T(256)S(1)}, f32[256]{0:T(256)}, u32[]{:S(2)}) copy-start(f32[256]{0:T(256)} %param.34) | copy-start | bytes 3076
  305.0 35.0 %copy-start.81 = (f32[256]{0:T(256)S(1)}, f32[256]{0:T(256)}, u32[]{:S(2)}) copy-start(f32[256]{0:T(256)} %param.32) | copy-start | bytes 3076
  305.0 44.1 %copy-start.76 = (f32[256]{0:T(256)S(1)}, f32[256]{0:T(256)}, u32[]{:S(2)}) copy-start(f32[256]{0:T(256)} %param.35) | copy-start | bytes 3076
  305.0 44.1 %copy-start.90 = (f32[256]{0:T(256)S(1)}, f32[256]{0:T(256)}, u32[]{:S(2)}) copy-start(f32[256]{0:T(256)} %param.36) | copy-start | bytes 3076
  305.0 70.6 %all-gather.10.cloned.1.call-start = ((), (), s32[]{:S(2)}) async-start(), calls=%async_computation.5 | async-start | bytes 2621440 | tf_op jit(solution)/shard_map/all_gather | solution.py:209
  337.4 62.5 %copy-start.93 = (f32[1024]{0:T(1024)S(1)}, f32[1024]{0:T(1024)}, u32[]{:S(2)}) copy-start(f32[1024]{0:T(1024)} %param.38) | copy-start | bytes 12292
  351.8 48.1 %all-gather.12.cloned.1.call-start = ((), (), s32[]{:S(2)}) async-start(), calls=%async_computation.7 | async-start | bytes 2621440 | tf_op jit(solution)/shard_map/all_gather | solution.py:217
  352.4 111.5 %reduce-scatter.6.cloned.1.call-start = ((), (), s32[]{:S(2)}) async-start(), calls=%async_computation.8 | async-start | bytes 5242880 | tf_op jit(solution)/shard_map/reduce_scatter | solution.py:225
  419.2 91.8 %reduce-scatter.4.cloned.1.call-start = ((), (), s32[]{:S(2)}) async-start(), calls=%async_computation.6 | async-start | bytes 5242880 | tf_op jit(solution)/shard_map/reduce_scatter | solution.py:214
  426.2 37.6 %copy-start.10 = (f32[8,128,256]{1,0,2:T(8,128)S(1)}, f32[8,128,256]{1,0,2:T(8,128)}, u32[]{:S(2)}) copy-start(f32[8,128,256]{1,0,2:T(8,128)} %get-tuple-element.179) | copy-start | bytes 3145732
  426.2 84.7 %copy-start.9 = (f32[8,128,256]{1,0,2:T(8,128)S(1)}, f32[8,128,256]{1,0,2:T(8,128)}, u32[]{:S(2)}) copy-start(f32[8,128,256]{1,0,2:T(8,128)} %copy.230) | copy-start | bytes 3145732
  426.2 84.7 %copy-start.91 = (f32[256]{0:T(256)S(1)}, f32[256]{0:T(256)}, u32[]{:S(2)}) copy-start(f32[256]{0:T(256)} %param.40) | copy-start | bytes 3076
  432.8 161.9 %reduce-scatter.8.cloned.1.call-start = ((), (), s32[]{:S(2)}) async-start(), calls=%async_computation.9 | async-start | bytes 5242880 | tf_op jit(solution)/shard_map/reduce_scatter | solution.py:239
  544.0 50.7 %copy-start.23 = (f32[8,128,256]{1,0,2:T(8,128)S(1)}, f32[8,128,256]{1,0,2:T(8,128)}, u32[]{:S(2)}) copy-start(f32[8,128,256]{1,0,2:T(8,128)} %get-tuple-element.241) | copy-start | bytes 3145732
  544.0 50.7 %copy-start.66 = (f32[8,128]{1,0:T(8,128)S(1)}, f32[8,128]{1,0:T(8,128)}, u32[]{:S(2)}) copy-start(f32[8,128]{1,0:T(8,128)} %copy-done.65) | copy-start | bytes 12292
  544.0 50.7 %copy-start.69 = (f32[8,128]{1,0:T(8,128)S(1)}, f32[8,128]{1,0:T(8,128)}, u32[]{:S(2)}) copy-start(f32[8,128]{1,0:T(8,128)} %copy-done.68) | copy-start | bytes 12292
  544.0 50.7 %copy-start.72 = (f32[8,128]{1,0:T(8,128)S(1)}, f32[8,128]{1,0:T(8,128)}, u32[]{:S(2)}) copy-start(f32[8,128]{1,0:T(8,128)} %copy-done.71) | copy-start | bytes 12292
  544.0 50.7 %copy-start.74 = (f32[256]{0:T(256)S(1)}, f32[256]{0:T(256)}, u32[]{:S(2)}) copy-start(f32[256]{0:T(256)} %param.23) | copy-start | bytes 3076
  544.0 50.7 %copy-start.80 = (f32[256]{0:T(256)S(1)}, f32[256]{0:T(256)}, u32[]{:S(2)}) copy-start(f32[256]{0:T(256)} %param.24) | copy-start | bytes 3076
  550.0 301.0 %all-gather.14.cloned.1.call-start = ((), (), s32[]{:S(2)}) async-start(), calls=%async_computation.10 | async-start | bytes 4718592 | tf_op jit(solution)/shard_map/all_gather | solution.py:244
  601.2 747.4 %all-reduce.24.cloned.1.call-start = ((), (), s32[]{:S(2)}) async-start(), calls=%async_computation.11 | async-start | bytes 21757952 | tf_op jit(solution)/shard_map/psum | solution.py:266
  707.8 108.0 %copy-start.51 = (f32[64,256]{1,0:T(8,128)S(1)}, f32[64,256]{1,0:T(8,128)}, u32[]{:S(2)}) copy-start(f32[64,256]{1,0:T(8,128)} %copy-done.50) | copy-start | bytes 196612
  707.8 108.0 %copy-start.53 = (f32[64,256]{1,0:T(8,128)S(1)}, f32[64,256]{1,0:T(8,128)}, u32[]{:S(2)}) copy-start(f32[64,256]{1,0:T(8,128)} %copy-done.52) | copy-start | bytes 196612
  707.8 108.0 %copy-start.55 = (f32[64,256]{1,0:T(8,128)S(1)}, f32[64,256]{1,0:T(8,128)}, u32[]{:S(2)}) copy-start(f32[64,256]{1,0:T(8,128)} %copy-done.54) | copy-start | bytes 196612
  707.8 108.0 %copy-start.57 = (f32[64,256]{1,0:T(8,128)S(1)}, f32[64,256]{1,0:T(8,128)}, u32[]{:S(2)}) copy-start(f32[64,256]{1,0:T(8,128)} %copy-done.56) | copy-start | bytes 196612
  883.6 18.1 %copy-start.14 = (f32[8,64,256]{1,0,2:T(8,128)}, f32[8,64,256]{1,0,2:T(8,128)S(1)}, u32[]{:S(2)}) copy-start(f32[8,64,256]{1,0,2:T(8,128)S(1)} %get-tuple-element.103) | copy-start | bytes 1572868
  883.6 18.1 %copy-start.16 = (f32[8,64,256]{1,0,2:T(8,128)}, f32[8,64,256]{1,0,2:T(8,128)S(1)}, u32[]{:S(2)}) copy-start(f32[8,64,256]{1,0,2:T(8,128)S(1)} %get-tuple-element.102) | copy-start | bytes 1572868
  956.4 45.4 %copy-start.48 = (f32[64,256]{1,0:T(8,128)S(1)}, f32[64,256]{1,0:T(8,128)}, u32[]{:S(2)}) copy-start(f32[64,256]{1,0:T(8,128)} %param.26) | copy-start | bytes 196612
  956.4 45.4 %copy-start.49 = (f32[64,256]{1,0:T(8,128)S(1)}, f32[64,256]{1,0:T(8,128)}, u32[]{:S(2)}) copy-start(f32[64,256]{1,0:T(8,128)} %param.25) | copy-start | bytes 196612
  956.4 45.4 %copy-start.58 = (f32[2,64,256]{2,1,0:T(8,128)S(1)}, f32[2,64,256]{2,1,0:T(8,128)}, u32[]{:S(2)}) copy-start(f32[2,64,256]{2,1,0:T(8,128)} %param.27) | copy-start | bytes 393220
  956.4 45.4 %copy-start.63 = (f32[64,256]{1,0:T(8,128)S(1)}, f32[64,256]{1,0:T(8,128)}, u32[]{:S(2)}) copy-start(f32[64,256]{1,0:T(8,128)} %get-tuple-element.183) | copy-start | bytes 196612
  956.4 45.4 %copy-start.78 = (f32[256]{0:T(256)S(1)}, f32[256]{0:T(256)}, u32[]{:S(2)}) copy-start(f32[256]{0:T(256)} %param.29) | copy-start | bytes 3076
  1046.1 18.1 %copy-start.79 = (f32[256]{0:T(256)S(1)}, f32[256]{0:T(256)}, u32[]{:S(2)}) copy-start(f32[256]{0:T(256)} %get-tuple-element.174) | copy-start | bytes 3076
  (56 other events, 557.7 us)
Sparse Core Ops, SparseCore 0:
  21.4 75.3 all-gather.5
  305.1 22.8 all-gather.7
  351.9 23.6 all-gather.9
  377.0 22.8 all-gather.11
  419.3 44.4 reduce-scatter.5
  466.4 44.5 reduce-scatter.3
  550.1 44.4 reduce-scatter.7
  601.3 74.9 all-gather.13
  1005.2 343.3 all-reduce.23
where the time goes:
time: 1390 us; the launch traced here: 1370 us
  waiting for transfers between devices  421 us (30%)
  other arithmetic  321 us (23%)
  local copies, waits for them, and re-layouts  308 us (22%)
  matrix products  243 us (17%)
  blocking collectives  65.6 us (5%)
  between operations  15.5 us (1%)
    psum x1, waiting for transfers between devices, body(): lax.psum((grad_norm1_gain, grad_norm1_bias, pulled[3], pulled[4], pulled[...  245 us
    scatter-add x1, other arithmetic, s4_out(): kernel[jnp.maximum(lags, 0)]  98.6 us
    gather x2, local copies, waits for them, and re-layouts, s4_out(): kernel[jnp.maximum(lags, 0)]  80.1 us
    reduce_sum x1, other arithmetic, s4_tables(): power_re = damping * jnp.cos(turn * counts)  45.4 us
    reduce_scatter x1, waiting for transfers between devices, body(): lax.psum_scatter(activ_terms, 'chan', scatter_dimension=2, tiled=True)  44.6 us
    psum x1, blocking collectives, body(): lax.psum((grad_norm1_gain, grad_norm1_bias, pulled[3], pulled[4], pulled[...  39.1 us
    reduce_scatter x1, waiting for transfers between devices, body(): lax.psum_scatter(down_terms, 'chan', scatter_dimension=2, tiled=True)  37.3 us
    dot_general x3, matrix products, s4_out(): jnp.einsum('tsh,bsh->bth', toeplitz, signal, precision=lax.Precision.HIGH...  35.3 us
  transfers between devices with their start and end apart: 9, of which 7 were waited for; matrix products, arithmetic and copies ran while one was open for 41% of the time, Pallas kernels for 0%

commit v1 on v0

v1 whole, which is shorter than its diff:
```python
import jax
import jax.numpy as jnp
from jax import lax
from jax.experimental import pallas as pl
from jax.experimental.pallas import tpu as pltpu
from jax.sharding import PartitionSpec as P

EPSILON = 1e-05
LOW = jnp.bfloat16
FULL = jnp.float32
CHANNELS = 32
UNROLL = 16
SCALE = 1.0e5
VMEM = 56 * 1024 * 1024


def swap(x, axis, distance):
    return lax.ppermute(x, axis, [(i, i ^ distance) for i in range(lax.axis_size(axis))])


def axis_bits(axis):
    size = lax.axis_size(axis)
    bits = size.bit_length() - 1
    assert size == 1 << bits
    return bits


def gather_pieces(x):
    pieces = {0: x}
    for bit in reversed(range(axis_bits("chan"))):
        for d in list(pieces):
            pieces[d ^ (1 << bit)] = swap(pieces[d], "chan", 1 << bit)
    return [pieces[d] for d in range(len(pieces))]


def reduce_pieces(parts, marks=None):
    sums = dict(enumerate(parts))
    for bit in range(axis_bits("chan")):
        if marks is not None and bit == axis_bits("chan") - 1:
            marks.append(sums[1 << bit])
        for d in sorted(sums, reverse=True):
            if d >> bit & 1:
                sums[d ^ (1 << bit)] = sums[d ^ (1 << bit)] + swap(
                    sums.pop(d).astype(LOW), "chan", 1 << bit
                ).astype(FULL)
    return sums[0]


def sum_chan(x):
    return x + sum(swap(x, "chan", d) for d in range(1, lax.axis_size("chan")))


def after(x, *others):
    return lax.optimization_barrier((x, others))[0]


def exchange_all(x):
    return lax.all_to_all(x, "seq", 0, 0, tiled=True)


def split_sum(parts, place, count):
    rows, columns = min(part.shape[0] for part, _ in parts), parts[0][0].shape[1]
    block = (rows // count, columns)
    scalars = jnp.stack([place] + [first for _, first in parts]).astype(jnp.int32)

    def kernel(scalars, *refs):
        del scalars
        ins, outs = refs[:-count], refs[-count:]
        total = sum(ref[...].astype(FULL) for ref in ins).astype(LOW)
        for e, out in enumerate(outs):

            @pl.when(pl.program_id(0) == e)
            def _(out=out):
                out[...] = total

    return pl.pallas_call(
        kernel,
        grid_spec=pltpu.PrefetchScalarGridSpec(
            num_scalar_prefetch=1,
            grid=(count,),
            in_specs=[
                pl.BlockSpec(block, lambda e, n, i=i: (n[i + 1] + (n[0] ^ e), 0)) for i in range(len(parts))
            ],
            out_specs=[pl.BlockSpec(block, lambda e, n: (0, 0))] * count,
        ),
        out_shape=[jax.ShapeDtypeStruct(block, LOW)] * count,
        compiler_params=pltpu.CompilerParams(vmem_limit_bytes=VMEM),
        cost_estimate=cost(2),
        name="split_sum",
    )(scalars, *[part for part, _ in parts])


def join(parts):
    rows, columns = parts[0].shape
    count = len(parts)

    def kernel(*refs):
        for e, ref in enumerate(refs[:-1]):

            @pl.when(pl.program_id(0) == e)
            def _(ref=ref):
                refs[-1][...] = ref[...]

    return pl.pallas_call(
        kernel,
        grid=(count,),
        in_specs=[pl.BlockSpec((rows, columns), lambda e: (0, 0))] * count,
        out_specs=pl.BlockSpec((rows, columns), lambda e: (e, 0)),
        out_shape=jax.ShapeDtypeStruct((count * rows, columns), LOW),
        compiler_params=pltpu.CompilerParams(vmem_limit_bytes=VMEM),
        cost_estimate=cost(2),
        name="join",
    )(*parts)


def sum_small(wide, narrow):
    seqs = lax.axis_size("seq")
    lanes = wide.shape[1]
    share = wide.shape[0] // seqs
    short = -(-narrow.shape[0] // (seqs * lanes))
    fill = -(-(share + 2 * short) // 16) * 16 - share - 2 * short

    def packed(wide, narrow):
        lead = wide.shape[:-2]
        high = lax.optimization_barrier(narrow.astype(LOW))
        low = (narrow - high.astype(FULL)).astype(LOW)
        return jnp.concatenate(
            [wide.astype(LOW), high, low, jnp.zeros((*lead, fill, lanes), LOW)], axis=-2
        )

    padded = jnp.pad(narrow, (0, seqs * short * lanes - narrow.shape[0])).reshape(seqs, short, lanes)
    parts = exchange_all(packed(wide.reshape(seqs, share, lanes), padded)).astype(FULL)
    total = jnp.sum(parts, axis=0)
    total = packed(total[:share], total[share : share + short] + total[share + short : share + 2 * short])
    parts = exchange_all(jnp.broadcast_to(total[None], (seqs, *total.shape))).astype(FULL)
    result = parts[:, share : share + short] + parts[:, share + short : share + 2 * short]
    return parts[:, :share].reshape(wide.shape), result.reshape(-1)[: narrow.shape[0]]


class Chain:
    def __init__(self, x, stages):
        me = lax.axis_index("seq")
        self.start = x
        self.masks, self.places = [], []
        for bits in stages:
            place = 0
            for bit in bits:
                place = 2 * place + ((me >> bit) & 1)
            self.places.append(place)
            self.masks.append(
                [
                    sum(1 << bit for i, bit in enumerate(reversed(bits)) if e >> i & 1)
                    for e in range(1 << len(bits))
                ]
            )
        self.level = 0
        size = x.shape[0] // 2
        sent = lax.dynamic_slice_in_dim(x, (1 - self.places[0]) * size, size, 0)
        self.parts = [x, swap(sent, "seq", self.masks[0][1])]

    def steps_left(self):
        return 2 * len(self.masks) - 1 - self.level

    def step(self, *deps):
        if self.steps_left() <= 0:
            return []
        count = len(self.masks)
        self.parts = list(after(tuple(self.parts), deps))
        self.level += 1
        if self.level < count:
            masks = self.masks[self.level]
            firsts = [0 * self.places[0]] * len(self.parts)
            if self.level == 1:
                firsts[0] = self.places[0] * len(masks)
            pieces = list(split_sum(list(zip(self.parts, firsts)), self.places[self.level], len(masks)))
            self.parts = pieces[:1] + [swap(p, "seq", mask) for p, mask in zip(pieces[1:], masks[1:])]
            return pieces
        if self.level == count:
            x = sum(part.astype(FULL) for part in self.parts).astype(LOW)
        else:
            x = join(self.parts)
        masks = self.masks[2 * count - 1 - self.level]
        self.parts = [x] + [swap(x, "seq", mask) for mask in masks[1:]]
        return [x]

    def place(self):
        total = 0
        for place, masks in zip(self.places, self.masks):
            total = len(masks) * total + place
        return total


def chain_stages(first, bits):
    rest = [bit for bit in range(bits) if bit != first]
    return [[first]] + [rest[i : i + 2] for i in range(0, len(rest), 2)]


def finish(chain, row_turn, half_turn, column_turn):
    assert chain.steps_left() <= 0
    rows, columns = chain.parts[0].shape
    width = columns // 4
    scalars = jnp.stack([chain.place() ^ row_turn, half_turn, column_turn]).astype(jnp.int32)
    count = 1 << (lax.axis_size("seq") - 1).bit_length()
    spec = pl.BlockSpec((rows, 2 * width), lambda half, n: (0, half))

    def kernel(scalars, own, received, out):
        size = out.shape[0] // count
        for q in range(count):
            ref, first = (own, q * size) if q < count // 2 else (received, (q - count // 2) * size)
            target = pl.ds(pl.multiple_of((scalars[0] ^ q) * size, size), size)
            for e in range(2):
                place = pl.ds(pl.multiple_of((e ^ scalars[2]) * width, width), width)
                out[target, place] = ref[first : first + size, e * width : (e + 1) * width].astype(FULL)

    return pl.pallas_call(
        kernel,
        grid_spec=pltpu.PrefetchScalarGridSpec(
            num_scalar_prefetch=1,
            grid=(2,),
            in_specs=[spec] * 2,
            out_specs=pl.BlockSpec((2 * rows, 2 * width), lambda half, n: (0, half ^ n[1])),
        ),
        out_shape=jax.ShapeDtypeStruct((2 * rows, columns), FULL),
        compiler_params=pltpu.CompilerParams(vmem_limit_bytes=VMEM),
        cost_estimate=cost(3),
        name="finish",
    )(scalars, *chain.parts)


def cost(us):
    return pl.CostEstimate(flops=0, bytes_accessed=int(us * SCALE), transcendentals=0)


def pair(re, im):
    return jnp.concatenate([re, im], axis=-1)


def factor(re, im):
    return pair(re, re), pair(-im, im)


def times(x, first, second):
    lanes = x.shape[-1]
    return x * first + pltpu.roll(x, lanes // 2, x.ndim - 1) * second


def cmul(a, b):
    return a[0] * b[0] - a[1] * b[1], a[0] * b[1] + a[1] * b[0]


def add(a, b):
    return a[0] + b[0], a[1] + b[1]


def scale(a, k):
    return a[0] * k, a[1] * k


BBAR, READ, CARRY, STRIDE, KERNEL, Z, RATIO, C, B, A_PART, STEP = 0, 2, 4, 10, 18, 19, 21, 23, 25, 27, 29
ROWS = 30


def less_one(x):
    total = 1.0 + x / 8.0
    for k in (7.0, 6.0, 5.0, 4.0, 3.0, 2.0):
        total = 1.0 + x / k * total
    return jnp.where(x > -0.25, x * total, jnp.exp(x) - 1.0)


def consts_kernel(block, decay_ref, freq_ref, b_ref, c_ref, step_ref, consts, base):
    states, width = decay_ref.shape
    lanes = 2 * states

    def wide(x):
        return jnp.concatenate([x, x], axis=0).T

    decay, freq = wide(decay_ref[...]), wide(freq_ref[...])
    b = (wide(b_ref[0]), wide(b_ref[1]))
    c = (wide(c_ref[0]), wide(c_ref[1]))
    step = jnp.broadcast_to(step_ref[...], (lanes, width)).T
    first = lax.broadcasted_iota(jnp.int32, (width, lanes), 1) < states
    rate = step * decay
    turn = step * freq
    size = jnp.exp(-rate)
    z = (size * jnp.cos(turn), size * jnp.sin(turn))
    half_turn = jnp.sin(0.5 * turn)
    less = (less_one(-rate) * jnp.cos(turn) - 2.0 * half_turn * half_turn, z[1])
    modulus = decay * decay + freq * freq
    ratio = (
        (freq * less[1] - decay * less[0]) / modulus,
        -(decay * less[1] + freq * less[0]) / modulus,
    )
    bbar = cmul(ratio, b)
    twice_c = scale(c, 2.0)

    def put_factor(k, x):
        consts[k] = x[0]
        consts[k + 1] = jnp.where(first, -x[1], x[1])

    def put_plain(k, x):
        consts[k] = x[0]
        consts[k + 1] = x[1]

    put_factor(BBAR, bbar)
    put_factor(READ, cmul(twice_c, z))
    kernel = cmul(twice_c, bbar)
    consts[KERNEL] = jnp.where(first, kernel[0], -kernel[1])
    put_plain(Z, z)
    put_plain(RATIO, ratio)
    put_plain(C, c)
    put_plain(B, b)
    consts[A_PART] = decay
    consts[A_PART + 1] = freq
    consts[STEP] = step
    power = (jnp.ones_like(size), jnp.zeros_like(size))
    for k in range(8):
        base[k] = jnp.where(first, power[0], power[1])
        power = cmul(power, z)
    k = 8
    while k < 4 * block:
        if k <= 64:
            put_factor(STRIDE + 2 * (k.bit_length() - 4), power)
        if k >= block:
            put_factor(CARRY + 2 * ((k // block).bit_length() - 1), power)
        power = cmul(power, power)
        k *= 2
    put_factor(CARRY + 4, power)


def s4_consts(a_decay, a_freq, b_state, c_state, step_size, block):
    states, width = a_decay.shape
    return pl.pallas_call(
        lambda *refs: consts_kernel(block, *refs),
        out_shape=[
            jax.ShapeDtypeStruct((ROWS, width, 2 * states), FULL),
            jax.ShapeDtypeStruct((8, width, 2 * states), FULL),
        ],
        compiler_params=pltpu.CompilerParams(vmem_limit_bytes=VMEM),
        cost_estimate=cost(6),
        name="s4_consts",
    )(a_decay, a_freq, b_state, c_state, step_size[None, :])


def half_turned(x):
    return pltpu.roll(x, x.shape[-1] // 2, x.ndim - 1)


def high_low(x):
    high = x.astype(LOW)
    return high, (x - high.astype(FULL)).astype(LOW)


def dot(a, b):
    return lax.dot_general(a, b, (((1,), (0,)), ((), ())), preferred_element_type=FULL)


def dot_t(a, b):
    return lax.dot_general(a, b, (((1,), (1,)), ((), ())), preferred_element_type=FULL)


def tables_kernel(base, consts, *refs):
    z_out, h_out = refs[-2:]
    channels, _, lanes = z_out.shape
    row8 = lax.broadcasted_iota(jnp.int32, (8, lanes), 0)
    row = lax.broadcasted_iota(jnp.int32, (lanes, lanes), 0)
    lane = lax.broadcasted_iota(jnp.int32, (lanes, lanes), 1)
    live = row + lane >= lanes - 1

    def one(c):
        first = jnp.concatenate([base[k, pl.ds(c, 1), :] for k in range(8)], axis=0)
        tiles = [(first, half_turned(first))]
        for level in range(4):
            k = STRIDE + 2 * level
            a, b = consts[k, pl.ds(c, 1), :], consts[k + 1, pl.ds(c, 1), :]
            tiles += [(t * a + u * b, u * a - t * b) for t, u in tiles]
        z = jnp.concatenate([t for t, _ in tiles], axis=0)
        high, low = high_low(z)
        z_out[c, :lanes, :] = high
        z_out[c, lanes:, :] = low
        f_high, f_low = high_low(jnp.broadcast_to(consts[KERNEL, pl.ds(c, 1), :], (8, lanes)))
        h = dot_t(jnp.concatenate([f_high, f_low], axis=0), high)
        h = h[:8] + h[8:] + dot_t(f_high, low)
        for bit in (1, 2, 4):
            h = jnp.where((7 - row8) & bit != 0, pltpu.roll(h, bit, 1), h)
        hankel = [pltpu.roll(h, lanes - 8 - k, 1) if k < lanes - 8 else h for k in range(0, lanes, 8)]
        hankel = jnp.concatenate(hankel, axis=0)
        h_out[c] = jnp.where(live, hankel, 0.0).astype(LOW)

    @pl.loop(0, channels, step=UNROLL)
    def _(c):
        for k in range(UNROLL):
            one(c + k)


def s4_tables(base, consts, part, parts, tables=(), deps=()):
    _, width, lanes = base.shape
    steps = width // CHANNELS // parts
    skip = part * steps
    anywhere = pl.BlockSpec(memory_space=pl.ANY)
    return pl.pallas_call(
        tables_kernel,
        grid=(steps,),
        in_specs=[
            pl.BlockSpec((8, CHANNELS, lanes), lambda i: (0, i + skip, 0)),
            pl.BlockSpec((ROWS, CHANNELS, lanes), lambda i: (0, i + skip, 0)),
        ]
        + [anywhere] * (len(tables) + len(deps)),
        out_specs=[
            pl.BlockSpec((CHANNELS, 2 * lanes, lanes), lambda i: (i + skip, 0, 0)),
            pl.BlockSpec((CHANNELS, lanes, lanes), lambda i: (i + skip, 0, 0)),
        ],
        out_shape=[
            jax.ShapeDtypeStruct((width, 2 * lanes, lanes), LOW),
            jax.ShapeDtypeStruct((width, lanes, lanes), LOW),
        ],
        input_output_aliases={2: 0, 3: 1} if tables else {},
        compiler_params=pltpu.CompilerParams(vmem_limit_bytes=VMEM),
        cost_estimate=cost(24 / parts),
        name="s4_tables",
    )(base, consts, *tables, *deps)


def flip_matrix(size):
    row = lax.broadcasted_iota(jnp.int32, (size, size), 0)
    lane = lax.broadcasted_iota(jnp.int32, (size, size), 1)
    return (row + lane == size - 1).astype(FULL).astype(LOW)


def rows_of_channels(consts, k):
    return jnp.stack([consts[k, c : c + 1, :] for c in range(consts.shape[1])])


def weighted_ends(x, place, z):
    high, low = high_low(x * place)
    x = x.astype(LOW)
    none = jnp.zeros_like(x)
    left = jnp.concatenate([x, high, low, none], axis=0)
    right = jnp.concatenate([x, high, none, none], axis=0)
    ends = dot(jnp.concatenate([left, right], axis=1), z)
    count = x.shape[0]
    return ends[:count], ends[count : 2 * count] + ends[2 * count : 3 * count]


def times_both(x, consts, k):
    first, second = rows_of_channels(consts, k), rows_of_channels(consts, k + 1)
    return x[0] * first + x[1] * second, x[1] * first - x[0] * second


def scan_blocks(x, consts, row, reverse):
    count = x[0].shape[1]
    for level, d in enumerate((1, 2, 4)):
        live = row < count - d if reverse else row >= d
        moved = [jnp.where(live, pltpu.roll(e, count - d if reverse else d, 1), 0.0) for e in x]
        x = add(x, times_both(moved, consts, CARRY + 2 * level))
    return x


def forward_kernel(
    signal, skip, consts, z, m, init, activ, slope, x_out, p_out, q_out, s_out, x_scr, y_scr
):
    step = pl.program_id(0)
    channels, _, lanes = z.shape
    count = signal.shape[0] // lanes
    width = signal.shape[1]

    @pl.when(step == 0)
    def _():
        flip = flip_matrix(lanes)
        for j in range(count):
            x_scr[pl.ds(j, width, stride=count), :] = dot(flip, signal[j * lanes : (j + 1) * lanes, :]).T

    rows = pl.ds(pl.multiple_of(step * channels * count, channels * count), channels * count)
    x = x_scr[rows, :].reshape(channels, count, lanes)
    place = lax.broadcasted_iota(jnp.int32, (count, lanes), 1).astype(FULL)
    row = lax.broadcasted_iota(jnp.int32, (channels, count, lanes), 1)
    plus = lax.broadcasted_iota(jnp.int32, (channels, count, lanes), 2) < lanes // 2
    ends = [weighted_ends(x[c], place, z[c]) for c in range(channels)]
    p = jnp.stack([e[0] for e in ends])
    q = jnp.stack([e[1] for e in ends])
    start = init[...][:, None, :]
    state = times_both((p, half_turned(p)), consts, BBAR)
    state = [
        jnp.where(row == 0, e, pltpu.roll(s, 1, 1)) for e, s in zip((start, half_turned(start)), state)
    ]
    state = scan_blocks(state, consts, row, False)
    read, _ = times_both(state, consts, READ)
    read = jnp.where(plus, read, -read).astype(LOW)
    y = [dot(x[c].astype(LOW), m[c]) + dot_t(read[c], z[c, :lanes, :]) for c in range(channels)]
    y_scr[rows, :] = jnp.concatenate(y, axis=0)
    x_out[...] = x
    p_out[...] = p
    q_out[...] = q
    s_out[...] = state[0]

    @pl.when(step == pl.num_programs(0) - 1)
    def _():
        for j in range(count):
            part = slice(j * lanes, (j + 1) * lanes)
            mixed = y_scr[pl.ds(j, width, stride=count), :].T + skip[...] * signal[part, :].astype(FULL)
            inner = 0.7978845608028654 * (mixed + 0.044715 * mixed * mixed * mixed)
            bent = jnp.tanh(inner)
            activ[part, :] = (0.5 * mixed * (1.0 + bent)).astype(LOW)
            slope[part, :] = 0.5 * (1.0 + bent) + 0.5 * mixed * (1.0 - bent * bent) * (
                0.7978845608028654 * (1.0 + 3 * 0.044715 * mixed * mixed)
            )


def s4_forward(signal, skip, consts, z, m, init):
    tokens, width = signal.shape
    lanes = z.shape[-1]
    count = tokens // lanes
    whole = pl.BlockSpec((tokens, width), lambda i: (0, 0))
    by_channel = pl.BlockSpec((CHANNELS, count, lanes), lambda i: (i, 0, 0))
    per_channel = jax.ShapeDtypeStruct((width, count, lanes), FULL)
    return pl.pallas_call(
        forward_kernel,
        grid=(width // CHANNELS,),
        in_specs=[
            whole,
            pl.BlockSpec((1, width), lambda i: (0, 0)),
            pl.BlockSpec((ROWS, CHANNELS, lanes), lambda i: (0, i, 0)),
            pl.BlockSpec((CHANNELS, 2 * lanes, lanes), lambda i: (i, 0, 0)),
            pl.BlockSpec((CHANNELS, lanes, lanes), lambda i: (i, 0, 0)),
            pl.BlockSpec((CHANNELS, lanes), lambda i: (i, 0)),
        ],
        out_specs=[whole, whole] + [by_channel] * 4,
        out_shape=[
            jax.ShapeDtypeStruct((tokens, width), LOW),
            jax.ShapeDtypeStruct((tokens, width), FULL),
        ]
        + [per_channel] * 4,
        scratch_shapes=[pltpu.VMEM((width * count, lanes), FULL)] * 2,
        compiler_params=pltpu.CompilerParams(vmem_limit_bytes=VMEM),
        cost_estimate=cost(18),
        name="s4_forward",
    )(signal, skip, consts, z, m, init)


def backward_kernel(
    grads, consts, z, m, init, out, g_out, u_out, v_out, h_out, g_scr, y_scr
):
    step = pl.program_id(0)
    channels, _, lanes = z.shape
    count = grads.shape[0] // lanes
    width = grads.shape[1]

    @pl.when(step == 0)
    def _():
        for j in range(count):
            g_scr[pl.ds(j, width, stride=count), :] = grads[j * lanes : (j + 1) * lanes, :].astype(FULL).T

    rows = pl.ds(pl.multiple_of(step * channels * count, channels * count), channels * count)
    g = g_scr[rows, :].reshape(channels, count, lanes)
    place = lax.broadcasted_iota(jnp.int32, (count, lanes), 1).astype(FULL)
    row = lax.broadcasted_iota(jnp.int32, (channels, count, lanes), 1)
    plus = lax.broadcasted_iota(jnp.int32, (channels, count, lanes), 2) < lanes // 2
    ends = [weighted_ends(g[c], place, z[c]) for c in range(channels)]
    u = jnp.stack([e[0] for e in ends])
    v = jnp.stack([e[1] for e in ends])
    start = init[...][:, None, :]
    later = times_both((u, half_turned(u)), consts, READ)
    later = [
        jnp.where(row == count - 1, e, pltpu.roll(s, count - 1, 1))
        for e, s in zip((start, half_turned(start)), later)
    ]
    later = scan_blocks(later, consts, row, True)
    write, _ = times_both(later, consts, BBAR)
    write = jnp.where(plus, write, -write).astype(LOW)
    y = [dot(g[c].astype(LOW), m[c]) + dot_t(write[c], z[c, :lanes, :]) for c in range(channels)]
    y_scr[rows, :] = jnp.concatenate(y, axis=0)
    g_out[...] = g
    u_out[...] = u
    v_out[...] = v
    h_out[...] = later[0]

    @pl.when(step == pl.num_programs(0) - 1)
    def _():
        flip = flip_matrix(lanes)
        for j in range(count):
            out[j * lanes : (j + 1) * lanes, :] = dot(
                flip, y_scr[pl.ds(j, width, stride=count), :].T.astype(LOW)
            )


def s4_backward(grads, consts, z, m, init):
    tokens, width = grads.shape
    lanes = z.shape[-1]
    count = tokens // lanes
    whole = pl.BlockSpec((tokens, width), lambda i: (0, 0))
    by_channel = pl.BlockSpec((CHANNELS, count, lanes), lambda i: (i, 0, 0))
    per_channel = jax.ShapeDtypeStruct((width, count, lanes), FULL)
    return pl.pallas_call(
        backward_kernel,
        grid=(width // CHANNELS,),
        in_specs=[
            whole,
            pl.BlockSpec((ROWS, CHANNELS, lanes), lambda i: (0, i, 0)),
            pl.BlockSpec((CHANNELS, 2 * lanes, lanes), lambda i: (i, 0, 0)),
            pl.BlockSpec((CHANNELS, lanes, lanes), lambda i: (i, 0, 0)),
            pl.BlockSpec((CHANNELS, lanes), lambda i: (i, 0)),
        ],
        out_specs=[whole] + [by_channel] * 4,
        out_shape=[jax.ShapeDtypeStruct((tokens, width), FULL)] + [per_channel] * 4,
        scratch_shapes=[pltpu.VMEM((width * count, lanes), FULL)] * 2,
        compiler_params=pltpu.CompilerParams(vmem_limit_bytes=VMEM),
        cost_estimate=cost(18),
        name="s4_backward",
    )(grads, consts, z, m, init)


def sums_kernel(block, x, g, p, q, s, u, v, h, z, consts, dep, out):
    del dep
    channels, count, lanes = x.shape
    states = lanes // 2
    row8 = lax.broadcasted_iota(jnp.int32, (8, lanes), 0)
    row = lax.broadcasted_iota(jnp.int32, (lanes, lanes), 0)
    lane = lax.broadcasted_iota(jnp.int32, (lanes, lanes), 1)
    place = lax.broadcasted_iota(jnp.int32, (8, lanes), 1).astype(FULL)
    live = row + lane >= lanes - 1
    first = lax.broadcasted_iota(jnp.int32, (channels, lanes), 1) < states
    w = []
    for c in range(channels):
        both = lax.dot_general(
            x[c].astype(LOW), g[c].astype(LOW), (((0,), (0,)), ((), ())), preferred_element_type=FULL
        )
        both = jnp.where(live, both, 0.0)
        tiles = [both[k : k + 8, :] for k in range(0, lanes, 8)]
        shift = 8
        while len(tiles) > 1:
            tiles = [a + pltpu.roll(b, shift, 1) for a, b in zip(tiles[::2], tiles[1::2])]
            shift *= 2
        total = pltpu.roll(tiles[0], 1, 1)
        for bit in (1, 2, 4):
            total = jnp.where(row8 & bit != 0, pltpu.roll(total, bit, 1), total)
        high, low = high_low(total)
        place_high, place_low = high_low(total * place)
        none = jnp.zeros_like(high)
        left = jnp.concatenate([high, low, place_high, place_low], axis=0)
        right = jnp.concatenate([high, none, place_high, none], axis=0)
        w.append(dot(jnp.concatenate([left, right], axis=1), z[c]))
    lag0 = jnp.sum(jnp.stack([e[:16] for e in w]), axis=1)
    lag1 = jnp.sum(jnp.stack([e[16:] for e in w]), axis=1)

    def both_halves(x):
        turned = half_turned(x)
        return jnp.where(first, x, turned), jnp.where(first, turned, x)

    def product(a, b):
        plain = jnp.sum(a * b, axis=1)
        crossed = jnp.sum(a * half_turned(b), axis=1)
        plain = jnp.where(first, plain, -plain)
        return plain + half_turned(plain), crossed + half_turned(crossed)

    states_read = product(u[...], s[...])
    slopes_read = product(u[...] + v[...], s[...])
    writes = product(h[...], p[...])
    slopes_write = product(h[...], q[...])
    carried = product(h[...], s[...])
    lag0, lag1 = both_halves(lag0), both_halves(lag1)

    def const(k):
        return consts[k]

    def const_factor(k):
        second = const(k + 1)
        return const(k), jnp.where(first, -second, second)

    bbar, read, carry = const_factor(BBAR), const_factor(READ), const_factor(CARRY)
    z_one, ratio = (const(Z), const(Z + 1)), (const(RATIO), const(RATIO + 1))
    c, b = (const(C), const(C + 1)), (const(B), const(B + 1))
    decay, freq, step = const(A_PART), const(A_PART + 1), const(STEP)
    modulus = decay * decay + freq * freq
    over_a = (-decay / modulus, -freq / modulus)
    to_c = scale(add(cmul(z_one, states_read), cmul(bbar, lag0)), 2.0)
    to_bbar = add(writes, scale(cmul(c, lag0), 2.0))
    to_log = add(
        add(cmul(read, slopes_read), cmul(bbar, slopes_write)),
        add(scale(cmul(carry, carried), float(block)), scale(cmul(cmul(c, bbar), lag1), 2.0)),
    )
    to_b = cmul(to_bbar, ratio)
    over = cmul(cmul(to_bbar, b), over_a)
    to_log = add(to_log, cmul(over, z_one))
    to_a = cmul(over, ratio)
    grad_decay = to_a[0] - step * to_log[0]
    grad_freq = to_a[1] - step * to_log[1]
    grad_step = jnp.where(first, -to_log[0] * decay, -to_log[1] * freq)
    out[0] = jnp.where(first, grad_decay, grad_freq)
    out[1] = jnp.where(first, to_b[0], -to_b[1])
    out[2] = jnp.where(first, to_c[0], -to_c[1])
    out[3] = jnp.broadcast_to(jnp.sum(grad_step, axis=1, keepdims=True), (channels, lanes))


def s4_sums(x, g, p, q, s, u, v, h, z, consts, block, dep, part, parts):
    width, count, lanes = x.shape
    steps = width // CHANNELS // parts
    skip = part * steps
    by_channel = pl.BlockSpec((CHANNELS, count, lanes), lambda i: (i + skip, 0, 0))
    return pl.pallas_call(
        lambda *refs: sums_kernel(block, *refs),
        grid=(steps,),
        in_specs=[by_channel] * 8
        + [
            pl.BlockSpec((CHANNELS, 2 * lanes, lanes), lambda i: (i + skip, 0, 0)),
            pl.BlockSpec((ROWS, CHANNELS, lanes), lambda i: (0, i + skip, 0)),
            pl.BlockSpec(memory_space=pl.ANY),
        ],
        out_specs=pl.BlockSpec((4, CHANNELS, lanes), lambda i: (0, i, 0)),
        out_shape=jax.ShapeDtypeStruct((4, width // parts, lanes), FULL),
        compiler_params=pltpu.CompilerParams(vmem_limit_bytes=VMEM),
        cost_estimate=cost(18 / parts),
        name="s4_sums",
    )(x, g, p, q, s, u, v, h, z, consts, dep)


def split(rows):
    half = rows.shape[-1] // 2
    return rows[..., :half], rows[..., half:]


def t_dot(a, b):
    return lax.dot_general(a, b, (((0,), (0,)), ((), ())), preferred_element_type=FULL)


def layer_forward(values, gain, bias, total_width, sums=None):
    if sums is None:
        sums = sum_chan(jnp.stack([jnp.sum(values, axis=-1), jnp.sum(values * values, axis=-1)]))
    center = sums[0] / total_width
    spread_var = sums[1] / total_width - center * center
    inverse = lax.rsqrt(spread_var + EPSILON)[..., None]
    normed = (values - center[..., None]) * inverse
    return normed * gain + bias, normed, inverse


def layer_backward(grad_out, normed, inverse, gain, total_width, work):
    scaled = grad_out * gain
    sums = jnp.stack([jnp.sum(scaled, axis=-1), jnp.sum(scaled * normed, axis=-1)])
    sums = after(sum_chan(sums), *work(sums))
    grad_in = inverse * (
        scaled - sums[0][..., None] / total_width - normed * sums[1][..., None] / total_width
    )
    return grad_in, jnp.sum(grad_out * normed, axis=0), jnp.sum(grad_out, axis=0)


def body(
    block_input,
    lengths,
    norm1_gain,
    norm1_bias,
    a_decay,
    a_freq,
    b_state,
    c_state,
    step_size,
    skip_gain,
    w_value,
    b_value,
    w_gate,
    b_gate,
    norm2_gain,
    norm2_bias,
    w_up,
    b_up,
    w_down,
    b_down,
    out_grad,
):
    batch, block, width = block_input.shape
    chans = lax.axis_size("chan")
    seqs = lax.axis_size("seq")
    assert seqs % batch == 0
    runs = seqs // batch
    total_width = width * chans
    assert chans == 4
    seq_me = lax.axis_index("seq")
    chan_me = lax.axis_index("chan")
    groups = None if runs == 1 else [[r * batch + j for j in range(batch)] for r in range(runs)]
    peers = None if runs == 1 else [[r * batch + j for r in range(runs)] for j in range(batch)]

    def exchange(x):
        return lax.all_to_all(x, "seq", 0, 0, axis_index_groups=groups, tiled=True)

    def rows_of(w):
        return [
            lax.dynamic_slice_in_dim(w, (chan_me ^ d) * width, width, 0) for d in range(chans)
        ]

    inputs_low = exchange(block_input).reshape(batch * block, width)

    consts, base = s4_consts(a_decay, a_freq, b_state, c_state, step_size, block)
    tables = s4_tables(base, consts, 0, 2)
    inputs_low = after(inputs_low, tables[0])
    inputs = inputs_low.astype(FULL)
    moments = jnp.stack([jnp.sum(inputs, axis=-1), jnp.sum(inputs * inputs, axis=-1)])
    grad_low = exchange(after(out_grad, moments)).reshape(batch * block, width)
    z, m = s4_tables(base, consts, 1, 2, tables, (moments,))
    moments = after(sum_chan(moments), m)
    states = a_decay.shape[0]

    def const_factor(k):
        return consts[k, :, :states], consts[k + 1, :, states:]

    begin = (seq_me // batch) * batch * block
    places = begin + jnp.arange(batch * block, dtype=jnp.int32)
    mask = (places < lengths[seq_me % batch]).astype(FULL)[:, None]
    norm_one, normed_one, inverse_one = layer_forward(inputs, norm1_gain, norm1_bias, total_width, moments)
    signal = (mask * norm_one).astype(LOW)
    skip = skip_gain[None, :]
    init = jnp.zeros((width, 2 * states), FULL)
    if runs > 1:
        _, _, _, p, _, s = s4_forward(signal, skip, consts, z, m, init)
        carry = const_factor(CARRY)
        end = add(cmul(carry, split(s[:, -1])), cmul(const_factor(BBAR), split(p[:, -1])))
        ends = lax.all_gather(pair(*end), "seq", axis_index_groups=peers)
        hop = carry
        for _ in range(3):
            hop = cmul(hop, hop)
        for r in range(runs - 1):
            moved = add(cmul(hop, split(init)), split(ends[r]))
            init = jnp.where(r < seq_me // batch, pair(*moved), init)
    activ, slope, xs, ps, qs, ss = s4_forward(signal, skip, consts, z, m, init)

    wv, wg = rows_of(w_value), rows_of(w_gate)
    w_gated = [jnp.concatenate([a, b], axis=1) for a, b in zip(wv, wg)]
    w_ups = rows_of(w_up)
    w_downs = [
        lax.dynamic_slice_in_dim(w_down, (chan_me ^ d) * width, width, 1) for d in range(chans)
    ]
    grads = gather_pieces(grad_low)
    activs = gather_pieces(after(activ, grads[2]))
    both = sum(dot(a, w) for a, w in zip(activs, w_gated))
    value = both[:, :width] + b_value
    gate = both[:, width:] + b_gate
    opened = jax.nn.sigmoid(gate)
    resid = inputs + value * opened
    norm_two, normed_two, inverse_two = layer_forward(resid, norm2_gain, norm2_bias, total_width)
    norms = gather_pieces(norm_two.astype(LOW))
    hidden = sum(dot(a, w) for a, w in zip(norms, w_ups)) + b_up
    spread, gelu_pull = jax.vjp(jax.nn.gelu, hidden)
    spread = spread.astype(LOW)
    downs = [dot(spread, w) for w in w_downs]
    output = (resid + reduce_pieces(downs) + b_down).astype(LOW)
    output = exchange(output.reshape(batch, block, width))

    grad_out = grad_low.astype(FULL)
    grad_spread = sum(dot_t(a, w) for a, w in zip(grads, w_downs))
    grad_hidden = gelu_pull(grad_spread)[0].astype(LOW)
    marks = []
    grad_norm_two = reduce_pieces([dot_t(grad_hidden, w) for w in w_ups], marks)
    bits = axis_bits("seq")
    orders = chain_stages(0, bits), chain_stages(1, bits)
    spread_late, hidden_late = after(spread, marks[0]), after(grad_hidden, marks[0])
    downs = [Chain(t_dot(spread_late, jnp.concatenate(grads, axis=1)).astype(LOW), orders[0])]
    ups = [Chain(t_dot(jnp.concatenate(norms, axis=1), hidden_late).astype(LOW), orders[1])]
    grad_norm_two = after(grad_norm_two, *[chain.start for chain in downs + ups])

    def steps(chains, *deps):
        return [made for chain in chains for made in chain.step(*deps)]

    grad_resid, grad_norm2_gain, grad_norm2_bias = layer_backward(
        grad_norm_two, normed_two, inverse_two, norm2_gain, total_width, lambda dep: []
    )
    grad_resid = grad_out + grad_resid
    grad_value = (grad_resid * opened).astype(LOW)
    grad_gate = (grad_resid * value * opened * (1.0 - opened)).astype(LOW)
    grad_both = jnp.concatenate([grad_value, grad_gate], axis=1)
    grad_activ = reduce_pieces([dot_t(grad_both, w) for w in w_gated], marks)
    gateds = [
        Chain(t_dot(jnp.concatenate(activs, axis=1), after(grad_both, marks[1])).astype(LOW), orders[0])
    ]
    grad_activ = after(grad_activ, gateds[0].start, *steps(downs, marks[1]))
    grad_mixed = (grad_activ * slope).astype(LOW)
    init = jnp.zeros((width, 2 * states), FULL)
    if runs > 1:
        _, _, u, _, h = s4_backward(grad_mixed, consts, z, m, init)
        end = add(cmul(carry, split(h[:, 0])), cmul(const_factor(READ), split(u[:, 0])))
        ends = lax.all_gather(pair(*end), "seq", axis_index_groups=peers)
        for r in reversed(range(1, runs)):
            moved = add(cmul(hop, split(init)), split(ends[r]))
            init = jnp.where(r > seq_me // batch, pair(*moved), init)
    grad_signal, gs, us, vs, hs = s4_backward(grad_mixed, consts, z, m, init)
    grad_signal = grad_signal + skip * grad_mixed.astype(FULL)
    s4_parts = (xs, gs, ps, qs, ss, us, vs, hs, z, consts, block)
    sums = []

    def sums_part(*deps):
        sums.append(s4_sums(*s4_parts, after(hs, *deps), len(sums), 4))
        return sums[-1]

    grad_input, grad_norm1_gain, grad_norm1_bias = layer_backward(
        grad_signal * mask,
        normed_one,
        inverse_one,
        norm1_gain,
        total_width,
        lambda dep: [sums_part(dep)],
    )
    grad_input_low = (grad_resid + grad_input).astype(LOW)
    grad_input = exchange(grad_input_low.reshape(batch, block, width))
    part = sums_part(grad_input_low, output, *steps(downs, sums[0]))
    part = sums_part(*steps(ups + gateds, part))
    part = sums_part(*steps(downs + gateds, part))
    work = steps(ups + gateds, part)
    grad_input = after(grad_input, part).astype(FULL)
    sums = jnp.concatenate(sums, axis=1)
    narrow = jnp.concatenate(
        [
            grad_norm1_gain,
            grad_norm1_bias,
            jnp.sum(grad_mixed.astype(FULL) * signal.astype(FULL), axis=0),
            jnp.sum(grad_value.astype(FULL), axis=0),
            jnp.sum(grad_gate.astype(FULL), axis=0),
            grad_norm2_gain,
            grad_norm2_bias,
            jnp.sum(grad_out, axis=0),
            sums[3, :, 0],
            jnp.sum(grad_hidden.astype(FULL), axis=0),
        ]
    )
    wide, narrow = sum_small(sums[:3].reshape(3 * width, 2 * states), narrow)
    wide = wide.reshape(3, width, 2 * states).transpose(0, 2, 1)
    chains = downs + ups + gateds
    while any(chain.steps_left() > 0 for chain in chains):
        work = steps(chains, *work)
    vectors = [narrow[k * width : (k + 1) * width] for k in range(9)]
    vectors.insert(2, vectors.pop(8))

    zero = 0 * chan_me
    down = finish(downs[0], zero, chan_me >> 1, chan_me & 1)
    up = finish(ups[0], chan_me * (seqs // chans), zero, zero)
    gated = finish(gateds[0], chan_me * (seqs // chans), zero, zero)
    return (
        output,
        grad_input,
        vectors[0],
        vectors[1],
        wide[0, :states],
        wide[0, states:],
        wide[1].reshape(2, states, width),
        wide[2].reshape(2, states, width),
        vectors[2],
        vectors[3],
        gated[:, :width],
        vectors[4],
        gated[:, width:],
        vectors[5],
        vectors[6],
        vectors[7],
        up,
        narrow[9 * width :],
        down,
        vectors[8],
    )


def solution(mesh):
    in_specs = (
        P(None, "seq", "chan"),
        P(),
        P("chan"),
        P("chan"),
        P(None, "chan"),
        P(None, "chan"),
        P(None, None, "chan"),
        P(None, None, "chan"),
        P("chan"),
        P("chan"),
        P(None, "chan"),
        P("chan"),
        P(None, "chan"),
        P("chan"),
        P("chan"),
        P("chan"),
        P(None, "chan"),
        P("chan"),
        P("chan", None),
        P("chan"),
        P(None, "seq", "chan"),
    )
    out_specs = (
        P(None, "seq", "chan"),
        P(None, "seq", "chan"),
        P("chan"),
        P("chan"),
        P(None, "chan"),
        P(None, "chan"),
        P(None, None, "chan"),
        P(None, None, "chan"),
        P("chan"),
        P("chan"),
        P(None, "chan"),
        P("chan"),
        P(None, "chan"),
        P("chan"),
        P("chan"),
        P("chan"),
        P(None, "chan"),
        P("chan"),
        P("chan", None),
        P("chan"),
    )
    return jax.shard_map(body, mesh=mesh, in_specs=in_specs, out_specs=out_specs, check_vma=False)
```

time: 1390 us -> 402 us (0.29)
  waiting for transfers between devices: 421 us -> 94.5 us
  other arithmetic: 321 us -> 25.9 us
  local copies, waits for them, and re-layouts: 308 us -> 22.8 us
  matrix products: 243 us -> 38.5 us
  Pallas kernels: 0 us -> 130 us
  starting transfers between devices: 0.37 us -> 83.7 us
  blocking collectives: 65.6 us -> 0 us
    psum x1 -> x0, waiting for transfers between devices: 245 us -> none  [body(): lax.psum((grad_norm1_gain, grad_norm1_bias, pulled[3], pulled[4], pulled[...]
    dot_general x27, matrix products: 243 us -> 38.5 us  [the longest x12 21.1 us: dot_t(): lax.dot_general(a, b, (((1,), (1,)), ((), ())), preferred_element_type=FULL)]
    pallas_call x0 -> x18, Pallas kernels: none -> 130 us  [the longest x4 33.7 us: s4_sums(): pl.pallas_call(lambda *refs: sums_kernel(block, *refs), grid=(steps,), in...]
    reduce_sum x9 -> x8, other arithmetic: 126 us -> 8.95 us  [the longest x2 3.2 us: layer_backward(): jnp.sum(grad_out * normed, axis=0)]
    reduce_scatter x3 -> x0, waiting for transfers between devices: 111 us -> none  [the longest x1 44.6 us: body(): lax.psum_scatter(activ_terms, 'chan', scatter_dimension=2, tiled=True)]
    gather x6 -> x0, local copies, waits for them, and re-layouts: 99.6 us -> none  [the longest x2 80.1 us: s4_out(): kernel[jnp.maximum(lags, 0)]]
    scatter-add x1 -> x0, other arithmetic: 98.6 us -> none  [s4_out(): kernel[jnp.maximum(lags, 0)]]
    ppermute x0 -> x54, waiting for transfers between devices: none -> 81.2 us  [swap(): lax.ppermute(x, axis, [(i, i ^ distance) for i in range(lax.axis_size(axi...]
  transfers between devices with their start and end apart: 9 -> 60, of which waited for: 7 -> 17; matrix products, arithmetic and copies ran while one was open for 41% -> 17% of each run, Pallas kernels for 0% -> 29%
where the time goes in v1:
time: 402 us; the launch traced here: 397 us
  Pallas kernels  130 us (32%)
  waiting for transfers between devices  94.5 us (24%)
  starting transfers between devices  83.7 us (21%)
  matrix products  38.5 us (10%)
  other arithmetic  25.9 us (6%)
  local copies, waits for them, and re-layouts  22.8 us (6%)
    ppermute x54, waiting for transfers between devices, swap(): lax.ppermute(x, axis, [(i, i ^ distance) for i in range(lax.axis_size(axi...  81.2 us
    ppermute x54, starting transfers between devices, swap(): lax.ppermute(x, axis, [(i, i ^ distance) for i in range(lax.axis_size(axi...  56.1 us
    pallas_call x4, Pallas kernels, s4_sums(): pl.pallas_call(lambda *refs: sums_kernel(block, *refs), grid=(steps,), in...  33.7 us
    pallas_call x2, Pallas kernels, s4_tables(): pl.pallas_call(tables_kernel, grid=(steps,), in_specs=[pl.BlockSpec((8, C...  22.8 us
    dot_general x12, matrix products, dot_t(): lax.dot_general(a, b, (((1,), (1,)), ((), ())), preferred_element_type=FULL)  21.1 us
    all_to_all x4, starting transfers between devices, exchange(): return lax.all_to_all(x, 'seq', 0, 0, axis_index_groups=groups, tiled=True)  20.7 us
    pallas_call x1, Pallas kernels, s4_forward(): pl.pallas_call(forward_kernel, grid=(width // CHANNELS,), in_specs=[whole...  18.7 us
    pallas_call x1, Pallas kernels, s4_backward(): pl.pallas_call(backward_kernel, grid=(width // CHANNELS,), in_specs=[whol...  17.6 us
  transfers between devices with their start and end apart: 60, of which 17 were waited for; matrix products, arithmetic and copies ran while one was open for 17% of the time, Pallas kernels for 29%

profile of v1, /device:TPU:0, one launch (start us, length us, event | category | flops | bytes accessed | tf_op | source)
XLA Modules:
  0.0 397.0 jit_solution(2917766857728810617)
XLA Ops:
  0.7 7.4 %all-to-all-start = ((bf16[8,128,256]{2,1,0:T(8,128)(2,1)}), bf16[8,128,256]{2,1,0:T(8,128)(2,1)S(1)}, u32[]{:S(2)}, u32[]{:S(2)}) async-start(bf16[8,128,256]{2,1,0:T(8,128)(2,1)} %param.21), calls=%async_computation | async-start | bytes 1048576 | tf_op jit(solution)/shard_map/all_to_all | solution.py:780
  8.1 5.1 %s4_consts.1 = (f32[30,256,128]{2,1,0:T(8,128)}, f32[8,256,128]{2,1,0:T(8,128)}) custom-call(f32[64,256]{1,0:T(8,128)} %refs_0_.1, f32[64,256]{1,0:T(8,128)} %refs_1_.1, f32[2,64,256]{2,1,0:T(8,128)} %refs_2_.1, f32[2,64,256]{2,1,0:T(8,128)} %refs_3_.1, f32[1,256]{1,0:T(1,128)} %bitcast.120), custom_call_target="tpu_custom_call" | custom-call | bytes 600000 | tf_op jit(solution)/shard_map/s4_consts/pallas_call | solution.py:332
  13.2 11.4 %s4_tables.2 = (bf16[256,256,128]{2,1,0:T(8,128)(2,1)}, bf16[256,128,128]{2,1,0:T(8,128)(2,1)}) custom-call(f32[8,256,128]{2,1,0:T(8,128)} %get-tuple-element.94.base, f32[30,256,128]{2,1,0:T(8,128)} %get-tuple-element.95.consts.refs_9_), custom_call_target="tpu_custom_call" | custom-call | bytes 1200000 | tf_op jit(solution)/shard_map/s4_tables/pallas_call | solution.py:400
  25.5 6.2 %all-to-all-start.1 = ((bf16[8,128,256]{2,1,0:T(8,128)(2,1)}), bf16[8,128,256]{2,1,0:T(8,128)(2,1)S(1)}, u32[]{:S(2)}, u32[]{:S(2)}) async-start(bf16[8,128,256]{2,1,0:T(8,128)(2,1)} %param.41), calls=%async_computation.1 | async-start | bytes 1048576 | tf_op jit(solution)/shard_map/all_to_all | solution.py:780
  38.5 11.4 %s4_tables.3 = (bf16[256,256,128]{2,1,0:T(8,128)(2,1)}, bf16[256,128,128]{2,1,0:T(8,128)(2,1)}) custom-call(f32[8,256,128]{2,1,0:T(8,128)} %get-tuple-element.94.base, f32[30,256,128]{2,1,0:T(8,128)} %get-tuple-element.95.consts.refs_9_, bf16[256,256,128]{2,1,0:T(8,128)(2,1)} %get-tuple-element.96.refs_0_, ...), custom_call_target="tpu_custom_call", output_to_operand_aliasing={{0}: (2, {}), {1}: (3, {})} | custom-call | bytes 1200000 | tf_op jit(solution)/shard_map/s4_tables/pallas_call | solution.py:400
  56.3 18.7 %s4_forward.1 = (bf16[1024,256]{1,0:T(8,128)(2,1)}, f32[1024,256]{1,0:T(8,128)}, f32[256,8,128]{2,1,0:T(8,128)}, f32[256,8,128]{2,1,0:T(8,128)}, f32[256,8,128]{2,1,0:T(8,128)}, /*index=5*/f32[256,8,128]{2,1,0:T(8,128)}) custom-call(bf16[1024,256]{1,0:T(8,128)(2,1)} %fusion.51.signal, f32[1,256]{1,0:T(1,128)} %bitcast.119, ...), custom_call_target="tpu_custom_call" | custom-call | bytes 1800000 | tf_op jit(solution)/shard_map/s4_forward/pallas_call | solution.py:515
  78.1 11.5 %collective-permute-done.5 = bf16[1024,256]{1,0:T(8,128)(2,1)S(1)} collective-permute-done((bf16[1024,256]{1,0:T(8,128)(2,1)}, bf16[1024,256]{1,0:T(8,128)(2,1)S(1)}, u32[]{:S(2)}, u32[]{:S(2)}) %collective-permute-start.5) | collective-permute-done | bytes 524320 | tf_op jit(solution)/shard_map/ppermute | solution.py:18
  100.0 2.8 fusion.72
  103.5 7.8 %collective-permute-done.11 = bf16[1024,256]{1,0:T(8,128)(2,1)S(1)} collective-permute-done((bf16[1024,256]{1,0:T(8,128)(2,1)S(1)}, bf16[1024,256]{1,0:T(8,128)(2,1)S(1)}, u32[]{:S(2)}, u32[]{:S(2)}) %collective-permute-start.11) | collective-permute-done | bytes 524320 | tf_op jit(solution)/shard_map/ppermute | solution.py:18
  113.3 3.2 multiply_convert_fusion
  116.5 6.7 %convert_reduce_fusion = (f32[1024]{0:T(1024)}, bf16[1024,1024]{1,0:T(8,128)(2,1)S(1)}) fusion(f32[1024,1024]{1,0:T(8,128)S(1)} %get-tuple-element.264, bf16[1024,256]{1,0:T(8,128)(2,1)} %collective-permute-done.17, bf16[1024,1024]{1,0:T(8,128)(2,1)} %param.39, s32[]{:T(128)S(6)} %select_n.51, f32[1024,1024]{1,0:T(8,128)S(1)} %fusion.66, ...), kind=kOutput, calls=%fused_computation.9 | convolution fusion | flops 563084288 | bytes 19927044 | tf_op jit(solution)/shard_map/dot_general | solution.py:358
  133.3 3.5 fusion.34.refs_0_
  136.8 2.6 fusion.31.refs_0_
  139.5 5.8 %collective-permute-done.20 = bf16[1024,256]{1,0:T(8,128)(2,1)S(1)} collective-permute-done((bf16[1024,256]{1,0:T(8,128)(2,1)S(1)}, bf16[1024,256]{1,0:T(8,128)(2,1)S(1)}, u32[]{:S(2)}, u32[]{:S(2)}) %collective-permute-start.20) | collective-permute-done | bytes 524320 | tf_op jit(solution)/shard_map/ppermute | solution.py:18
  149.8 5.3 %collective-permute-done.23 = f32[2,1024]{1,0:T(2,128)S(1)} collective-permute-done((f32[2,1024]{1,0:T(2,128)S(1)}, f32[2,1024]{1,0:T(2,128)S(1)}, u32[]{:S(2)}, u32[]{:S(2)}) %collective-permute-start.23) | collective-permute-done | bytes 8224 | tf_op jit(solution)/shard_map/ppermute | solution.py:18
  157.1 2.6 convert_reduce_fusion.3
  165.0 3.6 all-to-all-start.2
  176.2 6.4 %collective-permute-done.27.refs_1_ = bf16[512,1024]{1,0:T(8,128)(2,1)} collective-permute-done((bf16[512,1024]{1,0:T(8,128)(2,1)}, bf16[512,1024]{1,0:T(8,128)(2,1)}, u32[]{:S(2)}, u32[]{:S(2)}) %collective-permute-start.27) | collective-permute-done | bytes 1048608 | tf_op jit(solution)/shard_map/ppermute | solution.py:18
  182.6 4.2 %split_sum.3 = (bf16[128,1024]{1,0:T(8,128)(2,1)}, bf16[128,1024]{1,0:T(8,128)(2,1)}, bf16[128,1024]{1,0:T(8,128)(2,1)}, bf16[128,1024]{1,0:T(8,128)(2,1)}) custom-call(s32[3]{0:T(128)} %get-tuple-element.270.scalars, bf16[1024,1024]{1,0:T(8,128)(2,1)} %copy-done.4, bf16[512,1024]{1,0:T(8,128)(2,1)} %collective-permute-done.27.refs_1_), custom_call_target="tpu_custom_call" | custom-call | bytes 200000 | tf_op jit(solution)/shard_map/split_sum/pallas_call | solution.py:76
  186.8 3.1 collective-permute-start.31
  198.0 17.6 %s4_backward.1 = (f32[1024,256]{1,0:T(8,128)}, f32[256,8,128]{2,1,0:T(8,128)}, f32[256,8,128]{2,1,0:T(8,128)}, f32[256,8,128]{2,1,0:T(8,128)}, f32[256,8,128]{2,1,0:T(8,128)}) custom-call(bf16[1024,256]{1,0:T(8,128)(2,1)} %get-tuple-element.226.grads, f32[30,256,128]{2,1,0:T(8,128)} %get-tuple-element.95.consts.refs_9_, ...), custom_call_target="tpu_custom_call" | custom-call | bytes 1800000 | tf_op jit(solution)/shard_map/s4_backward/pallas_call | solution.py:592
  217.8 8.4 %s4_sums.4 = f32[4,64,128]{2,1,0:T(8,128)} custom-call(f32[256,8,128]{2,1,0:T(8,128)} %get-tuple-element.118.refs_0_, f32[256,8,128]{2,1,0:T(8,128)} %get-tuple-element.119.refs_1_, f32[256,8,128]{2,1,0:T(8,128)} %get-tuple-element.120.refs_2_, f32[256,8,128]{2,1,0:T(8,128)} %get-tuple-element.121.refs_3_, f32[256,8,128]{2,1,0:T(8,128)} %get-tuple-element.122.refs_4_, ...), custom_call_target="tpu_custom_call" | custom-call | bytes 450000 | tf_op jit(solution)/shard_map/s4_sums/pallas_call | solution.py:698
  233.1 8.4 %s4_sums.5 = f32[4,64,128]{2,1,0:T(8,128)} custom-call(f32[256,8,128]{2,1,0:T(8,128)} %get-tuple-element.118.refs_0_, f32[256,8,128]{2,1,0:T(8,128)} %get-tuple-element.119.refs_1_, f32[256,8,128]{2,1,0:T(8,128)} %get-tuple-element.120.refs_2_, f32[256,8,128]{2,1,0:T(8,128)} %get-tuple-element.121.refs_3_, f32[256,8,128]{2,1,0:T(8,128)} %get-tuple-element.122.refs_4_, ...), custom_call_target="tpu_custom_call" | custom-call | bytes 450000 | tf_op jit(solution)/shard_map/s4_sums/pallas_call | solution.py:698
  241.6 3.7 split_sum.5
  246.7 2.4 collective-permute-start.40
  251.1 5.2 %collective-permute-done.39 = bf16[128,512]{1,0:T(8,128)(2,1)S(1)} collective-permute-done((bf16[128,512]{1,0:T(8,128)(2,1)}, bf16[128,512]{1,0:T(8,128)(2,1)S(1)}, u32[]{:S(2)}, u32[]{:S(2)}) %collective-permute-start.39) | collective-permute-done | bytes 131104 | tf_op jit(solution)/shard_map/ppermute | solution.py:18
  256.3 2.6 collective-permute-start.36
  258.9 4.4 %split_sum.4 = (bf16[128,1024]{1,0:T(8,128)(2,1)}, bf16[128,1024]{1,0:T(8,128)(2,1)}, bf16[128,1024]{1,0:T(8,128)(2,1)}, bf16[128,1024]{1,0:T(8,128)(2,1)}) custom-call(s32[3]{0:T(128)} %get-tuple-element.269.scalars, bf16[1024,1024]{1,0:T(8,128)(2,1)} %copy-done.3, bf16[512,1024]{1,0:T(8,128)(2,1)} %collective-permute-done.37.refs_1_), custom_call_target="tpu_custom_call" | custom-call | bytes 200000 | tf_op jit(solution)/shard_map/split_sum/pallas_call | solution.py:76
  263.3 8.4 %s4_sums.6 = f32[4,64,128]{2,1,0:T(8,128)} custom-call(f32[256,8,128]{2,1,0:T(8,128)} %get-tuple-element.118.refs_0_, f32[256,8,128]{2,1,0:T(8,128)} %get-tuple-element.119.refs_1_, f32[256,8,128]{2,1,0:T(8,128)} %get-tuple-element.120.refs_2_, f32[256,8,128]{2,1,0:T(8,128)} %get-tuple-element.121.refs_3_, f32[256,8,128]{2,1,0:T(8,128)} %get-tuple-element.122.refs_4_, ...), custom_call_target="tpu_custom_call" | custom-call | bytes 450000 | tf_op jit(solution)/shard_map/s4_sums/pallas_call | solution.py:698
  273.3 2.8 join.3.own
  276.1 8.5 %s4_sums.7 = f32[4,64,128]{2,1,0:T(8,128)} custom-call(f32[256,8,128]{2,1,0:T(8,128)} %get-tuple-element.118.refs_0_, f32[256,8,128]{2,1,0:T(8,128)} %get-tuple-element.119.refs_1_, f32[256,8,128]{2,1,0:T(8,128)} %get-tuple-element.120.refs_2_, f32[256,8,128]{2,1,0:T(8,128)} %get-tuple-element.121.refs_3_, f32[256,8,128]{2,1,0:T(8,128)} %get-tuple-element.122.refs_4_, ...), custom_call_target="tpu_custom_call" | custom-call | bytes 450000 | tf_op jit(solution)/shard_map/s4_sums/pallas_call | solution.py:698
  287.4 3.4 all-to-all-start.4
  290.8 2.8 collective-permute-start.46
  296.4 2.8 collective-permute-start.42
  300.6 16.7 %collective-permute-done.46 = bf16[128,1024]{1,0:T(8,128)(2,1)S(1)} collective-permute-done((bf16[128,1024]{1,0:T(8,128)(2,1)}, bf16[128,1024]{1,0:T(8,128)(2,1)S(1)}, u32[]{:S(2)}, u32[]{:S(2)}) %collective-permute-start.46) | collective-permute-done | bytes 262176 | tf_op jit(solution)/shard_map/ppermute | solution.py:18
  318.2 8.4 %collective-permute-done.48 = bf16[128,1024]{1,0:T(8,128)(2,1)S(1)} collective-permute-done((bf16[128,1024]{1,0:T(8,128)(2,1)S(1)}, bf16[128,1024]{1,0:T(8,128)(2,1)S(1)}, u32[]{:S(2)}, u32[]{:S(2)}) %collective-permute-start.48) | collective-permute-done | bytes 262176 | tf_op jit(solution)/shard_map/ppermute | solution.py:18
  327.4 3.5 all-to-all-start.3
  332.1 2.9 collective-permute-start.49
  337.2 2.5 join.4.own
  341.8 13.2 %all-to-all-done.3 = bf16[8,128,256]{2,1,0:T(8,128)(2,1)S(1)} async-done(((bf16[8,128,256]{2,1,0:T(8,128)(2,1)}), bf16[8,128,256]{2,1,0:T(8,128)(2,1)S(1)}, u32[]{:S(2)}, u32[]{:S(2)}) %all-to-all-start.3) | async-done | bytes 524320 | tf_op jit(solution)/shard_map/all_to_all | solution.py:780
  355.7 3.4 all-to-all-start.5
  361.9 6.6 %collective-permute-done.51.refs_3_ = bf16[128,1024]{1,0:T(8,128)(2,1)} collective-permute-done((bf16[128,1024]{1,0:T(8,128)(2,1)S(1)}, bf16[128,1024]{1,0:T(8,128)(2,1)}, u32[]{:S(2)}, u32[]{:S(2)}) %collective-permute-start.51) | collective-permute-done | bytes 262176 | tf_op jit(solution)/shard_map/ppermute | solution.py:18
  368.5 2.8 join.5.own
  372.1 3.1 finish.3
  375.2 3.0 fusion.129
  383.6 4.2 %collective-permute-done.53.received = bf16[512,1024]{1,0:T(8,128)(2,1)} collective-permute-done((bf16[512,1024]{1,0:T(8,128)(2,1)S(1)}, bf16[512,1024]{1,0:T(8,128)(2,1)}, u32[]{:S(2)}, u32[]{:S(2)}) %collective-permute-start.53) | collective-permute-done | bytes 1048608 | tf_op jit(solution)/shard_map/ppermute | solution.py:18
  387.8 4.0 %finish.5 = f32[1024,1024]{1,0:T(8,128)} custom-call(s32[3]{0:T(128)} %pad_add_fusion.2.scalars, bf16[512,1024]{1,0:T(8,128)(2,1)} %join.3.own, bf16[512,1024]{1,0:T(8,128)(2,1)} %collective-permute-done.53.received), custom_call_target="tpu_custom_call" | custom-call | bytes 300000 | tf_op jit(solution)/shard_map/finish/pallas_call | solution.py:215
  391.8 4.2 %finish.4 = f32[1024,1024]{1,0:T(8,128)} custom-call(s32[3]{0:T(128)} %stack.102.scalars, bf16[512,1024]{1,0:T(8,128)(2,1)} %join.5.own, bf16[512,1024]{1,0:T(8,128)(2,1)} %collective-permute-done.52.received), custom_call_target="tpu_custom_call" | custom-call | bytes 300000 | tf_op jit(solution)/shard_map/finish/pallas_call | solution.py:215
  (343 shorter events, 105.6 us)
Async XLA Ops:
  0.7 23.9 %all-to-all-start = ((bf16[8,128,256]{2,1,0:T(8,128)(2,1)}), bf16[8,128,256]{2,1,0:T(8,128)(2,1)S(1)}, u32[]{:S(2)}, u32[]{:S(2)}) async-start(bf16[8,128,256]{2,1,0:T(8,128)(2,1)} %param.21), calls=%async_computation | async-start | bytes 1048576 | tf_op jit(solution)/shard_map/all_to_all | solution.py:780
  25.5 25.8 %all-to-all-start.1 = ((bf16[8,128,256]{2,1,0:T(8,128)(2,1)}), bf16[8,128,256]{2,1,0:T(8,128)(2,1)S(1)}, u32[]{:S(2)}, u32[]{:S(2)}) async-start(bf16[8,128,256]{2,1,0:T(8,128)(2,1)} %param.41), calls=%async_computation.1 | async-start | bytes 1048576 | tf_op jit(solution)/shard_map/all_to_all | solution.py:780
  35.2 14.8 %collective-permute-start.2 = (f32[2,1024]{1,0:T(2,128)}, f32[2,1024]{1,0:T(2,128)}, u32[]{:S(2)}, u32[]{:S(2)}) collective-permute-start(f32[2,1024]{1,0:T(2,128)} %pad_maximum_fusion.14.refs_2_), channel_id=1, source_target_pairs={{0,3},{1,2},{2,1},{3,0},{4,7},{5,6},{6,5},{7,4},{8,11},{9,10},{10,... | collective-permute-start | bytes 24584 | tf_op jit(solution)/shard_map/ppermute | solution.py:18
  35.3 14.7 %collective-permute-start = (f32[2,1024]{1,0:T(2,128)}, f32[2,1024]{1,0:T(2,128)}, u32[]{:S(2)}, u32[]{:S(2)}) collective-permute-start(f32[2,1024]{1,0:T(2,128)} %pad_maximum_fusion.14.refs_2_), channel_id=1, source_target_pairs={{0,1},{1,0},{2,3},{3,2},{4,5},{5,4},{6,7},{7,6},{8,9},{9,8},{10,11... | collective-permute-start | bytes 24584 | tf_op jit(solution)/shard_map/ppermute | solution.py:18
  36.8 13.2 %collective-permute-start.1 = (f32[2,1024]{1,0:T(2,128)}, f32[2,1024]{1,0:T(2,128)}, u32[]{:S(2)}, u32[]{:S(2)}) collective-permute-start(f32[2,1024]{1,0:T(2,128)} %pad_maximum_fusion.14.refs_2_), channel_id=1, source_target_pairs={{0,2},{1,3},{2,0},{3,1},{4,6},{5,7},{6,4},{7,5},{8,10},{9,11},{10,... | collective-permute-start | bytes 24584 | tf_op jit(solution)/shard_map/ppermute | solution.py:18
  51.3 23.7 %collective-permute-start.3 = (bf16[1024,256]{1,0:T(8,128)(2,1)S(1)}, bf16[1024,256]{1,0:T(8,128)(2,1)S(1)}, u32[]{:S(2)}, u32[]{:S(2)}) collective-permute-start(bf16[1024,256]{1,0:T(8,128)(2,1)S(1)} %bitcast.75), channel_id=1, source_target_pairs={{0,2},{1,3},{2,0},{3,1},{4,6},{5,7},{6,4},{7,5},{8,10},{9,11},{10,... | collective-permute-start | bytes 1572872 | tf_op jit(solution)/shard_map/ppermute | solution.py:18
  74.9 25.1 %collective-permute-start.16 = (bf16[1024,256]{1,0:T(8,128)(2,1)S(1)}, bf16[1024,256]{1,0:T(8,128)(2,1)S(1)}, u32[]{:S(2)}, u32[]{:S(2)}) collective-permute-start(bf16[1024,256]{1,0:T(8,128)(2,1)S(1)} %bitcast.76), channel_id=1, source_target_pairs={{0,1},{1,0},{2,3},{3,2},{4,5},{5,4},{6,7},{7,6},{8,9},{9,8},{10,11... | collective-permute-start | bytes 1572872 | tf_op jit(solution)/shard_map/ppermute | solution.py:18
  75.1 14.6 %collective-permute-start.5 = (bf16[1024,256]{1,0:T(8,128)(2,1)}, bf16[1024,256]{1,0:T(8,128)(2,1)S(1)}, u32[]{:S(2)}, u32[]{:S(2)}) collective-permute-start(bf16[1024,256]{1,0:T(8,128)(2,1)} %get-tuple-element.104), channel_id=1, source_target_pairs={{0,2},{1,3},{2,0},{3,1},{4,6},{5,7},{6,4},{7,5},{8,10},{9,11},{10,... | collective-permute-start | bytes 1572872 | tf_op jit(solution)/shard_map/ppermute | solution.py:18
  77.1 13.0 %collective-permute-start.4 = (bf16[1024,256]{1,0:T(8,128)(2,1)S(1)}, bf16[1024,256]{1,0:T(8,128)(2,1)S(1)}, u32[]{:S(2)}, u32[]{:S(2)}) collective-permute-start(bf16[1024,256]{1,0:T(8,128)(2,1)S(1)} %copy-done.29), channel_id=1, source_target_pairs={{0,1},{1,0},{2,3},{3,2},{4,5},{5,4},{6,7},{7,6},{8,9},{9,8},{10,11... | collective-permute-start | bytes 1572872 | tf_op jit(solution)/shard_map/ppermute | solution.py:18
  77.3 39.2 %collective-permute-start.17 = (bf16[1024,256]{1,0:T(8,128)(2,1)S(1)}, bf16[1024,256]{1,0:T(8,128)(2,1)}, u32[]{:S(2)}, u32[]{:S(2)}) collective-permute-start(bf16[1024,256]{1,0:T(8,128)(2,1)S(1)} %collective-permute-done.3), channel_id=1, source_target_pairs={{0,1},{1,0},{2,3},{3,2},{4,5},{5,4},{6,7},{7,6},{8,9},{9,8},{10,11... | collective-permute-start | bytes 1572872 | tf_op jit(solution)/shard_map/ppermute | solution.py:18
  98.4 12.9 %collective-permute-start.11 = (bf16[1024,256]{1,0:T(8,128)(2,1)S(1)}, bf16[1024,256]{1,0:T(8,128)(2,1)S(1)}, u32[]{:S(2)}, u32[]{:S(2)}) collective-permute-start(bf16[1024,256]{1,0:T(8,128)(2,1)S(1)} %add_convert_fusion.2), channel_id=1, source_target_pairs={{0,2},{1,3},{2,0},{3,1},{4,6},{5,7},{6,4},{7,5},{8,10},{9,11},{10,... | collective-permute-start | bytes 1572872 | tf_op jit(solution)/shard_map/ppermute | solution.py:18
  102.8 9.3 %collective-permute-start.10 = (bf16[1024,256]{1,0:T(8,128)(2,1)S(1)}, bf16[1024,256]{1,0:T(8,128)(2,1)S(1)}, u32[]{:S(2)}, u32[]{:S(2)}) collective-permute-start(bf16[1024,256]{1,0:T(8,128)(2,1)S(1)} %add_convert_fusion.2), channel_id=1, source_target_pairs={{0,1},{1,0},{2,3},{3,2},{4,5},{5,4},{6,7},{7,6},{8,9},{9,8},{10,11... | collective-permute-start | bytes 1572872 | tf_op jit(solution)/shard_map/ppermute | solution.py:18
  127.2 12.2 %collective-permute-start.18 = (bf16[1024,256]{1,0:T(8,128)(2,1)S(1)}, bf16[1024,256]{1,0:T(8,128)(2,1)S(1)}, u32[]{:S(2)}, u32[]{:S(2)}) collective-permute-start(bf16[1024,256]{1,0:T(8,128)(2,1)S(1)} %convolution_convert_fusion.3), channel_id=1, source_target_pairs={{0,1},{1,0},{2,3},{3,2},{4,5},{5,4},{6,7},{7,6},{8,9},{9,8},{10,11... | collective-permute-start | bytes 1572872 | tf_op jit(solution)/shard_map/ppermute | solution.py:18
  127.8 29.3 %collective-permute-start.13 = (bf16[1024,256]{1,0:T(8,128)(2,1)S(1)}, bf16[1024,256]{1,0:T(8,128)(2,1)S(1)}, u32[]{:S(2)}, u32[]{:S(2)}) collective-permute-start(bf16[1024,256]{1,0:T(8,128)(2,1)S(1)} %convolution_convert_fusion.5), channel_id=1, source_target_pairs={{0,1},{1,0},{2,3},{3,2},{4,5},{5,4},{6,7},{7,6},{8,9},{9,8},{10,11... | collective-permute-start | bytes 1572872 | tf_op jit(solution)/shard_map/ppermute | solution.py:18
  130.4 14.8 %collective-permute-start.20 = (bf16[1024,256]{1,0:T(8,128)(2,1)S(1)}, bf16[1024,256]{1,0:T(8,128)(2,1)S(1)}, u32[]{:S(2)}, u32[]{:S(2)}) collective-permute-start(bf16[1024,256]{1,0:T(8,128)(2,1)S(1)} %fusion.63), channel_id=1, source_target_pairs={{0,2},{1,3},{2,0},{3,1},{4,6},{5,7},{6,4},{7,5},{8,10},{9,11},{10,... | collective-permute-start | bytes 1572872 | tf_op jit(solution)/shard_map/ppermute | solution.py:18
  132.7 24.4 %collective-permute-start.15 = (bf16[1024,256]{1,0:T(8,128)(2,1)S(1)}, bf16[1024,256]{1,0:T(8,128)(2,1)S(1)}, u32[]{:S(2)}, u32[]{:S(2)}) collective-permute-start(bf16[1024,256]{1,0:T(8,128)(2,1)S(1)} %add_convert_fusion.1), channel_id=1, source_target_pairs={{0,2},{1,3},{2,0},{3,1},{4,6},{5,7},{6,4},{7,5},{8,10},{9,11},{10,... | collective-permute-start | bytes 1572872 | tf_op jit(solution)/shard_map/ppermute | solution.py:18
  146.6 10.4 %collective-permute-start.21 = (f32[2,1024]{1,0:T(2,128)S(1)}, f32[2,1024]{1,0:T(2,128)S(1)}, u32[]{:S(2)}, u32[]{:S(2)}) collective-permute-start(f32[2,1024]{1,0:T(2,128)S(1)} %pad_maximum_fusion.16), channel_id=1, source_target_pairs={{0,1},{1,0},{2,3},{3,2},{4,5},{5,4},{6,7},{7,6},{8,9},{9,8},{10,11... | collective-permute-start | bytes 24584 | tf_op jit(solution)/shard_map/ppermute | solution.py:18
  155.0 27.5 %collective-permute-start.27 = (bf16[512,1024]{1,0:T(8,128)(2,1)}, bf16[512,1024]{1,0:T(8,128)(2,1)}, u32[]{:S(2)}, u32[]{:S(2)}) collective-permute-start(bf16[512,1024]{1,0:T(8,128)(2,1)} %constant_dynamic-slice_fusion.2), channel_id=1, source_target_pairs={{0,4},{4,0},{8,12},{12,8},{16,20},{20,16},{24,28},{28,24},{1,5},{5... | collective-permute-start | bytes 3145736 | tf_op jit(solution)/shard_map/ppermute | solution.py:18
  161.8 10.5 %collective-permute-start.25 = (bf16[1024,256]{1,0:T(8,128)(2,1)}, bf16[1024,256]{1,0:T(8,128)(2,1)}, u32[]{:S(2)}, u32[]{:S(2)}) collective-permute-start(bf16[1024,256]{1,0:T(8,128)(2,1)} %convolution_convert_fusion), channel_id=1, source_target_pairs={{0,1},{1,0},{2,3},{3,2},{4,5},{5,4},{6,7},{7,6},{8,9},{9,8},{10,11... | collective-permute-start | bytes 1572872 | tf_op jit(solution)/shard_map/ppermute | solution.py:18
  163.5 86.4 %collective-permute-start.37 = (bf16[512,1024]{1,0:T(8,128)(2,1)}, bf16[512,1024]{1,0:T(8,128)(2,1)}, u32[]{:S(2)}, u32[]{:S(2)}) collective-permute-start(bf16[512,1024]{1,0:T(8,128)(2,1)} %constant_dynamic-slice_fusion.1), channel_id=1, source_target_pairs={{0,8},{4,12},{8,0},{12,4},{16,24},{20,28},{24,16},{28,20},{1,9},{5... | collective-permute-start | bytes 3145736 | tf_op jit(solution)/shard_map/ppermute | solution.py:18
  165.0 68.1 %all-to-all-start.2 = ((bf16[8,128,256]{2,1,0:T(8,128)(2,1)}), bf16[8,128,256]{2,1,0:T(8,128)(2,1)S(1)}, u32[]{:S(2)}, u32[]{:S(2)}) async-start(bf16[8,128,256]{2,1,0:T(8,128)(2,1)} %bitcast.13), calls=%async_computation.2 | async-start | bytes 1048576 | tf_op jit(solution)/shard_map/all_to_all | solution.py:780
  170.8 22.7 %collective-permute-start.24 = (bf16[1024,256]{1,0:T(8,128)(2,1)}, bf16[1024,256]{1,0:T(8,128)(2,1)S(1)}, u32[]{:S(2)}, u32[]{:S(2)}) collective-permute-start(bf16[1024,256]{1,0:T(8,128)(2,1)} %convolution_convert_fusion.1), channel_id=1, source_target_pairs={{0,1},{1,0},{2,3},{3,2},{4,5},{5,4},{6,7},{7,6},{8,9},{9,8},{10,11... | collective-permute-start | bytes 1572872 | tf_op jit(solution)/shard_map/ppermute | solution.py:18
  174.7 18.9 %collective-permute-start.26 = (bf16[1024,256]{1,0:T(8,128)(2,1)}, bf16[1024,256]{1,0:T(8,128)(2,1)}, u32[]{:S(2)}, u32[]{:S(2)}) collective-permute-start(bf16[1024,256]{1,0:T(8,128)(2,1)} %fusion.92), channel_id=1, source_target_pairs={{0,2},{1,3},{2,0},{3,1},{4,6},{5,7},{6,4},{7,5},{8,10},{9,11},{10,... | collective-permute-start | bytes 1572872 | tf_op jit(solution)/shard_map/ppermute | solution.py:18
  186.8 39.4 %collective-permute-start.31 = (bf16[128,1024]{1,0:T(8,128)(2,1)}, bf16[128,1024]{1,0:T(8,128)(2,1)S(1)}, u32[]{:S(2)}, u32[]{:S(2)}) collective-permute-start(bf16[128,1024]{1,0:T(8,128)(2,1)} %get-tuple-element.112), channel_id=1, source_target_pairs={{0,16},{4,20},{8,24},{12,28},{16,0},{20,4},{24,8},{28,12},{1,17},{... | collective-permute-start | bytes 786440 | tf_op jit(solution)/shard_map/ppermute | solution.py:18
  189.9 36.4 %collective-permute-start.32 = (bf16[128,1024]{1,0:T(8,128)(2,1)}, bf16[128,1024]{1,0:T(8,128)(2,1)}, u32[]{:S(2)}, u32[]{:S(2)}) collective-permute-start(bf16[128,1024]{1,0:T(8,128)(2,1)} %get-tuple-element.113), channel_id=1, source_target_pairs={{0,8},{4,12},{8,0},{12,4},{16,24},{20,28},{24,16},{28,20},{1,9},{5... | collective-permute-start | bytes 786440 | tf_op jit(solution)/shard_map/ppermute | solution.py:18
  193.6 34.3 %collective-permute-start.33 = (bf16[128,1024]{1,0:T(8,128)(2,1)}, bf16[128,1024]{1,0:T(8,128)(2,1)S(1)}, u32[]{:S(2)}, u32[]{:S(2)}) collective-permute-start(bf16[128,1024]{1,0:T(8,128)(2,1)} %get-tuple-element.114), channel_id=1, source_target_pairs={{0,24},{4,28},{8,16},{12,20},{16,8},{20,12},{24,0},{28,4},{1,25},{... | collective-permute-start | bytes 786440 | tf_op jit(solution)/shard_map/ppermute | solution.py:18
  193.8 47.7 %collective-permute-start.38 = (bf16[512,512]{1,0:T(8,128)(2,1)}, bf16[512,512]{1,0:T(8,128)(2,1)}, u32[]{:S(2)}, u32[]{:S(2)}) collective-permute-start(bf16[512,512]{1,0:T(8,128)(2,1)} %constant_dynamic-slice_fusion), channel_id=1, source_target_pairs={{0,4},{4,0},{8,12},{12,8},{16,20},{20,16},{24,28},{28,24},{1,5},{5... | collective-permute-start | bytes 1572872 | tf_op jit(solution)/shard_map/ppermute | solution.py:18
  229.8 42.1 %collective-permute-start.34 = (bf16[128,1024]{1,0:T(8,128)(2,1)S(1)}, bf16[128,1024]{1,0:T(8,128)(2,1)}, u32[]{:S(2)}, u32[]{:S(2)}) collective-permute-start(bf16[128,1024]{1,0:T(8,128)(2,1)S(1)} %add_convert_fusion.4.refs_0_), channel_id=1, source_target_pairs={{0,16},{4,20},{8,24},{12,28},{16,0},{20,4},{24,8},{28,12},{1,17},{... | collective-permute-start | bytes 786440 | tf_op jit(solution)/shard_map/ppermute | solution.py:18
  245.3 11.1 %collective-permute-start.39 = (bf16[128,512]{1,0:T(8,128)(2,1)}, bf16[128,512]{1,0:T(8,128)(2,1)S(1)}, u32[]{:S(2)}, u32[]{:S(2)}) collective-permute-start(bf16[128,512]{1,0:T(8,128)(2,1)} %get-tuple-element.142), channel_id=1, source_target_pairs={{0,16},{4,20},{8,24},{12,28},{16,0},{20,4},{24,8},{28,12},{1,17},{... | collective-permute-start | bytes 393224 | tf_op jit(solution)/shard_map/ppermute | solution.py:18
  246.7 25.0 %collective-permute-start.40 = (bf16[128,512]{1,0:T(8,128)(2,1)}, bf16[128,512]{1,0:T(8,128)(2,1)S(1)}, u32[]{:S(2)}, u32[]{:S(2)}) collective-permute-start(bf16[128,512]{1,0:T(8,128)(2,1)} %get-tuple-element.143), channel_id=1, source_target_pairs={{0,8},{4,12},{8,0},{12,4},{16,24},{20,28},{24,16},{28,20},{1,9},{5... | collective-permute-start | bytes 393224 | tf_op jit(solution)/shard_map/ppermute | solution.py:18
  249.2 22.6 %collective-permute-start.41 = (bf16[128,512]{1,0:T(8,128)(2,1)}, bf16[128,512]{1,0:T(8,128)(2,1)S(1)}, u32[]{:S(2)}, u32[]{:S(2)}) collective-permute-start(bf16[128,512]{1,0:T(8,128)(2,1)} %get-tuple-element.144), channel_id=1, source_target_pairs={{0,24},{4,28},{8,16},{12,20},{16,8},{20,12},{24,0},{28,4},{1,25},{... | collective-permute-start | bytes 393224 | tf_op jit(solution)/shard_map/ppermute | solution.py:18
  250.0 21.9 %collective-permute-start.35 = (bf16[128,1024]{1,0:T(8,128)(2,1)S(1)}, bf16[128,1024]{1,0:T(8,128)(2,1)S(1)}, u32[]{:S(2)}, u32[]{:S(2)}) collective-permute-start(bf16[128,1024]{1,0:T(8,128)(2,1)S(1)} %add_convert_fusion.4.refs_0_), channel_id=1, source_target_pairs={{0,8},{4,12},{8,0},{12,4},{16,24},{20,28},{24,16},{28,20},{1,9},{5... | collective-permute-start | bytes 786440 | tf_op jit(solution)/shard_map/ppermute | solution.py:18
  256.3 15.6 %collective-permute-start.36 = (bf16[128,1024]{1,0:T(8,128)(2,1)S(1)}, bf16[128,1024]{1,0:T(8,128)(2,1)S(1)}, u32[]{:S(2)}, u32[]{:S(2)}) collective-permute-start(bf16[128,1024]{1,0:T(8,128)(2,1)S(1)} %add_convert_fusion.4.refs_0_), channel_id=1, source_target_pairs={{0,24},{4,28},{8,16},{12,20},{16,8},{20,12},{24,0},{28,4},{1,25},{... | collective-permute-start | bytes 786440 | tf_op jit(solution)/shard_map/ppermute | solution.py:18
  287.4 39.3 %all-to-all-start.4 = ((bf16[8,112,128]{2,1,0:T(8,128)(2,1)}), bf16[8,112,128]{2,1,0:T(8,128)(2,1)S(1)}, u32[]{:S(2)}, u32[]{:S(2)}) async-start(bf16[8,112,128]{2,1,0:T(8,128)(2,1)} %maximum_maximum_fusion), calls=%async_computation.4 | async-start | bytes 458752 | tf_op jit(solution)/shard_map/all_to_all | solution.py:58
  290.8 26.5 %collective-permute-start.46 = (bf16[128,1024]{1,0:T(8,128)(2,1)}, bf16[128,1024]{1,0:T(8,128)(2,1)S(1)}, u32[]{:S(2)}, u32[]{:S(2)}) collective-permute-start(bf16[128,1024]{1,0:T(8,128)(2,1)} %get-tuple-element.136), channel_id=1, source_target_pairs={{0,16},{4,20},{8,24},{12,28},{16,0},{20,4},{24,8},{28,12},{1,17},{... | collective-permute-start | bytes 786440 | tf_op jit(solution)/shard_map/ppermute | solution.py:18
  293.7 24.6 %collective-permute-start.47 = (bf16[128,1024]{1,0:T(8,128)(2,1)S(1)}, bf16[128,1024]{1,0:T(8,128)(2,1)S(1)}, u32[]{:S(2)}, u32[]{:S(2)}) collective-permute-start(bf16[128,1024]{1,0:T(8,128)(2,1)S(1)} %copy-done.70), channel_id=1, source_target_pairs={{0,4},{4,0},{8,12},{12,8},{16,20},{20,16},{24,28},{28,24},{1,5},{5... | collective-permute-start | bytes 786440 | tf_op jit(solution)/shard_map/ppermute | solution.py:18
  295.2 31.5 %collective-permute-start.48 = (bf16[128,1024]{1,0:T(8,128)(2,1)S(1)}, bf16[128,1024]{1,0:T(8,128)(2,1)S(1)}, u32[]{:S(2)}, u32[]{:S(2)}) collective-permute-start(bf16[128,1024]{1,0:T(8,128)(2,1)S(1)} %copy-done.69), channel_id=1, source_target_pairs={{0,20},{4,16},{8,28},{12,24},{16,4},{20,0},{24,12},{28,8},{1,21},{... | collective-permute-start | bytes 786440 | tf_op jit(solution)/shard_map/ppermute | solution.py:18
  296.4 40.1 %collective-permute-start.42 = (bf16[128,512]{1,0:T(8,128)(2,1)S(1)}, bf16[128,512]{1,0:T(8,128)(2,1)S(1)}, u32[]{:S(2)}, u32[]{:S(2)}) collective-permute-start(bf16[128,512]{1,0:T(8,128)(2,1)S(1)} %add_convert_fusion.5.refs_0_), channel_id=1, source_target_pairs={{0,16},{4,20},{8,24},{12,28},{16,0},{20,4},{24,8},{28,12},{1,17},{... | collective-permute-start | bytes 393224 | tf_op jit(solution)/shard_map/ppermute | solution.py:18
  299.2 37.4 %collective-permute-start.43 = (bf16[128,512]{1,0:T(8,128)(2,1)S(1)}, bf16[128,512]{1,0:T(8,128)(2,1)S(1)}, u32[]{:S(2)}, u32[]{:S(2)}) collective-permute-start(bf16[128,512]{1,0:T(8,128)(2,1)S(1)} %add_convert_fusion.5.refs_0_), channel_id=1, source_target_pairs={{0,8},{4,12},{8,0},{12,4},{16,24},{20,28},{24,16},{28,20},{1,9},{5... | collective-permute-start | bytes 393224 | tf_op jit(solution)/shard_map/ppermute | solution.py:18
  317.3 19.2 %collective-permute-start.44 = (bf16[128,512]{1,0:T(8,128)(2,1)S(1)}, bf16[128,512]{1,0:T(8,128)(2,1)}, u32[]{:S(2)}, u32[]{:S(2)}) collective-permute-start(bf16[128,512]{1,0:T(8,128)(2,1)S(1)} %add_convert_fusion.5.refs_0_), channel_id=1, source_target_pairs={{0,24},{4,28},{8,16},{12,20},{16,8},{20,12},{24,0},{28,4},{1,25},{... | collective-permute-start | bytes 393224 | tf_op jit(solution)/shard_map/ppermute | solution.py:18
  327.4 27.6 %all-to-all-start.3 = ((bf16[8,128,256]{2,1,0:T(8,128)(2,1)}), bf16[8,128,256]{2,1,0:T(8,128)(2,1)S(1)}, u32[]{:S(2)}, u32[]{:S(2)}) async-start(bf16[8,128,256]{2,1,0:T(8,128)(2,1)} %bitcast.24), calls=%async_computation.3 | async-start | bytes 1048576 | tf_op jit(solution)/shard_map/all_to_all | solution.py:780
  332.1 29.8 %collective-permute-start.49 = (bf16[128,1024]{1,0:T(8,128)(2,1)S(1)}, bf16[128,1024]{1,0:T(8,128)(2,1)S(1)}, u32[]{:S(2)}, u32[]{:S(2)}) collective-permute-start(bf16[128,1024]{1,0:T(8,128)(2,1)S(1)} %add_convert_fusion.3.refs_0_), channel_id=1, source_target_pairs={{0,16},{4,20},{8,24},{12,28},{16,0},{20,4},{24,8},{28,12},{1,17},{... | collective-permute-start | bytes 786440 | tf_op jit(solution)/shard_map/ppermute | solution.py:18
  335.0 26.9 %collective-permute-start.50 = (bf16[128,1024]{1,0:T(8,128)(2,1)S(1)}, bf16[128,1024]{1,0:T(8,128)(2,1)}, u32[]{:S(2)}, u32[]{:S(2)}) collective-permute-start(bf16[128,1024]{1,0:T(8,128)(2,1)S(1)} %add_convert_fusion.3.refs_0_), channel_id=1, source_target_pairs={{0,4},{4,0},{8,12},{12,8},{16,20},{20,16},{24,28},{28,24},{1,5},{5... | collective-permute-start | bytes 786440 | tf_op jit(solution)/shard_map/ppermute | solution.py:18
  336.5 32.0 %collective-permute-start.51 = (bf16[128,1024]{1,0:T(8,128)(2,1)S(1)}, bf16[128,1024]{1,0:T(8,128)(2,1)}, u32[]{:S(2)}, u32[]{:S(2)}) collective-permute-start(bf16[128,1024]{1,0:T(8,128)(2,1)S(1)} %add_convert_fusion.3.refs_0_), channel_id=1, source_target_pairs={{0,20},{4,16},{8,28},{12,24},{16,4},{20,0},{24,12},{28,8},{1,21},{... | collective-permute-start | bytes 786440 | tf_op jit(solution)/shard_map/ppermute | solution.py:18
  339.7 31.6 %collective-permute-start.45 = (bf16[512,512]{1,0:T(8,128)(2,1)}, bf16[512,512]{1,0:T(8,128)(2,1)S(1)}, u32[]{:S(2)}, u32[]{:S(2)}) collective-permute-start(bf16[512,512]{1,0:T(8,128)(2,1)} %join.4.own), channel_id=1, source_target_pairs={{0,4},{4,0},{8,12},{12,8},{16,20},{20,16},{24,28},{28,24},{1,5},{5... | collective-permute-start | bytes 1572872 | tf_op jit(solution)/shard_map/ppermute | solution.py:18
  355.7 23.5 %all-to-all-start.5 = ((bf16[8,112,128]{2,1,0:T(8,128)(2,1)}), bf16[8,112,128]{2,1,0:T(8,128)(2,1)S(1)}, u32[]{:S(2)}, u32[]{:S(2)}) async-start(bf16[8,112,128]{2,1,0:T(8,128)(2,1)} %broadcast_in_dim.14), calls=%async_computation.5 | async-start | bytes 458752 | tf_op jit(solution)/shard_map/all_to_all | solution.py:58
  359.7 28.0 %collective-permute-start.53 = (bf16[512,1024]{1,0:T(8,128)(2,1)S(1)}, bf16[512,1024]{1,0:T(8,128)(2,1)}, u32[]{:S(2)}, u32[]{:S(2)}) collective-permute-start(bf16[512,1024]{1,0:T(8,128)(2,1)S(1)} %copy-done.5), channel_id=1, source_target_pairs={{0,4},{4,0},{8,12},{12,8},{16,20},{20,16},{24,28},{28,24},{1,5},{5... | collective-permute-start | bytes 3145736 | tf_op jit(solution)/shard_map/ppermute | solution.py:18
  371.3 20.5 %collective-permute-start.52 = (bf16[512,1024]{1,0:T(8,128)(2,1)}, bf16[512,1024]{1,0:T(8,128)(2,1)}, u32[]{:S(2)}, u32[]{:S(2)}) collective-permute-start(bf16[512,1024]{1,0:T(8,128)(2,1)} %join.5.own), channel_id=1, source_target_pairs={{0,8},{4,12},{8,0},{12,4},{16,24},{20,28},{24,16},{28,20},{1,9},{5... | collective-permute-start | bytes 3145736 | tf_op jit(solution)/shard_map/ppermute | solution.py:18
  (84 other events, 877.3 us)

commit v2 on v1

--- a/solution.py
+++ b/solution.py
@@ -37,12 +37,13 @@
     sums = dict(enumerate(parts))
     for bit in range(axis_bits("chan")):
         if marks is not None and bit == axis_bits("chan") - 1:
-            marks.append(sums[1 << bit])
+            marks += [sums[1 << bit], sums[0]]
         for d in sorted(sums, reverse=True):
             if d >> bit & 1:
-                sums[d ^ (1 << bit)] = sums[d ^ (1 << bit)] + swap(
-                    sums.pop(d).astype(LOW), "chan", 1 << bit
-                ).astype(FULL)
+                received = swap(sums.pop(d).astype(LOW), "chan", 1 << bit)
+                if marks is not None and d == 1 << (axis_bits("chan") - 1):
+                    marks.append(received)
+                sums[d ^ (1 << bit)] = sums[d ^ (1 << bit)] + received.astype(FULL)
     return sums[0]
 
 
@@ -58,173 +59,223 @@
     return lax.all_to_all(x, "seq", 0, 0, tiled=True)
 
 
-def split_sum(parts, place, count):
-    rows, columns = min(part.shape[0] for part, _ in parts), parts[0][0].shape[1]
-    block = (rows // count, columns)
-    scalars = jnp.stack([place] + [first for _, first in parts]).astype(jnp.int32)
-
-    def kernel(scalars, *refs):
-        del scalars
-        ins, outs = refs[:-count], refs[-count:]
-        total = sum(ref[...].astype(FULL) for ref in ins).astype(LOW)
-        for e, out in enumerate(outs):
-
-            @pl.when(pl.program_id(0) == e)
-            def _(out=out):
-                out[...] = total
-
+def small_kernel(share, parts, *refs):
+    out = refs[-1]
+    total = sum(parts[k].astype(FULL) for k in range(parts.shape[0]))
+    narrow = total[share : share + 8] + total[share + 8 : share + 16]
+    high = narrow.astype(LOW).astype(FULL)
+    rows = [total[:share], high, narrow - high]
+    fill = total.shape[0] - share - 16
+    if fill:
+        rows.append(jnp.zeros((fill, total.shape[1]), FULL))
+    total = jnp.concatenate(rows, axis=0).astype(LOW)
+    for k in range(parts.shape[0]):
+        out[k] = total
+
+
+def pack_kernel(share, sums, narrow, *refs):
+    packed = refs[-1]
+    seqs, rows, lanes = packed.shape
+    groups, width, _ = sums.shape
+    flat = sums[: groups - 1].reshape((groups - 1) * width, lanes)
+    for k in range(seqs):
+        part = narrow[k]
+        high = part.astype(LOW).astype(FULL)
+        pieces = [flat[k * share : (k + 1) * share], high, part - high]
+        if rows > share + 16:
+            pieces.append(jnp.zeros((rows - share - 16, lanes), FULL))
+        packed[k] = jnp.concatenate(pieces, axis=0).astype(LOW)
+
+
+def sum_small(sums, narrow, deps, late_deps):
+    seqs = lax.axis_size("seq")
+    groups, width, lanes = sums.shape
+    share = (groups - 1) * width // seqs
+    short = -(-narrow.shape[0] // (seqs * lanes))
+    assert short <= 8
+    rows = -(-(share + 16) // 16) * 16
+    narrow_rows = jnp.pad(narrow, (0, seqs * short * lanes - narrow.shape[0])).reshape(seqs, short, lanes)
+    narrow_rows = jnp.pad(narrow_rows, ((0, 0), (0, 8 - short), (0, 0)))
+    here, anywhere = pl.BlockSpec(memory_space=pltpu.VMEM), pl.BlockSpec(memory_space=pl.ANY)
+    packed = pl.pallas_call(
+        lambda *refs: pack_kernel(share, *refs),
+        in_specs=[here] * 2 + [anywhere] * len(deps),
+        out_specs=here,
+        out_shape=jax.ShapeDtypeStruct((seqs, rows, lanes), LOW),
+        compiler_params=pltpu.CompilerParams(vmem_limit_bytes=VMEM),
+        cost_estimate=cost(1),
+        name="pack_small",
+    )(sums, narrow_rows, *deps)
+    total = pl.pallas_call(
+        lambda *refs: small_kernel(share, *refs),
+        in_specs=[here] + [anywhere] * len(late_deps),
+        out_specs=here,
+        out_shape=jax.ShapeDtypeStruct(packed.shape, LOW),
+        compiler_params=pltpu.CompilerParams(vmem_limit_bytes=VMEM),
+        cost_estimate=cost(1),
+        name="sum_small",
+    )(exchange_all(packed), *late_deps)
+    parts = exchange_all(total).astype(FULL)
+    result = parts[:, share : share + short] + parts[:, share + 8 : share + 8 + short]
+    wide = parts[:, :share].reshape(groups - 1, width, lanes)
+    return wide, result.reshape(-1)[: narrow.shape[0]], packed
+
+
+QUAD = 4
+
+
+def deal(x):
+    seqs = lax.axis_size("seq")
+    groups = [list(range(i, i + QUAD)) for i in range(0, seqs, QUAD)]
+    return lax.all_to_all(x.reshape(QUAD, -1, x.shape[1]), "seq", 0, 0, axis_index_groups=groups, tiled=True)
+
+
+class Chain:
+    def __init__(self, parts, halves):
+        self.masks = [1 << bit for bit in range(axis_bits("seq")) if 1 << bit >= QUAD]
+        self.parts = parts
+        self.halves = halves
+        self.tasks = ["deal" if halves else "whole", "sum"]
+
+    def accept(self, task, outs):
+        if task == "deal":
+            self.parts = [outs[0], swap(outs[1], "seq", self.masks[0])]
+        elif task == "whole":
+            self.parts = [outs[0], swap(outs[0], "seq", self.masks[0])]
+        else:
+            total = outs[0]
+            for mask in self.masks[1:]:
+                total = (total.astype(FULL) + swap(total, "seq", mask).astype(FULL)).astype(LOW)
+            self.parts = [total]
+            if self.halves:
+                self.parts.append(swap(total, "seq", self.masks[0]))
+
+
+def gather(part):
+    return [part] + [swap(part, "seq", mask) for mask in range(1, QUAD)]
+
+
+def join_sum(left, own, received, deps):
+    rows, columns = left.shape
+
+    def kernel(left, own, received, *refs):
+        out = refs[-1]
+        out[:, :columns] = left[...]
+        out[:, columns:] = (own[...].astype(FULL) + received[...].astype(FULL)).astype(LOW)
+
+    here, anywhere = pl.BlockSpec(memory_space=pltpu.VMEM), pl.BlockSpec(memory_space=pl.ANY)
     return pl.pallas_call(
         kernel,
-        grid_spec=pltpu.PrefetchScalarGridSpec(
-            num_scalar_prefetch=1,
-            grid=(count,),
-            in_specs=[
-                pl.BlockSpec(block, lambda e, n, i=i: (n[i + 1] + (n[0] ^ e), 0)) for i in range(len(parts))
-            ],
-            out_specs=[pl.BlockSpec(block, lambda e, n: (0, 0))] * count,
-        ),
-        out_shape=[jax.ShapeDtypeStruct(block, LOW)] * count,
+        in_specs=[here] * 3 + [anywhere] * len(deps),
+        out_specs=here,
+        out_shape=jax.ShapeDtypeStruct((rows, columns + own.shape[1]), LOW),
         compiler_params=pltpu.CompilerParams(vmem_limit_bytes=VMEM),
         cost_estimate=cost(2),
-        name="split_sum",
-    )(scalars, *[part for part, _ in parts])
-
-
-def join(parts):
-    rows, columns = parts[0].shape
-    count = len(parts)
-
-    def kernel(*refs):
-        for e, ref in enumerate(refs[:-1]):
-
-            @pl.when(pl.program_id(0) == e)
-            def _(ref=ref):
-                refs[-1][...] = ref[...]
-
-    return pl.pallas_call(
-        kernel,
-        grid=(count,),
-        in_specs=[pl.BlockSpec((rows, columns), lambda e: (0, 0))] * count,
-        out_specs=pl.BlockSpec((rows, columns), lambda e: (e, 0)),
-        out_shape=jax.ShapeDtypeStruct((count * rows, columns), LOW),
-        compiler_params=pltpu.CompilerParams(vmem_limit_bytes=VMEM),
-        cost_estimate=cost(2),
-        name="join",
-    )(*parts)
-
-
-def sum_small(wide, narrow):
-    seqs = lax.axis_size("seq")
-    lanes = wide.shape[1]
-    share = wide.shape[0] // seqs
-    short = -(-narrow.shape[0] // (seqs * lanes))
-    fill = -(-(share + 2 * short) // 16) * 16 - share - 2 * short
-
-    def packed(wide, narrow):
-        lead = wide.shape[:-2]
-        high = lax.optimization_barrier(narrow.astype(LOW))
-        low = (narrow - high.astype(FULL)).astype(LOW)
-        return jnp.concatenate(
-            [wide.astype(LOW), high, low, jnp.zeros((*lead, fill, lanes), LOW)], axis=-2
-        )
-
-    padded = jnp.pad(narrow, (0, seqs * short * lanes - narrow.shape[0])).reshape(seqs, short, lanes)
-    parts = exchange_all(packed(wide.reshape(seqs, share, lanes), padded)).astype(FULL)
-    total = jnp.sum(parts, axis=0)
-    total = packed(total[:share], total[share : share + short] + total[share + short : share + 2 * short])
-    parts = exchange_all(jnp.broadcast_to(total[None], (seqs, *total.shape))).astype(FULL)
-    result = parts[:, share : share + short] + parts[:, share + short : share + 2 * short]
-    return parts[:, :share].reshape(wide.shape), result.reshape(-1)[: narrow.shape[0]]
-
-
-class Chain:
-    def __init__(self, x, stages):
-        me = lax.axis_index("seq")
-        self.start = x
-        self.masks, self.places = [], []
-        for bits in stages:
-            place = 0
-            for bit in bits:
-                place = 2 * place + ((me >> bit) & 1)
-            self.places.append(place)
-            self.masks.append(
-                [
-                    sum(1 << bit for i, bit in enumerate(reversed(bits)) if e >> i & 1)
-                    for e in range(1 << len(bits))
-                ]
-            )
-        self.level = 0
-        size = x.shape[0] // 2
-        sent = lax.dynamic_slice_in_dim(x, (1 - self.places[0]) * size, size, 0)
-        self.parts = [x, swap(sent, "seq", self.masks[0][1])]
-
-    def steps_left(self):
-        return 2 * len(self.masks) - 1 - self.level
-
-    def step(self, *deps):
-        if self.steps_left() <= 0:
-            return []
-        count = len(self.masks)
-        self.parts = list(after(tuple(self.parts), deps))
-        self.level += 1
-        if self.level < count:
-            masks = self.masks[self.level]
-            firsts = [0 * self.places[0]] * len(self.parts)
-            if self.level == 1:
-                firsts[0] = self.places[0] * len(masks)
-            pieces = list(split_sum(list(zip(self.parts, firsts)), self.places[self.level], len(masks)))
-            self.parts = pieces[:1] + [swap(p, "seq", mask) for p, mask in zip(pieces[1:], masks[1:])]
-            return pieces
-        if self.level == count:
-            x = sum(part.astype(FULL) for part in self.parts).astype(LOW)
+        name="join_sum",
+    )(left, own, received, *deps)
+
+
+def advance(chains, *deps):
+    tasks = [chain.tasks.pop(0) for chain in chains]
+    parts = [chain.parts for chain in chains]
+    shapes = []
+    for task, part in zip(tasks, parts):
+        rows, columns = part[0].shape[-2:]
+        made = {"deal": [rows // 2 * len(part)] * 2, "whole": [rows * len(part)], "sum": [rows]}[task]
+        shapes.append([jax.ShapeDtypeStruct((size, columns), LOW) for size in made])
+    counts = [len(part) for part in parts]
+    me = lax.axis_index("seq")
+    high = (me // QUAD % 2).astype(jnp.int32)[None]
+
+    def kernel(high, *refs):
+        ins = list(refs[: sum(counts)])
+        outs = list(refs[len(refs) - sum(len(shape) for shape in shapes) :])
+        for task, count in zip(tasks, counts):
+            refs = [ins.pop(0) for _ in range(count)]
+            if task == "deal":
+                half = refs[0].shape[1] // 2
+                for block in (high[0], 1 - high[0]):
+                    place = pl.ds(pl.multiple_of(block * half, half), half)
+                    out = outs.pop(0)
+                    for i, ref in enumerate(refs):
+                        out[i * half : (i + 1) * half, :] = sum(
+                            ref[k, place, :].astype(FULL) for k in range(QUAD)
+                        ).astype(LOW)
+            elif task == "whole":
+                out = outs.pop(0)
+                rows = refs[0].shape[1]
+                for i, ref in enumerate(refs):
+                    out[i * rows : (i + 1) * rows, :] = sum(ref[k].astype(FULL) for k in range(QUAD)).astype(LOW)
+            else:
+                outs.pop(0)[...] = (refs[0][...].astype(FULL) + refs[1][...].astype(FULL)).astype(LOW)
+
+    here, anywhere = pl.BlockSpec(memory_space=pltpu.VMEM), pl.BlockSpec(memory_space=pl.ANY)
+    results = list(
+        pl.pallas_call(
+            kernel,
+            in_specs=[pl.BlockSpec(memory_space=pltpu.SMEM)] + [here] * sum(counts) + [anywhere] * len(deps),
+            out_specs=[here] * sum(len(shape) for shape in shapes),
+            out_shape=[one for shape in shapes for one in shape],
+            compiler_params=pltpu.CompilerParams(vmem_limit_bytes=VMEM),
+            cost_estimate=cost(2),
+            name="advance",
+        )(high, *[array for part in parts for array in part], *deps)
+    )
+    rest = list(results)
+    for task, chain, shape in zip(tasks, chains, shapes):
+        chain.accept(task, [rest.pop(0) for _ in shape])
+    return results
+
+
+def finish(groups, slot, slots, columns, first, row_turn, half_turn, column_turn, outputs=1):
+    rows = groups[0][0].shape[0] // slots
+    width = columns // 4
+    skip = first // (2 * width)
+    me = lax.axis_index("seq")
+    high = me // QUAD % 2
+    scalars = jnp.stack([(me & (QUAD - 1)) ^ row_turn, half_turn, column_turn, high]).astype(jnp.int32)
+    count = len(groups)
+
+    def kernel(scalars, *refs):
+        ins, outs = refs[: count * QUAD], refs[-outputs:]
+
+        def put(out):
+            for k in range(count):
+                for q in range(QUAD):
+                    block = (scalars[0] ^ q) * count
+                    if count == 2:
+                        block = block + (scalars[3] ^ k)
+                    target = pl.ds(pl.multiple_of(block * rows, rows), rows)
+                    ref = ins[k * QUAD + q]
+                    for e in range(2):
+                        place = pl.ds(pl.multiple_of((e ^ scalars[2]) * width, width), width)
+                        out[target, place] = ref[:, e * width : (e + 1) * width].astype(FULL)
+
+        if outputs == 1:
+            put(outs[0])
         else:
-            x = join(self.parts)
-        masks = self.masks[2 * count - 1 - self.level]
-        self.parts = [x] + [swap(x, "seq", mask) for mask in masks[1:]]
-        return [x]
-
-    def place(self):
-        total = 0
-        for place, masks in zip(self.places, self.masks):
-            total = len(masks) * total + place
-        return total
-
-
-def chain_stages(first, bits):
-    rest = [bit for bit in range(bits) if bit != first]
-    return [[first]] + [rest[i : i + 2] for i in range(0, len(rest), 2)]
-
-
-def finish(chain, row_turn, half_turn, column_turn):
-    assert chain.steps_left() <= 0
-    rows, columns = chain.parts[0].shape
-    width = columns // 4
-    scalars = jnp.stack([chain.place() ^ row_turn, half_turn, column_turn]).astype(jnp.int32)
-    count = 1 << (lax.axis_size("seq") - 1).bit_length()
-    spec = pl.BlockSpec((rows, 2 * width), lambda half, n: (0, half))
-
-    def kernel(scalars, own, received, out):
-        size = out.shape[0] // count
-        for q in range(count):
-            ref, first = (own, q * size) if q < count // 2 else (received, (q - count // 2) * size)
-            target = pl.ds(pl.multiple_of((scalars[0] ^ q) * size, size), size)
-            for e in range(2):
-                place = pl.ds(pl.multiple_of((e ^ scalars[2]) * width, width), width)
-                out[target, place] = ref[first : first + size, e * width : (e + 1) * width].astype(FULL)
+            for k in range(2):
+                pl.when(pl.program_id(0) == k)(lambda k=k: put(outs[k]))
 
     return pl.pallas_call(
         kernel,
         grid_spec=pltpu.PrefetchScalarGridSpec(
             num_scalar_prefetch=1,
             grid=(2,),
-            in_specs=[spec] * 2,
-            out_specs=pl.BlockSpec((2 * rows, 2 * width), lambda half, n: (0, half ^ n[1])),
+            in_specs=[pl.BlockSpec((rows, 2 * width), lambda half, n: (slot, half + skip))] * (count * QUAD),
+            out_specs=[
+                pl.BlockSpec(
+                    (count * QUAD * rows, 2 * width),
+                    (lambda half, n: (0, half ^ n[1])) if outputs == 1 else (lambda half, n: (0, 0)),
+                )
+            ]
+            * outputs,
         ),
-        out_shape=jax.ShapeDtypeStruct((2 * rows, columns), FULL),
+        out_shape=[jax.ShapeDtypeStruct((count * QUAD * rows, columns // outputs), FULL)] * outputs,
         compiler_params=pltpu.CompilerParams(vmem_limit_bytes=VMEM),
         cost_estimate=cost(3),
         name="finish",
-    )(scalars, *chain.parts)
+    )(scalars, *[part for group in groups for part in group])
 
 
 def cost(us):
@@ -536,9 +587,8 @@
     )(signal, skip, consts, z, m, init)
 
 
-def backward_kernel(
-    grads, consts, z, m, init, out, g_out, u_out, v_out, h_out, g_scr, y_scr
-):
+def backward_kernel(grads, consts, z, m, init, *refs):
+    out, g_out, u_out, v_out, h_out, g_scr, y_scr = refs[-7:]
     step = pl.program_id(0)
     channels, _, lanes = z.shape
     count = grads.shape[0] // lanes
@@ -582,7 +632,7 @@
             )
 
 
-def s4_backward(grads, consts, z, m, init):
+def s4_backward(grads, consts, z, m, init, deps=()):
     tokens, width = grads.shape
     lanes = z.shape[-1]
     count = tokens // lanes
@@ -598,18 +648,19 @@
             pl.BlockSpec((CHANNELS, 2 * lanes, lanes), lambda i: (i, 0, 0)),
             pl.BlockSpec((CHANNELS, lanes, lanes), lambda i: (i, 0, 0)),
             pl.BlockSpec((CHANNELS, lanes), lambda i: (i, 0)),
-        ],
+        ]
+        + [pl.BlockSpec(memory_space=pl.ANY)] * len(deps),
         out_specs=[whole] + [by_channel] * 4,
         out_shape=[jax.ShapeDtypeStruct((tokens, width), FULL)] + [per_channel] * 4,
         scratch_shapes=[pltpu.VMEM((width * count, lanes), FULL)] * 2,
         compiler_params=pltpu.CompilerParams(vmem_limit_bytes=VMEM),
         cost_estimate=cost(18),
         name="s4_backward",
-    )(grads, consts, z, m, init)
-
-
-def sums_kernel(block, x, g, p, q, s, u, v, h, z, consts, dep, out):
-    del dep
+    )(grads, consts, z, m, init, *deps)
+
+
+def sums_kernel(block, x, g, p, q, s, u, v, h, z, consts, *refs):
+    out = refs[-1]
     channels, count, lanes = x.shape
     states = lanes // 2
     row8 = lax.broadcasted_iota(jnp.int32, (8, lanes), 0)
@@ -690,10 +741,8 @@
     out[3] = jnp.broadcast_to(jnp.sum(grad_step, axis=1, keepdims=True), (channels, lanes))
 
 
-def s4_sums(x, g, p, q, s, u, v, h, z, consts, block, dep, part, parts):
+def s4_sums(x, g, p, q, s, u, v, h, z, consts, block, deps, skip, steps):
     width, count, lanes = x.shape
-    steps = width // CHANNELS // parts
-    skip = part * steps
     by_channel = pl.BlockSpec((CHANNELS, count, lanes), lambda i: (i + skip, 0, 0))
     return pl.pallas_call(
         lambda *refs: sums_kernel(block, *refs),
@@ -702,14 +751,14 @@
         + [
             pl.BlockSpec((CHANNELS, 2 * lanes, lanes), lambda i: (i + skip, 0, 0)),
             pl.BlockSpec((ROWS, CHANNELS, lanes), lambda i: (0, i + skip, 0)),
-            pl.BlockSpec(memory_space=pl.ANY),
-        ],
+        ]
+        + [pl.BlockSpec(memory_space=pl.ANY)] * len(deps),
         out_specs=pl.BlockSpec((4, CHANNELS, lanes), lambda i: (0, i, 0)),
-        out_shape=jax.ShapeDtypeStruct((4, width // parts, lanes), FULL),
+        out_shape=jax.ShapeDtypeStruct((4, steps * CHANNELS, lanes), FULL),
         compiler_params=pltpu.CompilerParams(vmem_limit_bytes=VMEM),
-        cost_estimate=cost(18 / parts),
+        cost_estimate=cost(18 * steps * CHANNELS / width),
         name="s4_sums",
-    )(x, g, p, q, s, u, v, h, z, consts, dep)
+    )(x, g, p, q, s, u, v, h, z, consts, *deps)
 
 
 def split(rows):
@@ -784,16 +833,14 @@
             lax.dynamic_slice_in_dim(w, (chan_me ^ d) * width, width, 0) for d in range(chans)
         ]
 
-    inputs_low = exchange(block_input).reshape(batch * block, width)
+    moved = exchange(jnp.concatenate([block_input, out_grad], axis=-1)).reshape(batch * block, 2 * width)
 
     consts, base = s4_consts(a_decay, a_freq, b_state, c_state, step_size, block)
-    tables = s4_tables(base, consts, 0, 2)
-    inputs_low = after(inputs_low, tables[0])
-    inputs = inputs_low.astype(FULL)
-    moments = jnp.stack([jnp.sum(inputs, axis=-1), jnp.sum(inputs * inputs, axis=-1)])
-    grad_low = exchange(after(out_grad, moments)).reshape(batch * block, width)
-    z, m = s4_tables(base, consts, 1, 2, tables, (moments,))
-    moments = after(sum_chan(moments), m)
+    z, m = s4_tables(base, consts, 0, 1)
+    moved = after(moved, z)
+    inputs = moved[:, :width].astype(FULL)
+    grad_low = moved[:, width:]
+    moments = sum_chan(jnp.stack([jnp.sum(inputs, axis=-1), jnp.sum(inputs * inputs, axis=-1)]))
     states = a_decay.shape[0]
 
     def const_factor(k):
@@ -837,38 +884,38 @@
     hidden = sum(dot(a, w) for a, w in zip(norms, w_ups)) + b_up
     spread, gelu_pull = jax.vjp(jax.nn.gelu, hidden)
     spread = spread.astype(LOW)
-    downs = [dot(spread, w) for w in w_downs]
-    output = (resid + reduce_pieces(downs) + b_down).astype(LOW)
-    output = exchange(output.reshape(batch, block, width))
 
     grad_out = grad_low.astype(FULL)
     grad_spread = sum(dot_t(a, w) for a, w in zip(grads, w_downs))
     grad_hidden = gelu_pull(grad_spread)[0].astype(LOW)
+    grad_w_down = t_dot(after(spread, grad_hidden), jnp.concatenate(grads, axis=1)).astype(LOW)
+    downs_dealt = deal(grad_w_down)
     marks = []
-    grad_norm_two = reduce_pieces([dot_t(grad_hidden, w) for w in w_ups], marks)
-    bits = axis_bits("seq")
-    orders = chain_stages(0, bits), chain_stages(1, bits)
-    spread_late, hidden_late = after(spread, marks[0]), after(grad_hidden, marks[0])
-    downs = [Chain(t_dot(spread_late, jnp.concatenate(grads, axis=1)).astype(LOW), orders[0])]
-    ups = [Chain(t_dot(jnp.concatenate(norms, axis=1), hidden_late).astype(LOW), orders[1])]
-    grad_norm_two = after(grad_norm_two, *[chain.start for chain in downs + ups])
-
-    def steps(chains, *deps):
-        return [made for chain in chains for made in chain.step(*deps)]
+    hidden_late = after(grad_hidden, grad_w_down)
+    grad_norm_two = reduce_pieces([dot_t(hidden_late, w) for w in w_ups], marks)
+    grad_w_up = t_dot(jnp.concatenate(norms, axis=1), after(grad_hidden, *marks[:2])).astype(LOW)
+    grad_norm_two = after(grad_norm_two, grad_w_up)
+    chains = []
+
+    def start_ups(dep):
+        chains.append(Chain([downs_dealt, deal(after(grad_w_up, dep))], True))
+        return []
 
     grad_resid, grad_norm2_gain, grad_norm2_bias = layer_backward(
-        grad_norm_two, normed_two, inverse_two, norm2_gain, total_width, lambda dep: []
+        grad_norm_two, normed_two, inverse_two, norm2_gain, total_width, start_ups
     )
+    wide_chain = chains[0]
     grad_resid = grad_out + grad_resid
     grad_value = (grad_resid * opened).astype(LOW)
     grad_gate = (grad_resid * value * opened * (1.0 - opened)).astype(LOW)
     grad_both = jnp.concatenate([grad_value, grad_gate], axis=1)
+    marks = []
     grad_activ = reduce_pieces([dot_t(grad_both, w) for w in w_gated], marks)
-    gateds = [
-        Chain(t_dot(jnp.concatenate(activs, axis=1), after(grad_both, marks[1])).astype(LOW), orders[0])
-    ]
-    grad_activ = after(grad_activ, gateds[0].start, *steps(downs, marks[1]))
+    grad_w_gated = t_dot(jnp.concatenate(activs, axis=1), after(grad_both, *marks[:2])).astype(LOW)
+    gated_chain = Chain([deal(after(grad_w_gated, grad_activ))], False)
+    grad_activ = after(grad_activ, grad_w_gated)
     grad_mixed = (grad_activ * slope).astype(LOW)
+    made = advance([wide_chain], grad_mixed)
     init = jnp.zeros((width, 2 * states), FULL)
     if runs > 1:
         _, _, u, _, h = s4_backward(grad_mixed, consts, z, m, init)
@@ -877,31 +924,20 @@
         for r in reversed(range(1, runs)):
             moved = add(cmul(hop, split(init)), split(ends[r]))
             init = jnp.where(r > seq_me // batch, pair(*moved), init)
-    grad_signal, gs, us, vs, hs = s4_backward(grad_mixed, consts, z, m, init)
+    grad_signal, gs, us, vs, hs = s4_backward(grad_mixed, consts, z, m, init, made)
+    grad_signal = after(grad_signal, *advance([wide_chain, gated_chain], grad_signal))
     grad_signal = grad_signal + skip * grad_mixed.astype(FULL)
     s4_parts = (xs, gs, ps, qs, ss, us, vs, hs, z, consts, block)
-    sums = []
-
-    def sums_part(*deps):
-        sums.append(s4_sums(*s4_parts, after(hs, *deps), len(sums), 4))
-        return sums[-1]
-
     grad_input, grad_norm1_gain, grad_norm1_bias = layer_backward(
-        grad_signal * mask,
-        normed_one,
-        inverse_one,
-        norm1_gain,
-        total_width,
-        lambda dep: [sums_part(dep)],
+        grad_signal * mask, normed_one, inverse_one, norm1_gain, total_width, lambda dep: []
     )
-    grad_input_low = (grad_resid + grad_input).astype(LOW)
-    grad_input = exchange(grad_input_low.reshape(batch, block, width))
-    part = sums_part(grad_input_low, output, *steps(downs, sums[0]))
-    part = sums_part(*steps(ups + gateds, part))
-    part = sums_part(*steps(downs + gateds, part))
-    work = steps(ups + gateds, part)
-    grad_input = after(grad_input, part).astype(FULL)
-    sums = jnp.concatenate(sums, axis=1)
+    grad_input = (grad_resid + grad_input).astype(LOW)
+    wide_own = gather(wide_chain.parts[0])
+    sums = s4_sums(*s4_parts, [grad_input], 0, width // CHANNELS)
+    grad_input_moved = exchange(grad_input.reshape(batch, block, width))
+    made = join_sum(wide_chain.parts[1], *gated_chain.parts, [sums, *wide_own[1:]])
+    last = gather(made)
+    grad_input = grad_input_moved.astype(FULL)
     narrow = jnp.concatenate(
         [
             grad_norm1_gain,
@@ -916,18 +952,18 @@
             jnp.sum(grad_hidden.astype(FULL), axis=0),
         ]
     )
-    wide, narrow = sum_small(sums[:3].reshape(3 * width, 2 * states), narrow)
-    wide = wide.reshape(3, width, 2 * states).transpose(0, 2, 1)
-    chains = downs + ups + gateds
-    while any(chain.steps_left() > 0 for chain in chains):
-        work = steps(chains, *work)
+    wide, narrow, packed = sum_small(sums, narrow, [made, grad_input_moved], last[1:])
+    wide = wide.transpose(0, 2, 1)
+    spread_late = after(spread, made)
+    output = reduce_pieces([dot(spread_late, w) for w in w_downs])
+    output = exchange((resid + output + b_down).astype(LOW).reshape(batch, block, width))
     vectors = [narrow[k * width : (k + 1) * width] for k in range(9)]
     vectors.insert(2, vectors.pop(8))
 
     zero = 0 * chan_me
-    down = finish(downs[0], zero, chan_me >> 1, chan_me & 1)
-    up = finish(ups[0], chan_me * (seqs // chans), zero, zero)
-    gated = finish(gateds[0], chan_me * (seqs // chans), zero, zero)
+    (down,) = finish([wide_own, last], 0, 2, total_width, 0, zero, chan_me >> 1, chan_me & 1)
+    (up,) = finish([wide_own, last], 1, 2, grad_w_up.shape[1], 0, chan_me, zero, zero)
+    grad_w_value, grad_w_gate = finish([last], 0, 1, 2 * width, total_width, chan_me, zero, zero, 2)
     return (
         output,
         grad_input,
@@ -939,9 +975,9 @@
         wide[2].reshape(2, states, width),
         vectors[2],
         vectors[3],
-        gated[:, :width],
+        grad_w_value,
         vectors[4],
-        gated[:, width:],
+        grad_w_gate,
         vectors[5],
         vectors[6],
         vectors[7],

time: 402 us -> 372 us (0.925)
  Pallas kernels: 130 us -> 111 us
  starting transfers between devices: 83.7 us -> 68.9 us
  waiting for transfers between devices: 94.5 us -> 105 us
  other arithmetic: 25.9 us -> 16.5 us
  matrix products: 38.5 us -> 46.7 us
  local copies, waits for them, and re-layouts: 22.8 us -> 15 us
    ppermute x54 -> x39, starting transfers between devices: 56.1 us -> 30.9 us  [swap(): lax.ppermute(x, axis, [(i, i ^ distance) for i in range(lax.axis_size(axi...]
    all_to_all x0 -> x3, starting transfers between devices: none -> 13.5 us  [deal(): lax.all_to_all(x.reshape(QUAD, -1, x.shape[1]), 'seq', 0, 0, axis_index_g...]
    all_to_all x4 -> x3, waiting for transfers between devices: 13.2 us -> 3.26 us  [exchange(): return lax.all_to_all(x, 'seq', 0, 0, axis_index_groups=groups, tiled=True)]
    pallas_call x6 -> x5, Pallas kernels: 20.3 us -> 11.8 us  [the longest x2 6.22 us: advance(): pl.pallas_call(kernel, in_specs=[pl.BlockSpec(memory_space=pltpu.SMEM)] +...]
    pallas_call x4 -> x1, Pallas kernels: 33.7 us -> 25.4 us  [s4_sums(): pl.pallas_call(lambda *refs: sums_kernel(block, *refs), grid=(steps,), in...]
    dot_general x12, matrix products: 10 us -> 18.3 us  [dot(): lax.dot_general(a, b, (((1,), (0,)), ((), ())), preferred_element_type=FULL)]
    ppermute x54 -> x39, waiting for transfers between devices: 81.2 us -> 89 us  [swap(): lax.ppermute(x, axis, [(i, i ^ distance) for i in range(lax.axis_size(axi...]
    all_to_all x2, waiting for transfers between devices: 0.01 us -> 6.95 us  [exchange_all(): return lax.all_to_all(x, 'seq', 0, 0, tiled=True)]
  transfers between devices with their start and end apart: 60 -> 47, of which waited for: 17 -> 23; matrix products, arithmetic and copies ran while one was open for 17% -> 16% of each run, Pallas kernels for 29% -> 29%
where the time goes in v2:
time: 372 us; the launch traced here: 365 us
  Pallas kernels  111 us (30%)
  waiting for transfers between devices  105 us (28%)
  starting transfers between devices  68.9 us (19%)
  matrix products  46.7 us (13%)
  other arithmetic  16.5 us (4%)
  local copies, waits for them, and re-layouts  15 us (4%)
    ppermute x39, waiting for transfers between devices, swap(): lax.ppermute(x, axis, [(i, i ^ distance) for i in range(lax.axis_size(axi...  89 us
    ppermute x39, starting transfers between devices, swap(): lax.ppermute(x, axis, [(i, i ^ distance) for i in range(lax.axis_size(axi...  30.9 us
    pallas_call x1, Pallas kernels, s4_sums(): pl.pallas_call(lambda *refs: sums_kernel(block, *refs), grid=(steps,), in...  25.4 us
    pallas_call x1, Pallas kernels, s4_tables(): pl.pallas_call(tables_kernel, grid=(steps,), in_specs=[pl.BlockSpec((8, C...  20 us
    pallas_call x1, Pallas kernels, s4_forward(): pl.pallas_call(forward_kernel, grid=(width // CHANNELS,), in_specs=[whole...  18.8 us
    dot_general x12, matrix products, dot(): lax.dot_general(a, b, (((1,), (0,)), ((), ())), preferred_element_type=FULL)  18.3 us
    pallas_call x1, Pallas kernels, s4_backward(): pl.pallas_call(backward_kernel, grid=(width // CHANNELS,), in_specs=[whol...  17.6 us
    all_to_all x3, starting transfers between devices, exchange(): return lax.all_to_all(x, 'seq', 0, 0, axis_index_groups=groups, tiled=True)  17.3 us
  transfers between devices with their start and end apart: 47, of which 23 were waited for; matrix products, arithmetic and copies ran while one was open for 16% of the time, Pallas kernels for 29%

profile of v2, /device:TPU:0, one launch (start us, length us, event | category | flops | bytes accessed | tf_op | source)
XLA Modules:
  0.0 364.9 jit_solution(6542317327409232862)
XLA Ops:
  0.7 2.4 pad_maximum_fusion
  3.1 7.3 %all-to-all-start = ((bf16[8,128,512]{2,1,0:T(8,128)(2,1)}), bf16[8,128,512]{2,1,0:T(8,128)(2,1)S(1)}, u32[]{:S(2)}, u32[]{:S(2)}) async-start(bf16[8,128,512]{2,1,0:T(8,128)(2,1)} %pad_maximum_fusion), calls=%async_computation | async-start | bytes 2097152 | tf_op jit(solution)/shard_map/all_to_all | solution.py:829
  10.3 5.1 %s4_consts.1 = (f32[30,256,128]{2,1,0:T(8,128)}, f32[8,256,128]{2,1,0:T(8,128)}) custom-call(f32[64,256]{1,0:T(8,128)} %refs_0_.1, f32[64,256]{1,0:T(8,128)} %refs_1_.1, f32[2,64,256]{2,1,0:T(8,128)} %refs_2_.1, f32[2,64,256]{2,1,0:T(8,128)} %refs_3_.1, f32[1,256]{1,0:T(1,128)} %bitcast.114), custom_call_target="tpu_custom_call" | custom-call | bytes 600000 | tf_op jit(solution)/shard_map/s4_consts/pallas_call | solution.py:383
  15.5 20.0 %s4_tables.1 = (bf16[256,256,128]{2,1,0:T(8,128)(2,1)}, bf16[256,128,128]{2,1,0:T(8,128)(2,1)}) custom-call(f32[8,256,128]{2,1,0:T(8,128)} %get-tuple-element.53.base, f32[30,256,128]{2,1,0:T(8,128)} %get-tuple-element.54.consts.refs_9_), custom_call_target="tpu_custom_call" | custom-call | bytes 2400000 | tf_op jit(solution)/shard_map/s4_tables/pallas_call | solution.py:451
  36.1 2.2 constant_dynamic-slice_fusion
  46.1 18.8 %s4_forward.1 = (bf16[1024,256]{1,0:T(8,128)(2,1)}, f32[1024,256]{1,0:T(8,128)}, f32[256,8,128]{2,1,0:T(8,128)}, f32[256,8,128]{2,1,0:T(8,128)}, f32[256,8,128]{2,1,0:T(8,128)}, /*index=5*/f32[256,8,128]{2,1,0:T(8,128)}) custom-call(bf16[1024,256]{1,0:T(8,128)(2,1)} %fusion.56.signal, f32[1,256]{1,0:T(1,128)} %bitcast.113, ...), custom_call_target="tpu_custom_call" | custom-call | bytes 1800000 | tf_op jit(solution)/shard_map/s4_forward/pallas_call | solution.py:566
  67.3 11.4 %collective-permute-done.5 = bf16[1024,256]{1,0:T(8,128)(2,1)S(1)} collective-permute-done((bf16[1024,256]{1,0:T(8,128)(2,1)}, bf16[1024,256]{1,0:T(8,128)(2,1)S(1)}, u32[]{:S(2)}, u32[]{:S(2)}) %collective-permute-start.5) | collective-permute-done | bytes 524320 | tf_op jit(solution)/shard_map/ppermute | solution.py:18
  90.0 10.3 %collective-permute-done.11 = bf16[1024,256]{1,0:T(8,128)(2,1)S(1)} collective-permute-done((bf16[1024,256]{1,0:T(8,128)(2,1)S(1)}, bf16[1024,256]{1,0:T(8,128)(2,1)S(1)}, u32[]{:S(2)}, u32[]{:S(2)}) %collective-permute-start.11) | collective-permute-done | bytes 524320 | tf_op jit(solution)/shard_map/ppermute | solution.py:18
  102.3 3.2 multiply_convert_fusion
  105.6 6.6 %convert_reduce_fusion = (f32[1024]{0:T(1024)S(1)}, bf16[1024,1024]{1,0:T(8,128)(2,1)}) fusion(f32[1024,1024]{1,0:T(8,128)S(1)} %get-tuple-element.138, bf16[1024,256]{1,0:T(8,128)(2,1)} %collective-permute-done.14, bf16[1024,1024]{1,0:T(8,128)(2,1)S(1)} %copy-done.29, s32[]{:T(128)S(6)} %select_n.63, f32[1024,1024]{1,0:T(8,128)S(1)} %fusion.71, ...), kind=kOutput, calls=%fused_computation.9 | convolution fusion | flops 563084288 | bytes 19927044 | tf_op jit(solution)/shard_map/dot_general | solution.py:409
  112.2 5.0 %fusion.34 = bf16[1024,1024]{1,0:T(8,128)(2,1)} fusion(bf16[1024,1024]{1,0:T(8,128)(2,1)S(1)} %get-tuple-element.83, bf16[1024,256]{1,0:T(8,128)(2,1)} %collective-permute-done.14, bf16[1024,256]{1,0:T(8,128)(2,1)} %collective-permute-done.3, bf16[1024,256]{1,0:T(8,128)(2,1)S(1)} %copy-done.58, bf16[1024,256]{1,0:T(8,128)(2,1)S(1)} %copy-done.49), kind=kOutput, calls=%fused_computation.38 | convolution fusion | flops 2156920832 | bytes 6291456 | tf_op jit(solution)/shard_map/dot_general | solution.py:770
  117.2 4.4 %all-to-all-start.1 = ((bf16[4,256,1024]{2,1,0:T(8,128)(2,1)}), bf16[4,256,1024]{2,1,0:T(8,128)(2,1)}, u32[]{:S(2)}, u32[]{:S(2)}) async-start(bf16[4,256,1024]{2,1,0:T(8,128)(2,1)} %bitcast.72), calls=%async_computation.1 | async-start | bytes 4194304 | tf_op jit(solution)/shard_map/all_to_all | solution.py:130
  121.6 2.5 convolution_convert_fusion.5
  128.7 4.7 %fusion.31 = bf16[1024,1024]{1,0:T(8,128)(2,1)} fusion(bf16[1024,1024]{1,0:T(8,128)(2,1)S(1)} %copy-done.70, bf16[1024,256]{1,0:T(8,128)(2,1)} %collective-permute-done.12, bf16[1024,256]{1,0:T(8,128)(2,1)S(1)} %copy-done.26, bf16[1024,256]{1,0:T(8,128)(2,1)S(1)} %copy-done.28, bf16[1024,256]{1,0:T(8,128)(2,1)S(1)} %copy-done.20), kind=kOutput, calls=%fused_computation.37 | convolution fusion | flops 2156920832 | bytes 6291456 | tf_op jit(solution)/shard_map/dot_general | solution.py:770
  133.4 7.5 %collective-permute-done.17 = bf16[1024,256]{1,0:T(8,128)(2,1)S(1)} collective-permute-done((bf16[1024,256]{1,0:T(8,128)(2,1)S(1)}, bf16[1024,256]{1,0:T(8,128)(2,1)S(1)}, u32[]{:S(2)}, u32[]{:S(2)}) %collective-permute-start.17) | collective-permute-done | bytes 524320 | tf_op jit(solution)/shard_map/ppermute | solution.py:18
  141.7 5.7 %all-to-all-done.1.refs_0_ = bf16[4,256,1024]{2,1,0:T(8,128)(2,1)} async-done(((bf16[4,256,1024]{2,1,0:T(8,128)(2,1)}), bf16[4,256,1024]{2,1,0:T(8,128)(2,1)}, u32[]{:S(2)}, u32[]{:S(2)}) %all-to-all-start.1) | async-done | bytes 2097184 | tf_op jit(solution)/shard_map/all_to_all | solution.py:130
  147.4 4.6 %all-to-all-start.2 = ((bf16[4,256,1024]{2,1,0:T(8,128)(2,1)}), bf16[4,256,1024]{2,1,0:T(8,128)(2,1)}, u32[]{:S(2)}, u32[]{:S(2)}) async-start(bf16[4,256,1024]{2,1,0:T(8,128)(2,1)} %bitcast.71), calls=%async_computation.2 | async-start | bytes 4194304 | tf_op jit(solution)/shard_map/all_to_all | solution.py:130
  156.9 2.2 convert_reduce_fusion.3
  164.3 2.3 fusion.37
  166.6 10.5 %collective-permute-done.23 = bf16[1024,256]{1,0:T(8,128)(2,1)S(1)} collective-permute-done((bf16[1024,256]{1,0:T(8,128)(2,1)S(1)}, bf16[1024,256]{1,0:T(8,128)(2,1)S(1)}, u32[]{:S(2)}, u32[]{:S(2)}) %collective-permute-start.23) | collective-permute-done | bytes 524320 | tf_op jit(solution)/shard_map/ppermute | solution.py:18
  177.3 4.5 %all-to-all-start.3 = ((bf16[4,256,512]{2,1,0:T(8,128)(2,1)}), bf16[4,256,512]{2,1,0:T(8,128)(2,1)}, u32[]{:S(2)}, u32[]{:S(2)}) async-start(bf16[4,256,512]{2,1,0:T(8,128)(2,1)} %bitcast.76), calls=%async_computation.3 | async-start | bytes 2097152 | tf_op jit(solution)/shard_map/all_to_all | solution.py:130
  181.8 2.4 fusion.47
  184.2 3.6 advance.2
  187.9 2.6 collective-permute-start.24
  190.5 17.6 %s4_backward.1 = (f32[1024,256]{1,0:T(8,128)}, f32[256,8,128]{2,1,0:T(8,128)}, f32[256,8,128]{2,1,0:T(8,128)}, f32[256,8,128]{2,1,0:T(8,128)}, f32[256,8,128]{2,1,0:T(8,128)}) custom-call(bf16[1024,256]{1,0:T(8,128)(2,1)} %get-tuple-element.105.refs_2_.grads, f32[30,256,128]{2,1,0:T(8,128)} %get-tuple-element.54.consts.refs_9_, ...), custom_call_target="tpu_custom_call" | custom-call | bytes 1800000 | tf_op jit(solution)/shard_map/s4_backward/pallas_call | solution.py:642
  208.1 5.4 %collective-permute-done.24.refs_1_ = bf16[256,1024]{1,0:T(8,128)(2,1)S(1)} collective-permute-done((bf16[256,1024]{1,0:T(8,128)(2,1)}, bf16[256,1024]{1,0:T(8,128)(2,1)S(1)}, u32[]{:S(2)}, u32[]{:S(2)}) %collective-permute-start.24) | collective-permute-done | bytes 524320 | tf_op jit(solution)/shard_map/ppermute | solution.py:18
  214.3 2.6 advance.3
  216.9 2.9 collective-permute-start.26
  229.8 25.4 %s4_sums.1.refs_0_ = f32[4,256,128]{2,1,0:T(8,128)} custom-call(f32[256,8,128]{2,1,0:T(8,128)} %get-tuple-element.74.refs_0_, f32[256,8,128]{2,1,0:T(8,128)} %get-tuple-element.75.refs_1_, f32[256,8,128]{2,1,0:T(8,128)} %get-tuple-element.76.refs_2_, f32[256,8,128]{2,1,0:T(8,128)} %get-tuple-element.77.refs_3_, f32[256,8,128]{2,1,0:T(8,128)} %get-tuple-element.78.refs_4_, ...), custom_call_target="tpu_custom_call" | custom-call | bytes 1800000 | tf_op jit(solution)/shard_map/s4_sums/pallas_call | solution.py:747
  256.1 9.7 %collective-permute-done.32.refs_3_ = bf16[256,1024]{1,0:T(8,128)(2,1)S(1)} collective-permute-done((bf16[256,1024]{1,0:T(8,128)(2,1)S(1)}, bf16[256,1024]{1,0:T(8,128)(2,1)S(1)}, u32[]{:S(2)}, u32[]{:S(2)}) %collective-permute-start.32) | collective-permute-done | bytes 524320 | tf_op jit(solution)/shard_map/ppermute | solution.py:18
  266.6 2.2 join_sum.1.refs_2_.refs_0_.refs_4_
  270.7 6.6 %all-to-all-start.5 = ((bf16[8,128,256]{2,1,0:T(8,128)(2,1)}), bf16[8,128,256]{2,1,0:T(8,128)(2,1)S(1)}, u32[]{:S(2)}, u32[]{:S(2)}) async-start(bf16[8,128,256]{2,1,0:T(8,128)(2,1)} %bitcast.25), calls=%async_computation.5 | async-start | bytes 1048576 | tf_op jit(solution)/shard_map/all_to_all | solution.py:829
  278.4 2.1 collective-permute-start.36
  282.0 3.2 convolution_convert_fusion.3
  285.2 2.6 fusion.44
  289.3 3.3 all-to-all-done.5.refs_3_
  295.1 3.8 %all-to-all-start.6 = ((bf16[8,112,128]{2,1,0:T(8,128)(2,1)}), bf16[8,112,128]{2,1,0:T(8,128)(2,1)S(1)}, u32[]{:S(2)}, u32[]{:S(2)}) async-start(bf16[8,112,128]{2,1,0:T(8,128)(2,1)} %pack_small.1), calls=%async_computation.6 | async-start | bytes 458752 | tf_op jit(solution)/shard_map/all_to_all | solution.py:59
  298.9 4.3 %collective-permute-done.36.refs_1_.refs_5_ = bf16[256,1536]{1,0:T(8,128)(2,1)S(1)} collective-permute-done((bf16[256,1536]{1,0:T(8,128)(2,1)S(1)}, bf16[256,1536]{1,0:T(8,128)(2,1)S(1)}, u32[]{:S(2)}, u32[]{:S(2)}) %collective-permute-start.36) | collective-permute-done | bytes 786464 | tf_op jit(solution)/shard_map/ppermute | solution.py:18
  303.2 4.1 %collective-permute-done.37.refs_2_.refs_6_ = bf16[256,1536]{1,0:T(8,128)(2,1)} collective-permute-done((bf16[256,1536]{1,0:T(8,128)(2,1)S(1)}, bf16[256,1536]{1,0:T(8,128)(2,1)}, u32[]{:S(2)}, u32[]{:S(2)}) %collective-permute-start.37) | collective-permute-done | bytes 786464 | tf_op jit(solution)/shard_map/ppermute | solution.py:18
  307.3 18.0 %collective-permute-done.38.refs_3_.refs_7_ = bf16[256,1536]{1,0:T(8,128)(2,1)} collective-permute-done((bf16[256,1536]{1,0:T(8,128)(2,1)S(1)}, bf16[256,1536]{1,0:T(8,128)(2,1)}, u32[]{:S(2)}, u32[]{:S(2)}) %collective-permute-start.38) | collective-permute-done | bytes 786464 | tf_op jit(solution)/shard_map/ppermute | solution.py:18
  325.3 3.2 all-to-all-done.6.refs_0_
  330.9 3.4 all-to-all-start.7
  334.9 3.6 fusion.43
  338.5 3.7 %all-to-all-done.7 = bf16[8,112,128]{2,1,0:T(8,128)(2,1)S(1)} async-done(((bf16[8,112,128]{2,1,0:T(8,128)(2,1)}), bf16[8,112,128]{2,1,0:T(8,128)(2,1)S(1)}, u32[]{:S(2)}, u32[]{:S(2)}) %all-to-all-start.7) | async-done | bytes 229408 | tf_op jit(solution)/shard_map/all_to_all | solution.py:59
  342.2 3.5 all-to-all-start.4
  347.4 3.4 finish.3
  350.8 4.1 %finish.4 = f32[1024,1024]{1,0:T(8,128)} custom-call(s32[4]{0:T(128)} %add_add_fusion.6.scalars, bf16[256,1024]{1,0:T(8,128)(2,1)} %get-tuple-element.72.refs_0_, bf16[256,1024]{1,0:T(8,128)(2,1)} %copy-done.13, bf16[256,1024]{1,0:T(8,128)(2,1)} %copy-done.14, bf16[256,1024]{1,0:T(8,128)(2,1)} %copy-done.15, ...), custom_call_target="tpu_custom_call" | custom-call | bytes 300000 | tf_op jit(solution)/shard_map/finish/pallas_call | solution.py:260
  354.9 4.3 %finish.5 = f32[1024,1024]{1,0:T(8,128)} custom-call(s32[4]{0:T(128)} %add_add_fusion.7.scalars, bf16[256,1024]{1,0:T(8,128)(2,1)} %get-tuple-element.72.refs_0_, bf16[256,1024]{1,0:T(8,128)(2,1)} %copy-done.13, bf16[256,1024]{1,0:T(8,128)(2,1)} %copy-done.14, bf16[256,1024]{1,0:T(8,128)(2,1)} %copy-done.15, ...), custom_call_target="tpu_custom_call" | custom-call | bytes 300000 | tf_op jit(solution)/shard_map/finish/pallas_call | solution.py:260
  (288 shorter events, 69.9 us)
Async XLA Ops:
  0.7 88.6 %copy-start = (bf16[1024,1024]{1,0:T(8,128)(2,1)S(1)}, bf16[1024,1024]{1,0:T(8,128)(2,1)}, u32[]{:S(2)}) copy-start(bf16[1024,1024]{1,0:T(8,128)(2,1)} %param.37) | copy-start | bytes 6291460
  3.1 35.2 %all-to-all-start = ((bf16[8,128,512]{2,1,0:T(8,128)(2,1)}), bf16[8,128,512]{2,1,0:T(8,128)(2,1)S(1)}, u32[]{:S(2)}, u32[]{:S(2)}) async-start(bf16[8,128,512]{2,1,0:T(8,128)(2,1)} %pad_maximum_fusion), calls=%async_computation | async-start | bytes 2097152 | tf_op jit(solution)/shard_map/all_to_all | solution.py:829
  38.7 4.5 %collective-permute-start.2 = (f32[2,1024]{1,0:T(2,128)S(1)}, f32[2,1024]{1,0:T(2,128)S(1)}, u32[]{:S(2)}, u32[]{:S(2)}) collective-permute-start(f32[2,1024]{1,0:T(2,128)S(1)} %pad_maximum_fusion.14), channel_id=1, source_target_pairs={{0,3},{1,2},{2,1},{3,0},{4,7},{5,6},{6,5},{7,4},{8,11},{9,10},{10,... | collective-permute-start | bytes 24584 | tf_op jit(solution)/shard_map/ppermute | solution.py:18
  39.4 3.8 %collective-permute-start = (f32[2,1024]{1,0:T(2,128)S(1)}, f32[2,1024]{1,0:T(2,128)S(1)}, u32[]{:S(2)}, u32[]{:S(2)}) collective-permute-start(f32[2,1024]{1,0:T(2,128)S(1)} %pad_maximum_fusion.14), channel_id=1, source_target_pairs={{0,1},{1,0},{2,3},{3,2},{4,5},{5,4},{6,7},{7,6},{8,9},{9,8},{10,11... | collective-permute-start | bytes 24584 | tf_op jit(solution)/shard_map/ppermute | solution.py:18
  40.4 3.7 %collective-permute-start.1 = (f32[2,1024]{1,0:T(2,128)S(1)}, f32[2,1024]{1,0:T(2,128)S(1)}, u32[]{:S(2)}, u32[]{:S(2)}) collective-permute-start(f32[2,1024]{1,0:T(2,128)S(1)} %pad_maximum_fusion.14), channel_id=1, source_target_pairs={{0,2},{1,3},{2,0},{3,1},{4,6},{5,7},{6,4},{7,5},{8,10},{9,11},{10,... | collective-permute-start | bytes 24584 | tf_op jit(solution)/shard_map/ppermute | solution.py:18
  41.6 23.3 %collective-permute-start.3 = (bf16[1024,256]{1,0:T(8,128)(2,1)S(1)}, bf16[1024,256]{1,0:T(8,128)(2,1)}, u32[]{:S(2)}, u32[]{:S(2)}) collective-permute-start(bf16[1024,256]{1,0:T(8,128)(2,1)S(1)} %slice.104), channel_id=1, source_target_pairs={{0,2},{1,3},{2,0},{3,1},{4,6},{5,7},{6,4},{7,5},{8,10},{9,11},{10,... | collective-permute-start | bytes 1572872 | tf_op jit(solution)/shard_map/ppermute | solution.py:18
  43.2 45.2 %collective-permute-start.13 = (bf16[1024,256]{1,0:T(8,128)(2,1)S(1)}, bf16[1024,256]{1,0:T(8,128)(2,1)S(1)}, u32[]{:S(2)}, u32[]{:S(2)}) collective-permute-start(bf16[1024,256]{1,0:T(8,128)(2,1)S(1)} %slice.104), channel_id=1, source_target_pairs={{0,1},{1,0},{2,3},{3,2},{4,5},{5,4},{6,7},{7,6},{8,9},{9,8},{10,11... | collective-permute-start | bytes 1572872 | tf_op jit(solution)/shard_map/ppermute | solution.py:18
  65.0 13.7 %collective-permute-start.5 = (bf16[1024,256]{1,0:T(8,128)(2,1)}, bf16[1024,256]{1,0:T(8,128)(2,1)S(1)}, u32[]{:S(2)}, u32[]{:S(2)}) collective-permute-start(bf16[1024,256]{1,0:T(8,128)(2,1)} %get-tuple-element.59), channel_id=1, source_target_pairs={{0,2},{1,3},{2,0},{3,1},{4,6},{5,7},{6,4},{7,5},{8,10},{9,11},{10,... | collective-permute-start | bytes 1572872 | tf_op jit(solution)/shard_map/ppermute | solution.py:18
  66.3 12.9 %collective-permute-start.4 = (bf16[1024,256]{1,0:T(8,128)(2,1)S(1)}, bf16[1024,256]{1,0:T(8,128)(2,1)S(1)}, u32[]{:S(2)}, u32[]{:S(2)}) collective-permute-start(bf16[1024,256]{1,0:T(8,128)(2,1)S(1)} %copy-done.50), channel_id=1, source_target_pairs={{0,1},{1,0},{2,3},{3,2},{4,5},{5,4},{6,7},{7,6},{8,9},{9,8},{10,11... | collective-permute-start | bytes 1572872 | tf_op jit(solution)/shard_map/ppermute | solution.py:18
  66.3 39.2 %collective-permute-start.14 = (bf16[1024,256]{1,0:T(8,128)(2,1)}, bf16[1024,256]{1,0:T(8,128)(2,1)}, u32[]{:S(2)}, u32[]{:S(2)}) collective-permute-start(bf16[1024,256]{1,0:T(8,128)(2,1)} %collective-permute-done.3), channel_id=1, source_target_pairs={{0,1},{1,0},{2,3},{3,2},{4,5},{5,4},{6,7},{7,6},{8,9},{9,8},{10,11... | collective-permute-start | bytes 1572872 | tf_op jit(solution)/shard_map/ppermute | solution.py:18
  78.7 1.9 collective-permute-start.6
  82.0 4.0 %collective-permute-start.9 = (f32[2,1024]{1,0:T(2,128)S(1)}, f32[2,1024]{1,0:T(2,128)S(1)}, u32[]{:S(2)}, u32[]{:S(2)}) collective-permute-start(f32[2,1024]{1,0:T(2,128)S(1)} %pad_maximum_fusion.15), channel_id=1, source_target_pairs={{0,3},{1,2},{2,1},{3,0},{4,7},{5,6},{6,5},{7,4},{8,11},{9,10},{10,... | collective-permute-start | bytes 24584 | tf_op jit(solution)/shard_map/ppermute | solution.py:18
  82.3 3.7 %collective-permute-start.7 = (f32[2,1024]{1,0:T(2,128)S(1)}, f32[2,1024]{1,0:T(2,128)S(1)}, u32[]{:S(2)}, u32[]{:S(2)}) collective-permute-start(f32[2,1024]{1,0:T(2,128)S(1)} %pad_maximum_fusion.15), channel_id=1, source_target_pairs={{0,1},{1,0},{2,3},{3,2},{4,5},{5,4},{6,7},{7,6},{8,9},{9,8},{10,11... | collective-permute-start | bytes 24584 | tf_op jit(solution)/shard_map/ppermute | solution.py:18
  82.7 3.7 %collective-permute-start.8 = (f32[2,1024]{1,0:T(2,128)S(1)}, f32[2,1024]{1,0:T(2,128)S(1)}, u32[]{:S(2)}, u32[]{:S(2)}) collective-permute-start(f32[2,1024]{1,0:T(2,128)S(1)} %pad_maximum_fusion.15), channel_id=1, source_target_pairs={{0,2},{1,3},{2,0},{3,1},{4,6},{5,7},{6,4},{7,5},{8,10},{9,11},{10,... | collective-permute-start | bytes 24584 | tf_op jit(solution)/shard_map/ppermute | solution.py:18
  86.8 13.5 %collective-permute-start.11 = (bf16[1024,256]{1,0:T(8,128)(2,1)S(1)}, bf16[1024,256]{1,0:T(8,128)(2,1)S(1)}, u32[]{:S(2)}, u32[]{:S(2)}) collective-permute-start(bf16[1024,256]{1,0:T(8,128)(2,1)S(1)} %add_convert_fusion), channel_id=1, source_target_pairs={{0,2},{1,3},{2,0},{3,1},{4,6},{5,7},{6,4},{7,5},{8,10},{9,11},{10,... | collective-permute-start | bytes 1572872 | tf_op jit(solution)/shard_map/ppermute | solution.py:18
  89.2 11.9 %collective-permute-start.10 = (bf16[1024,256]{1,0:T(8,128)(2,1)S(1)}, bf16[1024,256]{1,0:T(8,128)(2,1)S(1)}, u32[]{:S(2)}, u32[]{:S(2)}) collective-permute-start(bf16[1024,256]{1,0:T(8,128)(2,1)S(1)} %add_convert_fusion), channel_id=1, source_target_pairs={{0,1},{1,0},{2,3},{3,2},{4,5},{5,4},{6,7},{7,6},{8,9},{9,8},{10,11... | collective-permute-start | bytes 1572872 | tf_op jit(solution)/shard_map/ppermute | solution.py:18
  100.3 2.0 collective-permute-start.12
  117.2 30.3 %all-to-all-start.1 = ((bf16[4,256,1024]{2,1,0:T(8,128)(2,1)}), bf16[4,256,1024]{2,1,0:T(8,128)(2,1)}, u32[]{:S(2)}, u32[]{:S(2)}) async-start(bf16[4,256,1024]{2,1,0:T(8,128)(2,1)} %bitcast.72), calls=%async_computation.1 | async-start | bytes 4194304 | tf_op jit(solution)/shard_map/all_to_all | solution.py:130
  124.1 2.0 collective-permute-start.15
  125.1 2.8 collective-permute-start.16
  126.9 14.0 %collective-permute-start.17 = (bf16[1024,256]{1,0:T(8,128)(2,1)S(1)}, bf16[1024,256]{1,0:T(8,128)(2,1)S(1)}, u32[]{:S(2)}, u32[]{:S(2)}) collective-permute-start(bf16[1024,256]{1,0:T(8,128)(2,1)S(1)} %convert_add_fusion.7), channel_id=1, source_target_pairs={{0,2},{1,3},{2,0},{3,1},{4,6},{5,7},{6,4},{7,5},{8,10},{9,11},{10,... | collective-permute-start | bytes 1572872 | tf_op jit(solution)/shard_map/ppermute | solution.py:18
  147.4 29.8 %all-to-all-start.2 = ((bf16[4,256,1024]{2,1,0:T(8,128)(2,1)}), bf16[4,256,1024]{2,1,0:T(8,128)(2,1)}, u32[]{:S(2)}, u32[]{:S(2)}) async-start(bf16[4,256,1024]{2,1,0:T(8,128)(2,1)} %bitcast.71), calls=%async_computation.2 | async-start | bytes 4194304 | tf_op jit(solution)/shard_map/all_to_all | solution.py:130
  152.0 3.1 collective-permute-start.20
  152.3 2.9 collective-permute-start.18
  153.2 3.7 %collective-permute-start.19 = (f32[2,1024]{1,0:T(2,128)S(1)}, f32[2,1024]{1,0:T(2,128)S(1)}, u32[]{:S(2)}, u32[]{:S(2)}) collective-permute-start(f32[2,1024]{1,0:T(2,128)S(1)} %pad_maximum_fusion.16), channel_id=1, source_target_pairs={{0,2},{1,3},{2,0},{3,1},{4,6},{5,7},{6,4},{7,5},{8,10},{9,11},{10,... | collective-permute-start | bytes 24584 | tf_op jit(solution)/shard_map/ppermute | solution.py:18
  160.6 2.0 collective-permute-start.22
  161.2 5.4 %collective-permute-start.21 = (bf16[1024,256]{1,0:T(8,128)(2,1)S(1)}, bf16[1024,256]{1,0:T(8,128)(2,1)S(1)}, u32[]{:S(2)}, u32[]{:S(2)}) collective-permute-start(bf16[1024,256]{1,0:T(8,128)(2,1)S(1)} %convolution_convert_fusion.1), channel_id=1, source_target_pairs={{0,1},{1,0},{2,3},{3,2},{4,5},{5,4},{6,7},{7,6},{8,9},{9,8},{10,11... | collective-permute-start | bytes 1572872 | tf_op jit(solution)/shard_map/ppermute | solution.py:18
  163.1 14.0 %collective-permute-start.23 = (bf16[1024,256]{1,0:T(8,128)(2,1)S(1)}, bf16[1024,256]{1,0:T(8,128)(2,1)S(1)}, u32[]{:S(2)}, u32[]{:S(2)}) collective-permute-start(bf16[1024,256]{1,0:T(8,128)(2,1)S(1)} %fusion.96), channel_id=1, source_target_pairs={{0,2},{1,3},{2,0},{3,1},{4,6},{5,7},{6,4},{7,5},{8,10},{9,11},{10,... | collective-permute-start | bytes 1572872 | tf_op jit(solution)/shard_map/ppermute | solution.py:18
  177.3 30.8 %all-to-all-start.3 = ((bf16[4,256,512]{2,1,0:T(8,128)(2,1)}), bf16[4,256,512]{2,1,0:T(8,128)(2,1)}, u32[]{:S(2)}, u32[]{:S(2)}) async-start(bf16[4,256,512]{2,1,0:T(8,128)(2,1)} %bitcast.76), calls=%async_computation.3 | async-start | bytes 2097152 | tf_op jit(solution)/shard_map/all_to_all | solution.py:130
  187.9 25.6 %collective-permute-start.24 = (bf16[256,1024]{1,0:T(8,128)(2,1)}, bf16[256,1024]{1,0:T(8,128)(2,1)S(1)}, u32[]{:S(2)}, u32[]{:S(2)}) collective-permute-start(bf16[256,1024]{1,0:T(8,128)(2,1)} %get-tuple-element.69.refs_1_), channel_id=1, source_target_pairs={{0,16},{4,20},{8,24},{12,28},{16,0},{20,4},{24,8},{28,12},{1,17},{... | collective-permute-start | bytes 1572872 | tf_op jit(solution)/shard_map/ppermute | solution.py:18
  216.9 38.3 %collective-permute-start.25 = (bf16[256,1024]{1,0:T(8,128)(2,1)}, bf16[256,1024]{1,0:T(8,128)(2,1)S(1)}, u32[]{:S(2)}, u32[]{:S(2)}) collective-permute-start(bf16[256,1024]{1,0:T(8,128)(2,1)} %get-tuple-element.72.refs_0_), channel_id=1, source_target_pairs={{0,16},{4,20},{8,24},{12,28},{16,0},{20,4},{24,8},{28,12},{1,17},{... | collective-permute-start | bytes 1572872 | tf_op jit(solution)/shard_map/ppermute | solution.py:18
  216.9 38.3 %collective-permute-start.26 = (bf16[256,512]{1,0:T(8,128)(2,1)}, bf16[256,512]{1,0:T(8,128)(2,1)S(1)}, u32[]{:S(2)}, u32[]{:S(2)}) collective-permute-start(bf16[256,512]{1,0:T(8,128)(2,1)} %get-tuple-element.73.own), channel_id=1, source_target_pairs={{0,16},{4,20},{8,24},{12,28},{16,0},{20,4},{24,8},{28,12},{1,17},{... | collective-permute-start | bytes 786440 | tf_op jit(solution)/shard_map/ppermute | solution.py:18
  220.8 3.1 collective-permute-start.29
  220.8 5.0 %collective-permute-start.27 = (f32[2,1024]{1,0:T(2,128)S(1)}, f32[2,1024]{1,0:T(2,128)S(1)}, u32[]{:S(2)}, u32[]{:S(2)}) collective-permute-start(f32[2,1024]{1,0:T(2,128)S(1)} %pad_maximum_fusion.17), channel_id=1, source_target_pairs={{0,1},{1,0},{2,3},{3,2},{4,5},{5,4},{6,7},{7,6},{8,9},{9,8},{10,11... | collective-permute-start | bytes 24584 | tf_op jit(solution)/shard_map/ppermute | solution.py:18
  222.0 4.9 %collective-permute-start.28 = (f32[2,1024]{1,0:T(2,128)S(1)}, f32[2,1024]{1,0:T(2,128)S(1)}, u32[]{:S(2)}, u32[]{:S(2)}) collective-permute-start(f32[2,1024]{1,0:T(2,128)S(1)} %pad_maximum_fusion.17), channel_id=1, source_target_pairs={{0,2},{1,3},{2,0},{3,1},{4,6},{5,7},{6,4},{7,5},{8,10},{9,11},{10,... | collective-permute-start | bytes 24584 | tf_op jit(solution)/shard_map/ppermute | solution.py:18
  223.9 31.3 %collective-permute-start.30 = (bf16[256,1024]{1,0:T(8,128)(2,1)S(1)}, bf16[256,1024]{1,0:T(8,128)(2,1)S(1)}, u32[]{:S(2)}, u32[]{:S(2)}) collective-permute-start(bf16[256,1024]{1,0:T(8,128)(2,1)S(1)} %copy-done.24), channel_id=1, source_target_pairs={{0,4},{4,0},{8,12},{12,8},{16,20},{20,16},{24,28},{28,24},{1,5},{5... | collective-permute-start | bytes 1572872 | tf_op jit(solution)/shard_map/ppermute | solution.py:18
  225.8 30.3 %collective-permute-start.31 = (bf16[256,1024]{1,0:T(8,128)(2,1)S(1)}, bf16[256,1024]{1,0:T(8,128)(2,1)S(1)}, u32[]{:S(2)}, u32[]{:S(2)}) collective-permute-start(bf16[256,1024]{1,0:T(8,128)(2,1)S(1)} %copy-done.24), channel_id=1, source_target_pairs={{0,8},{4,12},{8,0},{12,4},{16,24},{20,28},{24,16},{28,20},{1,9},{5... | collective-permute-start | bytes 1572872 | tf_op jit(solution)/shard_map/ppermute | solution.py:18
  226.9 38.9 %collective-permute-start.32 = (bf16[256,1024]{1,0:T(8,128)(2,1)S(1)}, bf16[256,1024]{1,0:T(8,128)(2,1)S(1)}, u32[]{:S(2)}, u32[]{:S(2)}) collective-permute-start(bf16[256,1024]{1,0:T(8,128)(2,1)S(1)} %copy-done.24), channel_id=1, source_target_pairs={{0,12},{4,8},{8,4},{12,0},{16,28},{20,24},{24,20},{28,16},{1,13},{... | collective-permute-start | bytes 1572872 | tf_op jit(solution)/shard_map/ppermute | solution.py:18
  270.6 14.5 %collective-permute-start.34 = (bf16[1024,256]{1,0:T(8,128)(2,1)S(1)}, bf16[1024,256]{1,0:T(8,128)(2,1)S(1)}, u32[]{:S(2)}, u32[]{:S(2)}) collective-permute-start(bf16[1024,256]{1,0:T(8,128)(2,1)S(1)} %convolution_convert_fusion.2), channel_id=1, source_target_pairs={{0,1},{1,0},{2,3},{3,2},{4,5},{5,4},{6,7},{7,6},{8,9},{9,8},{10,11... | collective-permute-start | bytes 1572872 | tf_op jit(solution)/shard_map/ppermute | solution.py:18
  270.7 21.8 %all-to-all-start.5 = ((bf16[8,128,256]{2,1,0:T(8,128)(2,1)}), bf16[8,128,256]{2,1,0:T(8,128)(2,1)S(1)}, u32[]{:S(2)}, u32[]{:S(2)}) async-start(bf16[8,128,256]{2,1,0:T(8,128)(2,1)} %bitcast.25), calls=%async_computation.5 | async-start | bytes 1048576 | tf_op jit(solution)/shard_map/all_to_all | solution.py:829
  278.4 24.8 %collective-permute-start.36 = (bf16[256,1536]{1,0:T(8,128)(2,1)S(1)}, bf16[256,1536]{1,0:T(8,128)(2,1)S(1)}, u32[]{:S(2)}, u32[]{:S(2)}) collective-permute-start(bf16[256,1536]{1,0:T(8,128)(2,1)S(1)} %copy-done.4), channel_id=1, source_target_pairs={{0,4},{4,0},{8,12},{12,8},{16,20},{20,16},{24,28},{28,24},{1,5},{5... | collective-permute-start | bytes 2359304 | tf_op jit(solution)/shard_map/ppermute | solution.py:18
  280.4 26.8 %collective-permute-start.37 = (bf16[256,1536]{1,0:T(8,128)(2,1)S(1)}, bf16[256,1536]{1,0:T(8,128)(2,1)}, u32[]{:S(2)}, u32[]{:S(2)}) collective-permute-start(bf16[256,1536]{1,0:T(8,128)(2,1)S(1)} %copy-done.4), channel_id=1, source_target_pairs={{0,8},{4,12},{8,0},{12,4},{16,24},{20,28},{24,16},{28,20},{1,9},{5... | collective-permute-start | bytes 2359304 | tf_op jit(solution)/shard_map/ppermute | solution.py:18
  281.9 43.4 %collective-permute-start.38 = (bf16[256,1536]{1,0:T(8,128)(2,1)S(1)}, bf16[256,1536]{1,0:T(8,128)(2,1)}, u32[]{:S(2)}, u32[]{:S(2)}) collective-permute-start(bf16[256,1536]{1,0:T(8,128)(2,1)S(1)} %copy-done.4), channel_id=1, source_target_pairs={{0,12},{4,8},{8,4},{12,0},{16,28},{20,24},{24,20},{28,16},{1,13},{... | collective-permute-start | bytes 2359304 | tf_op jit(solution)/shard_map/ppermute | solution.py:18
  285.2 49.7 %collective-permute-start.33 = (bf16[1024,256]{1,0:T(8,128)(2,1)}, bf16[1024,256]{1,0:T(8,128)(2,1)}, u32[]{:S(2)}, u32[]{:S(2)}) collective-permute-start(bf16[1024,256]{1,0:T(8,128)(2,1)} %convolution_convert_fusion.3), channel_id=1, source_target_pairs={{0,1},{1,0},{2,3},{3,2},{4,5},{5,4},{6,7},{7,6},{8,9},{9,8},{10,11... | collective-permute-start | bytes 1572872 | tf_op jit(solution)/shard_map/ppermute | solution.py:18
  287.7 47.2 %collective-permute-start.35 = (bf16[1024,256]{1,0:T(8,128)(2,1)}, bf16[1024,256]{1,0:T(8,128)(2,1)}, u32[]{:S(2)}, u32[]{:S(2)}) collective-permute-start(bf16[1024,256]{1,0:T(8,128)(2,1)} %fusion.44), channel_id=1, source_target_pairs={{0,2},{1,3},{2,0},{3,1},{4,6},{5,7},{6,4},{7,5},{8,10},{9,11},{10,... | collective-permute-start | bytes 1572872 | tf_op jit(solution)/shard_map/ppermute | solution.py:18
  295.1 33.4 %all-to-all-start.6 = ((bf16[8,112,128]{2,1,0:T(8,128)(2,1)}), bf16[8,112,128]{2,1,0:T(8,128)(2,1)S(1)}, u32[]{:S(2)}, u32[]{:S(2)}) async-start(bf16[8,112,128]{2,1,0:T(8,128)(2,1)} %pack_small.1), calls=%async_computation.6 | async-start | bytes 458752 | tf_op jit(solution)/shard_map/all_to_all | solution.py:59
  330.9 11.4 %all-to-all-start.7 = ((bf16[8,112,128]{2,1,0:T(8,128)(2,1)}), bf16[8,112,128]{2,1,0:T(8,128)(2,1)S(1)}, u32[]{:S(2)}, u32[]{:S(2)}) async-start(bf16[8,112,128]{2,1,0:T(8,128)(2,1)} %sum_small.1), calls=%async_computation.7 | async-start | bytes 458752 | tf_op jit(solution)/shard_map/all_to_all | solution.py:59
  342.2 21.5 %all-to-all-start.4 = ((bf16[8,128,256]{2,1,0:T(8,128)(2,1)}), bf16[8,128,256]{2,1,0:T(8,128)(2,1)S(1)}, u32[]{:S(2)}, u32[]{:S(2)}) async-start(bf16[8,128,256]{2,1,0:T(8,128)(2,1)} %bitcast.24), calls=%async_computation.4 | async-start | bytes 1048576 | tf_op jit(solution)/shard_map/all_to_all | solution.py:829
  (70 other events, 487.5 us)

commit v3 on v2

--- a/solution.py
+++ b/solution.py
@@ -59,66 +59,97 @@
     return lax.all_to_all(x, "seq", 0, 0, tiled=True)
 
 
-def small_kernel(share, parts, *refs):
-    out = refs[-1]
-    total = sum(parts[k].astype(FULL) for k in range(parts.shape[0]))
-    narrow = total[share : share + 8] + total[share + 8 : share + 16]
-    high = narrow.astype(LOW).astype(FULL)
-    rows = [total[:share], high, narrow - high]
-    fill = total.shape[0] - share - 16
-    if fill:
-        rows.append(jnp.zeros((fill, total.shape[1]), FULL))
-    total = jnp.concatenate(rows, axis=0).astype(LOW)
-    for k in range(parts.shape[0]):
-        out[k] = total
-
-
-def pack_kernel(share, sums, narrow, *refs):
-    packed = refs[-1]
-    seqs, rows, lanes = packed.shape
-    groups, width, _ = sums.shape
-    flat = sums[: groups - 1].reshape((groups - 1) * width, lanes)
-    for k in range(seqs):
-        part = narrow[k]
-        high = part.astype(LOW).astype(FULL)
-        pieces = [flat[k * share : (k + 1) * share], high, part - high]
-        if rows > share + 16:
-            pieces.append(jnp.zeros((rows - share - 16, lanes), FULL))
-        packed[k] = jnp.concatenate(pieces, axis=0).astype(LOW)
-
-
-def sum_small(sums, narrow, deps, late_deps):
+def small_shares(sums, size):
     seqs = lax.axis_size("seq")
     groups, width, lanes = sums.shape
+    short = -(-size // (seqs * lanes))
+    assert short <= 8
     share = (groups - 1) * width // seqs
-    short = -(-narrow.shape[0] // (seqs * lanes))
-    assert short <= 8
-    rows = -(-(share + 16) // 16) * 16
-    narrow_rows = jnp.pad(narrow, (0, seqs * short * lanes - narrow.shape[0])).reshape(seqs, short, lanes)
+    return share, short, -(-(share + 16) // 16) * 16
+
+
+def pack_small(sums, narrow):
+    seqs = lax.axis_size("seq")
+    groups, width, lanes = sums.shape
+    size = narrow.shape[0]
+    share, short, rows = small_shares(sums, size)
+    narrow_rows = jnp.pad(narrow, (0, seqs * short * lanes - size)).reshape(seqs, short, lanes)
     narrow_rows = jnp.pad(narrow_rows, ((0, 0), (0, 8 - short), (0, 0)))
+
+    def pack(sums, narrow, packed):
+        flat = sums[: groups - 1].reshape((groups - 1) * width, lanes)
+        for k in range(seqs):
+            part = narrow[k]
+            high = part.astype(LOW).astype(FULL)
+            pieces = [flat[k * share : (k + 1) * share], high, part - high]
+            if rows > share + 16:
+                pieces.append(jnp.zeros((rows - share - 16, lanes), FULL))
+            packed[k] = jnp.concatenate(pieces, axis=0).astype(LOW)
+
+    shape = jax.ShapeDtypeStruct((seqs, rows, lanes), LOW)
+    return call_here(pack, [sums, narrow_rows], [], [shape], "pack_small")[0]
+
+
+def sum_small(dealt, sums, size, deps):
+    seqs, rows, lanes = dealt.shape
+    groups, width, _ = sums.shape
+    share, short, _ = small_shares(sums, size)
+
+    def add(dealt, out):
+        total = sum(dealt[k].astype(FULL) for k in range(seqs))
+        narrow = total[share : share + 8] + total[share + 8 : share + 16]
+        high = narrow.astype(LOW).astype(FULL)
+        pieces = [total[:share], high, narrow - high] + ([total[share + 16 :]] if rows > share + 16 else [])
+        total = jnp.concatenate(pieces, axis=0).astype(LOW)
+        for k in range(seqs):
+            out[k] = total
+
+    parts = exchange_all(call_here(add, [dealt], deps, [jax.ShapeDtypeStruct(dealt.shape, LOW)], "sum_small")[0])
+    states = lanes // 2
+
+    def unpack(parts, decay, freq, b, c, narrow):
+        flat = jnp.concatenate([parts[k, :share, :].astype(FULL) for k in range(seqs)], axis=0)
+        a, b_both, c_both = (flat[g * width : (g + 1) * width].T for g in range(3))
+        decay[...], freq[...] = a[:states], a[states:]
+        b[0], b[1] = b_both[:states], b_both[states:]
+        c[0], c[1] = c_both[:states], c_both[states:]
+        for k in range(seqs):
+            part = parts[k].astype(FULL)
+            narrow[k] = part[share : share + 8] + part[share + 8 : share + 16]
+
+    one, two = (states, width), (2, states, width)
+    *wide, narrow = call_here(
+        unpack,
+        [parts],
+        [],
+        [jax.ShapeDtypeStruct(shape, FULL) for shape in (one, one, two, two, (seqs, 8, lanes))],
+        "unpack_small",
+    )
+    return parts, wide, narrow[:, :short].reshape(-1)[:size]
+
+
+def beside(left, right, deps):
+    rows, columns = left.shape
+
+    def kernel(left, right, out):
+        out[:, :columns] = left[...]
+        out[:, columns:] = right[...]
+
+    shape = jax.ShapeDtypeStruct((rows, columns + right.shape[1]), left.dtype)
+    return call_here(kernel, [left, right], deps, [shape], "beside")[0]
+
+
+def call_here(kernel, ins, deps, outs, name):
     here, anywhere = pl.BlockSpec(memory_space=pltpu.VMEM), pl.BlockSpec(memory_space=pl.ANY)
-    packed = pl.pallas_call(
-        lambda *refs: pack_kernel(share, *refs),
-        in_specs=[here] * 2 + [anywhere] * len(deps),
-        out_specs=here,
-        out_shape=jax.ShapeDtypeStruct((seqs, rows, lanes), LOW),
+    return pl.pallas_call(
+        lambda *refs: kernel(*refs[: len(ins)], *refs[len(ins) + len(deps) :]),
+        in_specs=[here] * len(ins) + [anywhere] * len(deps),
+        out_specs=[here] * len(outs),
+        out_shape=outs,
         compiler_params=pltpu.CompilerParams(vmem_limit_bytes=VMEM),
-        cost_estimate=cost(1),
-        name="pack_small",
-    )(sums, narrow_rows, *deps)
-    total = pl.pallas_call(
-        lambda *refs: small_kernel(share, *refs),
-        in_specs=[here] + [anywhere] * len(late_deps),
-        out_specs=here,
-        out_shape=jax.ShapeDtypeStruct(packed.shape, LOW),
-        compiler_params=pltpu.CompilerParams(vmem_limit_bytes=VMEM),
-        cost_estimate=cost(1),
-        name="sum_small",
-    )(exchange_all(packed), *late_deps)
-    parts = exchange_all(total).astype(FULL)
-    result = parts[:, share : share + short] + parts[:, share + 8 : share + 8 + short]
-    wide = parts[:, :share].reshape(groups - 1, width, lanes)
-    return wide, result.reshape(-1)[: narrow.shape[0]], packed
+        cost_estimate=cost(2),
+        name=name,
+    )(*ins, *deps)
 
 
 QUAD = 4
@@ -153,6 +184,13 @@
 
 def gather(part):
     return [part] + [swap(part, "seq", mask) for mask in range(1, QUAD)]
+
+
+def gather_relayed(part):
+    first, second = swap(part, "seq", 1), swap(part, "seq", 2)
+    half = part.shape[0] // 2
+    third = jnp.concatenate([swap(second[:half], "seq", 1), swap(first[half:], "seq", 2)])
+    return [part, first, second, third]
 
 
 def join_sum(left, own, received, deps):
@@ -934,10 +972,6 @@
     grad_input = (grad_resid + grad_input).astype(LOW)
     wide_own = gather(wide_chain.parts[0])
     sums = s4_sums(*s4_parts, [grad_input], 0, width // CHANNELS)
-    grad_input_moved = exchange(grad_input.reshape(batch, block, width))
-    made = join_sum(wide_chain.parts[1], *gated_chain.parts, [sums, *wide_own[1:]])
-    last = gather(made)
-    grad_input = grad_input_moved.astype(FULL)
     narrow = jnp.concatenate(
         [
             grad_norm1_gain,
@@ -952,11 +986,17 @@
             jnp.sum(grad_hidden.astype(FULL), axis=0),
         ]
     )
-    wide, narrow, packed = sum_small(sums, narrow, [made, grad_input_moved], last[1:])
-    wide = wide.transpose(0, 2, 1)
+    packed = pack_small(sums, narrow)
+    dealt = exchange_all(packed)
+    made = join_sum(wide_chain.parts[1], *gated_chain.parts, [packed, *wide_own[1:]])
+    last = gather_relayed(made)
     spread_late = after(spread, made)
     output = reduce_pieces([dot(spread_late, w) for w in w_downs])
-    output = exchange((resid + output + b_down).astype(LOW).reshape(batch, block, width))
+    output = (resid + output + b_down).astype(LOW)
+    parts, wide, narrow = sum_small(dealt, sums, narrow.shape[0], last[1:3])
+    moved = beside(grad_input, output, [parts, *last[1:]])
+    moved = exchange(moved.reshape(batch, block, 2 * width))
+    grad_input, output = moved[:, :, :width].astype(FULL), moved[:, :, width:]
     vectors = [narrow[k * width : (k + 1) * width] for k in range(9)]
     vectors.insert(2, vectors.pop(8))
 
@@ -969,10 +1009,7 @@
         grad_input,
         vectors[0],
         vectors[1],
-        wide[0, :states],
-        wide[0, states:],
-        wide[1].reshape(2, states, width),
-        wide[2].reshape(2, states, width),
+        *wide,
         vectors[2],
         vectors[3],
         grad_w_value,

time: 372 us -> 354 us (0.952)
  waiting for transfers between devices: 105 us -> 85 us
  starting transfers between devices: 68.9 us -> 63.6 us
  other arithmetic: 16.5 us -> 21 us
  Pallas kernels: 111 us -> 115 us
    ppermute x39 -> x40, waiting for transfers between devices: 89 us -> 71.7 us  [swap(): lax.ppermute(x, axis, [(i, i ^ distance) for i in range(lax.axis_size(axi...]
    all_to_all x3 -> x2, starting transfers between devices: 17.3 us -> 11.8 us  [exchange(): return lax.all_to_all(x, 'seq', 0, 0, axis_index_groups=groups, tiled=True)]
    all_to_all x2, waiting for transfers between devices: 6.95 us -> 2.51 us  [exchange_all(): return lax.all_to_all(x, 'seq', 0, 0, tiled=True)]
    pallas_call x2 -> x4, Pallas kernels: 3.42 us -> 7.61 us  [call_here(): pl.pallas_call(lambda *refs: kernel(*refs[:len(ins)], *refs[len(ins) + le...]
    ppermute x39 -> x40, starting transfers between devices: 30.9 us -> 29.7 us  [swap(): lax.ppermute(x, axis, [(i, i ^ distance) for i in range(lax.axis_size(axi...]
  transfers between devices with their start and end apart: 47 -> 47, of which waited for: 23 -> 19; matrix products, arithmetic and copies ran while one was open for 16% -> 16% of each run, Pallas kernels for 29% -> 31%
where the time goes in v3:
time: 354 us; the launch traced here: 347 us
  Pallas kernels  115 us (32%)
  waiting for transfers between devices  85 us (24%)
  starting transfers between devices  63.6 us (18%)
  matrix products  45.1 us (13%)
  other arithmetic  21 us (6%)
  local copies, waits for them, and re-layouts  15.1 us (4%)
    ppermute x40, waiting for transfers between devices, swap(): lax.ppermute(x, axis, [(i, i ^ distance) for i in range(lax.axis_size(axi...  71.7 us
    ppermute x40, starting transfers between devices, swap(): lax.ppermute(x, axis, [(i, i ^ distance) for i in range(lax.axis_size(axi...  29.7 us
    pallas_call x1, Pallas kernels, s4_sums(): pl.pallas_call(lambda *refs: sums_kernel(block, *refs), grid=(steps,), in...  25.4 us
    pallas_call x1, Pallas kernels, s4_tables(): pl.pallas_call(tables_kernel, grid=(steps,), in_specs=[pl.BlockSpec((8, C...  20 us
    pallas_call x1, Pallas kernels, s4_forward(): pl.pallas_call(forward_kernel, grid=(width // CHANNELS,), in_specs=[whole...  18.8 us
    dot_general x12, matrix products, dot_t(): lax.dot_general(a, b, (((1,), (1,)), ((), ())), preferred_element_type=FULL)  18.4 us
    pallas_call x1, Pallas kernels, s4_backward(): pl.pallas_call(backward_kernel, grid=(width // CHANNELS,), in_specs=[whol...  17.6 us
    dot_general x12, matrix products, dot(): lax.dot_general(a, b, (((1,), (0,)), ((), ())), preferred_element_type=FULL)  15.6 us
  transfers between devices with their start and end apart: 47, of which 19 were waited for; matrix products, arithmetic and copies ran while one was open for 16% of the time, Pallas kernels for 31%

profile of v3, /device:TPU:0, one launch (start us, length us, event | category | flops | bytes accessed | tf_op | source)
XLA Modules:
  0.0 346.7 jit_solution(449571684828399462)
XLA Ops:
  0.7 2.4 pad_maximum_fusion
  3.1 7.3 %all-to-all-start = ((bf16[8,128,512]{2,1,0:T(8,128)(2,1)}), bf16[8,128,512]{2,1,0:T(8,128)(2,1)S(1)}, u32[]{:S(2)}, u32[]{:S(2)}) async-start(bf16[8,128,512]{2,1,0:T(8,128)(2,1)} %pad_maximum_fusion), calls=%async_computation | async-start | bytes 2097152 | tf_op jit(solution)/shard_map/all_to_all | solution.py:867
  10.9 5.1 %s4_consts.1 = (f32[30,256,128]{2,1,0:T(8,128)}, f32[8,256,128]{2,1,0:T(8,128)}) custom-call(f32[64,256]{1,0:T(8,128)} %refs_0_.1, f32[64,256]{1,0:T(8,128)} %refs_1_.1, f32[2,64,256]{2,1,0:T(8,128)} %refs_2_.1, f32[2,64,256]{2,1,0:T(8,128)} %refs_3_.1, f32[1,256]{1,0:T(1,128)} %bitcast.101), custom_call_target="tpu_custom_call" | custom-call | bytes 600000 | tf_op jit(solution)/shard_map/s4_consts/pallas_call | solution.py:421
  16.1 20.0 %s4_tables.1 = (bf16[256,256,128]{2,1,0:T(8,128)(2,1)}, bf16[256,128,128]{2,1,0:T(8,128)(2,1)}) custom-call(f32[8,256,128]{2,1,0:T(8,128)} %get-tuple-element.58.base, f32[30,256,128]{2,1,0:T(8,128)} %get-tuple-element.59.consts.refs_9_), custom_call_target="tpu_custom_call" | custom-call | bytes 2400000 | tf_op jit(solution)/shard_map/s4_tables/pallas_call | solution.py:489
  36.1 2.1 constant_dynamic-slice_fusion
  43.9 1.9 fusion.56.signal
  46.5 18.8 %s4_forward.1 = (bf16[1024,256]{1,0:T(8,128)(2,1)}, f32[1024,256]{1,0:T(8,128)}, f32[256,8,128]{2,1,0:T(8,128)}, f32[256,8,128]{2,1,0:T(8,128)}, f32[256,8,128]{2,1,0:T(8,128)}, /*index=5*/f32[256,8,128]{2,1,0:T(8,128)}) custom-call(bf16[1024,256]{1,0:T(8,128)(2,1)} %fusion.56.signal, f32[1,256]{1,0:T(1,128)} %bitcast.100, ...), custom_call_target="tpu_custom_call" | custom-call | bytes 1800000 | tf_op jit(solution)/shard_map/s4_forward/pallas_call | solution.py:604
  67.3 12.3 %collective-permute-done.5 = bf16[1024,256]{1,0:T(8,128)(2,1)S(1)} collective-permute-done((bf16[1024,256]{1,0:T(8,128)(2,1)}, bf16[1024,256]{1,0:T(8,128)(2,1)S(1)}, u32[]{:S(2)}, u32[]{:S(2)}) %collective-permute-start.5) | collective-permute-done | bytes 524320 | tf_op jit(solution)/shard_map/ppermute | solution.py:18
  88.8 1.8 fusion.91
  91.5 10.2 %collective-permute-done.13 = bf16[1024,256]{1,0:T(8,128)(2,1)S(1)} collective-permute-done((bf16[1024,256]{1,0:T(8,128)(2,1)S(1)}, bf16[1024,256]{1,0:T(8,128)(2,1)S(1)}, u32[]{:S(2)}, u32[]{:S(2)}) %collective-permute-start.13) | collective-permute-done | bytes 524320 | tf_op jit(solution)/shard_map/ppermute | solution.py:18
  103.6 3.2 multiply_convert_fusion
  106.9 7.5 %convert_reduce_fusion = (f32[1024]{0:T(1024)}, bf16[1024,1024]{1,0:T(8,128)(2,1)}) fusion(f32[1024,1024]{1,0:T(8,128)S(1)} %get-tuple-element.146, bf16[1024,256]{1,0:T(8,128)(2,1)} %collective-permute-done.11, bf16[1024,1024]{1,0:T(8,128)(2,1)} %param.39, s32[]{:T(128)S(6)} %select_n.63, f32[1024,1024]{1,0:T(8,128)S(1)} %fusion.88, ...), kind=kOutput, calls=%fused_computation.9 | convolution fusion | flops 563084288 | bytes 19927044 | tf_op jit(solution)/shard_map/dot_general | solution.py:447
  114.4 5.1 %fusion.34 = bf16[1024,1024]{1,0:T(8,128)(2,1)} fusion(bf16[1024,1024]{1,0:T(8,128)(2,1)S(1)} %get-tuple-element.88, bf16[1024,256]{1,0:T(8,128)(2,1)} %collective-permute-done.11, bf16[1024,256]{1,0:T(8,128)(2,1)} %collective-permute-done.3, bf16[1024,256]{1,0:T(8,128)(2,1)} %collective-permute-done.10, bf16[1024,256]{1,0:T(8,128)(2,1)S(1)} %slice.95), kind=kOutput, calls=%fused_computation.38 | convolution fusion | flops 2156920832 | bytes 6291456 | tf_op jit(solution)/shard_map/dot_general | solution.py:808
  119.5 4.5 %all-to-all-start.1 = ((bf16[4,256,1024]{2,1,0:T(8,128)(2,1)}), bf16[4,256,1024]{2,1,0:T(8,128)(2,1)}, u32[]{:S(2)}, u32[]{:S(2)}) async-start(bf16[4,256,1024]{2,1,0:T(8,128)(2,1)} %bitcast.64), calls=%async_computation.1 | async-start | bytes 4194304 | tf_op jit(solution)/shard_map/all_to_all | solution.py:161
  124.0 2.5 convolution_convert_fusion.4
  131.2 3.7 %fusion.31 = bf16[1024,1024]{1,0:T(8,128)(2,1)} fusion(bf16[1024,1024]{1,0:T(8,128)(2,1)S(1)} %copy-done.79, bf16[1024,256]{1,0:T(8,128)(2,1)S(1)} %copy-done.36, bf16[1024,256]{1,0:T(8,128)(2,1)S(1)} %copy-done.26, bf16[1024,256]{1,0:T(8,128)(2,1)S(1)} %copy-done.28, bf16[1024,256]{1,0:T(8,128)(2,1)S(1)} %copy-done.20), kind=kOutput, calls=%fused_computation.37 | convolution fusion | flops 2156920832 | bytes 6291456 | tf_op jit(solution)/shard_map/dot_general | solution.py:808
  134.9 8.3 %collective-permute-done.17 = bf16[1024,256]{1,0:T(8,128)(2,1)S(1)} collective-permute-done((bf16[1024,256]{1,0:T(8,128)(2,1)S(1)}, bf16[1024,256]{1,0:T(8,128)(2,1)S(1)}, u32[]{:S(2)}, u32[]{:S(2)}) %collective-permute-start.17) | collective-permute-done | bytes 524320 | tf_op jit(solution)/shard_map/ppermute | solution.py:18
  145.8 4.0 %all-to-all-done.1.refs_0_ = bf16[4,256,1024]{2,1,0:T(8,128)(2,1)} async-done(((bf16[4,256,1024]{2,1,0:T(8,128)(2,1)}), bf16[4,256,1024]{2,1,0:T(8,128)(2,1)}, u32[]{:S(2)}, u32[]{:S(2)}) %all-to-all-start.1) | async-done | bytes 2097184 | tf_op jit(solution)/shard_map/all_to_all | solution.py:161
  149.8 4.6 %all-to-all-start.2 = ((bf16[4,256,1024]{2,1,0:T(8,128)(2,1)}), bf16[4,256,1024]{2,1,0:T(8,128)(2,1)}, u32[]{:S(2)}, u32[]{:S(2)}) async-start(bf16[4,256,1024]{2,1,0:T(8,128)(2,1)} %bitcast.63), calls=%async_computation.2 | async-start | bytes 4194304 | tf_op jit(solution)/shard_map/all_to_all | solution.py:161
  156.3 2.1 collective-permute-done.19
  159.7 3.0 convert_reduce_fusion.3
  168.3 2.3 fusion.37
  170.6 10.5 %collective-permute-done.23 = bf16[1024,256]{1,0:T(8,128)(2,1)S(1)} collective-permute-done((bf16[1024,256]{1,0:T(8,128)(2,1)S(1)}, bf16[1024,256]{1,0:T(8,128)(2,1)S(1)}, u32[]{:S(2)}, u32[]{:S(2)}) %collective-permute-start.23) | collective-permute-done | bytes 524320 | tf_op jit(solution)/shard_map/ppermute | solution.py:18
  181.2 4.2 %all-to-all-start.3 = ((bf16[4,256,512]{2,1,0:T(8,128)(2,1)}), bf16[4,256,512]{2,1,0:T(8,128)(2,1)S(1)}, u32[]{:S(2)}, u32[]{:S(2)}) async-start(bf16[4,256,512]{2,1,0:T(8,128)(2,1)} %bitcast.65), calls=%async_computation.3 | async-start | bytes 2097152 | tf_op jit(solution)/shard_map/all_to_all | solution.py:161
  185.5 2.4 fusion.47
  187.9 3.6 %advance.2 = (bf16[256,1024]{1,0:T(8,128)(2,1)}, bf16[256,1024]{1,0:T(8,128)(2,1)}) custom-call(s32[1]{0:T(128)} %bitcast.16.high, bf16[4,256,1024]{2,1,0:T(8,128)(2,1)} %all-to-all-done.1.refs_0_, bf16[4,256,1024]{2,1,0:T(8,128)(2,1)} %all-to-all-done.2.refs_1_, bf16[1024,256]{1,0:T(8,128)(2,1)} %get-tuple-element.115.refs_2_.grads), custom_call_target="tpu_custom_call" | custom-call | bytes 200000 | tf_op jit(solution)/shard_map/advance/pallas_call | solution.py:252
  191.6 2.6 collective-permute-start.24
  194.2 17.6 %s4_backward.1 = (f32[1024,256]{1,0:T(8,128)}, f32[256,8,128]{2,1,0:T(8,128)}, f32[256,8,128]{2,1,0:T(8,128)}, f32[256,8,128]{2,1,0:T(8,128)}, f32[256,8,128]{2,1,0:T(8,128)}) custom-call(bf16[1024,256]{1,0:T(8,128)(2,1)} %get-tuple-element.115.refs_2_.grads, f32[30,256,128]{2,1,0:T(8,128)} %get-tuple-element.59.consts.refs_9_, ...), custom_call_target="tpu_custom_call" | custom-call | bytes 1800000 | tf_op jit(solution)/shard_map/s4_backward/pallas_call | solution.py:680
  211.9 5.2 %collective-permute-done.24.refs_1_ = bf16[256,1024]{1,0:T(8,128)(2,1)S(1)} collective-permute-done((bf16[256,1024]{1,0:T(8,128)(2,1)}, bf16[256,1024]{1,0:T(8,128)(2,1)S(1)}, u32[]{:S(2)}, u32[]{:S(2)}) %collective-permute-start.24) | collective-permute-done | bytes 524320 | tf_op jit(solution)/shard_map/ppermute | solution.py:18
  217.9 2.5 advance.3
  225.3 4.2 %collective-permute-start.31 = (bf16[256,1024]{1,0:T(8,128)(2,1)S(1)}, bf16[256,1024]{1,0:T(8,128)(2,1)S(1)}, u32[]{:S(2)}, u32[]{:S(2)}) collective-permute-start(bf16[256,1024]{1,0:T(8,128)(2,1)S(1)} %copy-done.23), channel_id=1, source_target_pairs={{0,8},{4,12},{8,0},{12,4},{16,24},{20,28},{24,16},{28,20},{1,9},{5... | collective-permute-start | bytes 1572872 | tf_op jit(solution)/shard_map/ppermute | solution.py:18
  232.2 25.4 %s4_sums.1.refs_0_ = f32[4,256,128]{2,1,0:T(8,128)} custom-call(f32[256,8,128]{2,1,0:T(8,128)} %get-tuple-element.80.refs_0_, f32[256,8,128]{2,1,0:T(8,128)} %get-tuple-element.81.refs_1_, f32[256,8,128]{2,1,0:T(8,128)} %get-tuple-element.82.refs_2_, f32[256,8,128]{2,1,0:T(8,128)} %get-tuple-element.83.refs_3_, f32[256,8,128]{2,1,0:T(8,128)} %get-tuple-element.84.refs_4_, ...), custom_call_target="tpu_custom_call" | custom-call | bytes 1800000 | tf_op jit(solution)/shard_map/s4_sums/pallas_call | solution.py:785
  259.3 1.9 pack_small.1.refs_0_
  261.2 2.3 collective-permute-done.29.received
  263.6 4.9 %collective-permute-done.32.refs_3_ = bf16[256,1024]{1,0:T(8,128)(2,1)S(1)} collective-permute-done((bf16[256,1024]{1,0:T(8,128)(2,1)S(1)}, bf16[256,1024]{1,0:T(8,128)(2,1)S(1)}, u32[]{:S(2)}, u32[]{:S(2)}) %collective-permute-start.32) | collective-permute-done | bytes 524320 | tf_op jit(solution)/shard_map/ppermute | solution.py:18
  269.3 2.2 join_sum.1.refs_0_.refs_4_
  271.5 1.9 convolution_convert_fusion.2
  280.1 3.4 all-to-all-start.4
  283.5 12.4 %collective-permute-done.37.refs_2_.refs_4_.refs_6_ = bf16[256,1536]{1,0:T(8,128)(2,1)S(1)} collective-permute-done((bf16[256,1536]{1,0:T(8,128)(2,1)}, bf16[256,1536]{1,0:T(8,128)(2,1)S(1)}, u32[]{:S(2)}, u32[]{:S(2)}) %collective-permute-start.37) | collective-permute-done | bytes 786464 | tf_op jit(solution)/shard_map/ppermute | solution.py:18
  300.9 5.5 %all-to-all-start.5 = ((bf16[8,112,128]{2,1,0:T(8,128)(2,1)}), bf16[8,112,128]{2,1,0:T(8,128)(2,1)S(1)}, u32[]{:S(2)}, u32[]{:S(2)}) async-start(bf16[8,112,128]{2,1,0:T(8,128)(2,1)} %sum_small.1), calls=%async_computation.5 | async-start | bytes 458752 | tf_op jit(solution)/shard_map/all_to_all | solution.py:59
  306.4 3.5 %fusion.43.refs_1_ = bf16[1024,256]{1,0:T(8,128)(2,1)} fusion(f32[1024,256]{1,0:T(8,128)S(1)} %copy-done.8, bf16[1024,1024]{1,0:T(8,128)(2,1)} %copy-done.21, bf16[1024,256]{1,0:T(8,128)(2,1)} %collective-permute-done.35, bf16[1024,256]{1,0:T(8,128)(2,1)} %collective-permute-done.33, f32[256]{0:T(256)S(1)} %copy-done.77, bf16[1024,1024]{1,0:T(8,128)(2,1)} %param.39, ...), kind=kOutput, calls=%fused_computation.53 | convolution fusion | flops 538705920 | bytes 5243908 | tf_op jit(solution)/shard_map/dot_general | solution.py:443
  312.0 2.3 all-to-all-done.5.refs_2_.refs_0_
  315.0 2.2 beside.1
  317.3 4.5 %all-to-all-start.6 = ((bf16[8,128,512]{2,1,0:T(8,128)(2,1)}), bf16[8,128,512]{2,1,0:T(8,128)(2,1)S(1)}, u32[]{:S(2)}, u32[]{:S(2)}) async-start(bf16[8,128,512]{2,1,0:T(8,128)(2,1)} %bitcast.62), calls=%async_computation.6 | async-start | bytes 2097152 | tf_op jit(solution)/shard_map/all_to_all | solution.py:867
  323.0 4.1 %finish.4 = f32[1024,1024]{1,0:T(8,128)} custom-call(s32[4]{0:T(128)} %add_add_fusion.6.scalars, bf16[256,1024]{1,0:T(8,128)(2,1)} %get-tuple-element.77.refs_0_, bf16[256,1024]{1,0:T(8,128)(2,1)} %copy-done.14, bf16[256,1024]{1,0:T(8,128)(2,1)} %copy-done.15, bf16[256,1024]{1,0:T(8,128)(2,1)} %copy-done.16, bf16[256,1536]{1,0:T(8,128)(2,1)} %join_sum.1.refs_0_.refs_4_, ...), custom_call_target="tpu_custom_call" | custom-call | bytes 300000 | tf_op jit(solution)/shard_map/finish/pallas_call | solution.py:298
  327.1 3.4 finish.3
  330.5 4.3 %finish.5 = f32[1024,1024]{1,0:T(8,128)} custom-call(s32[4]{0:T(128)} %add_add_fusion.7.scalars, bf16[256,1024]{1,0:T(8,128)(2,1)} %get-tuple-element.77.refs_0_, bf16[256,1024]{1,0:T(8,128)(2,1)} %copy-done.14, bf16[256,1024]{1,0:T(8,128)(2,1)} %copy-done.15, bf16[256,1024]{1,0:T(8,128)(2,1)} %copy-done.16, bf16[256,1536]{1,0:T(8,128)(2,1)} %join_sum.1.refs_0_.refs_4_, ...), custom_call_target="tpu_custom_call" | custom-call | bytes 300000 | tf_op jit(solution)/shard_map/finish/pallas_call | solution.py:298
  338.5 6.8 %all-to-all-done.6 = bf16[8,128,512]{2,1,0:T(8,128)(2,1)S(1)} async-done(((bf16[8,128,512]{2,1,0:T(8,128)(2,1)}), bf16[8,128,512]{2,1,0:T(8,128)(2,1)S(1)}, u32[]{:S(2)}, u32[]{:S(2)}) %all-to-all-start.6) | async-done | bytes 1048608 | tf_op jit(solution)/shard_map/all_to_all | solution.py:867
  (306 shorter events, 67.7 us)
Async XLA Ops:
  0.7 90.1 %copy-start = (bf16[1024,1024]{1,0:T(8,128)(2,1)S(1)}, bf16[1024,1024]{1,0:T(8,128)(2,1)}, u32[]{:S(2)}) copy-start(bf16[1024,1024]{1,0:T(8,128)(2,1)} %param.37) | copy-start | bytes 6291460
  3.1 35.1 %all-to-all-start = ((bf16[8,128,512]{2,1,0:T(8,128)(2,1)}), bf16[8,128,512]{2,1,0:T(8,128)(2,1)S(1)}, u32[]{:S(2)}, u32[]{:S(2)}) async-start(bf16[8,128,512]{2,1,0:T(8,128)(2,1)} %pad_maximum_fusion), calls=%async_computation | async-start | bytes 2097152 | tf_op jit(solution)/shard_map/all_to_all | solution.py:867
  39.1 4.3 %collective-permute-start = (f32[2,1024]{1,0:T(2,128)S(1)}, f32[2,1024]{1,0:T(2,128)S(1)}, u32[]{:S(2)}, u32[]{:S(2)}) collective-permute-start(f32[2,1024]{1,0:T(2,128)S(1)} %pad_maximum_fusion.14), channel_id=1, source_target_pairs={{0,1},{1,0},{2,3},{3,2},{4,5},{5,4},{6,7},{7,6},{8,9},{9,8},{10,11... | collective-permute-start | bytes 24584 | tf_op jit(solution)/shard_map/ppermute | solution.py:18
  39.2 4.2 %collective-permute-start.1 = (f32[2,1024]{1,0:T(2,128)S(1)}, f32[2,1024]{1,0:T(2,128)S(1)}, u32[]{:S(2)}, u32[]{:S(2)}) collective-permute-start(f32[2,1024]{1,0:T(2,128)S(1)} %pad_maximum_fusion.14), channel_id=1, source_target_pairs={{0,2},{1,3},{2,0},{3,1},{4,6},{5,7},{6,4},{7,5},{8,10},{9,11},{10,... | collective-permute-start | bytes 24584 | tf_op jit(solution)/shard_map/ppermute | solution.py:18
  40.7 3.1 collective-permute-start.2
  41.7 23.6 %collective-permute-start.3 = (bf16[1024,256]{1,0:T(8,128)(2,1)S(1)}, bf16[1024,256]{1,0:T(8,128)(2,1)}, u32[]{:S(2)}, u32[]{:S(2)}) collective-permute-start(bf16[1024,256]{1,0:T(8,128)(2,1)S(1)} %slice.95), channel_id=1, source_target_pairs={{0,2},{1,3},{2,0},{3,1},{4,6},{5,7},{6,4},{7,5},{8,10},{9,11},{10,... | collective-permute-start | bytes 1572872 | tf_op jit(solution)/shard_map/ppermute | solution.py:18
  43.3 45.5 %collective-permute-start.10 = (bf16[1024,256]{1,0:T(8,128)(2,1)S(1)}, bf16[1024,256]{1,0:T(8,128)(2,1)}, u32[]{:S(2)}, u32[]{:S(2)}) collective-permute-start(bf16[1024,256]{1,0:T(8,128)(2,1)S(1)} %slice.95), channel_id=1, source_target_pairs={{0,1},{1,0},{2,3},{3,2},{4,5},{5,4},{6,7},{7,6},{8,9},{9,8},{10,11... | collective-permute-start | bytes 1572872 | tf_op jit(solution)/shard_map/ppermute | solution.py:18
  65.4 14.3 %collective-permute-start.5 = (bf16[1024,256]{1,0:T(8,128)(2,1)}, bf16[1024,256]{1,0:T(8,128)(2,1)S(1)}, u32[]{:S(2)}, u32[]{:S(2)}) collective-permute-start(bf16[1024,256]{1,0:T(8,128)(2,1)} %get-tuple-element.64), channel_id=1, source_target_pairs={{0,2},{1,3},{2,0},{3,1},{4,6},{5,7},{6,4},{7,5},{8,10},{9,11},{10,... | collective-permute-start | bytes 1572872 | tf_op jit(solution)/shard_map/ppermute | solution.py:18
  66.8 13.3 %collective-permute-start.4 = (bf16[1024,256]{1,0:T(8,128)(2,1)S(1)}, bf16[1024,256]{1,0:T(8,128)(2,1)S(1)}, u32[]{:S(2)}, u32[]{:S(2)}) collective-permute-start(bf16[1024,256]{1,0:T(8,128)(2,1)S(1)} %copy-done.47), channel_id=1, source_target_pairs={{0,1},{1,0},{2,3},{3,2},{4,5},{5,4},{6,7},{7,6},{8,9},{9,8},{10,11... | collective-permute-start | bytes 1572872 | tf_op jit(solution)/shard_map/ppermute | solution.py:18
  79.6 1.9 collective-permute-start.6
  83.0 4.2 %collective-permute-start.7 = (f32[2,1024]{1,0:T(2,128)S(1)}, f32[2,1024]{1,0:T(2,128)S(1)}, u32[]{:S(2)}, u32[]{:S(2)}) collective-permute-start(f32[2,1024]{1,0:T(2,128)S(1)} %pad_maximum_fusion.15), channel_id=1, source_target_pairs={{0,1},{1,0},{2,3},{3,2},{4,5},{5,4},{6,7},{7,6},{8,9},{9,8},{10,11... | collective-permute-start | bytes 24584 | tf_op jit(solution)/shard_map/ppermute | solution.py:18
  83.2 4.0 %collective-permute-start.8 = (f32[2,1024]{1,0:T(2,128)S(1)}, f32[2,1024]{1,0:T(2,128)S(1)}, u32[]{:S(2)}, u32[]{:S(2)}) collective-permute-start(f32[2,1024]{1,0:T(2,128)S(1)} %pad_maximum_fusion.15), channel_id=1, source_target_pairs={{0,2},{1,3},{2,0},{3,1},{4,6},{5,7},{6,4},{7,5},{8,10},{9,11},{10,... | collective-permute-start | bytes 24584 | tf_op jit(solution)/shard_map/ppermute | solution.py:18
  83.8 3.5 %collective-permute-start.9 = (f32[2,1024]{1,0:T(2,128)S(1)}, f32[2,1024]{1,0:T(2,128)S(1)}, u32[]{:S(2)}, u32[]{:S(2)}) collective-permute-start(f32[2,1024]{1,0:T(2,128)S(1)} %pad_maximum_fusion.15), channel_id=1, source_target_pairs={{0,3},{1,2},{2,1},{3,0},{4,7},{5,6},{6,5},{7,4},{8,11},{9,10},{10,... | collective-permute-start | bytes 24584 | tf_op jit(solution)/shard_map/ppermute | solution.py:18
  86.7 20.1 %collective-permute-start.11 = (bf16[1024,256]{1,0:T(8,128)(2,1)}, bf16[1024,256]{1,0:T(8,128)(2,1)}, u32[]{:S(2)}, u32[]{:S(2)}) collective-permute-start(bf16[1024,256]{1,0:T(8,128)(2,1)} %collective-permute-done.3), channel_id=1, source_target_pairs={{0,1},{1,0},{2,3},{3,2},{4,5},{5,4},{6,7},{7,6},{8,9},{9,8},{10,11... | collective-permute-start | bytes 1572872 | tf_op jit(solution)/shard_map/ppermute | solution.py:18
  87.7 14.0 %collective-permute-start.13 = (bf16[1024,256]{1,0:T(8,128)(2,1)S(1)}, bf16[1024,256]{1,0:T(8,128)(2,1)S(1)}, u32[]{:S(2)}, u32[]{:S(2)}) collective-permute-start(bf16[1024,256]{1,0:T(8,128)(2,1)S(1)} %add_convert_fusion), channel_id=1, source_target_pairs={{0,2},{1,3},{2,0},{3,1},{4,6},{5,7},{6,4},{7,5},{8,10},{9,11},{10,... | collective-permute-start | bytes 1572872 | tf_op jit(solution)/shard_map/ppermute | solution.py:18
  90.6 11.8 %collective-permute-start.12 = (bf16[1024,256]{1,0:T(8,128)(2,1)S(1)}, bf16[1024,256]{1,0:T(8,128)(2,1)S(1)}, u32[]{:S(2)}, u32[]{:S(2)}) collective-permute-start(bf16[1024,256]{1,0:T(8,128)(2,1)S(1)} %add_convert_fusion), channel_id=1, source_target_pairs={{0,1},{1,0},{2,3},{3,2},{4,5},{5,4},{6,7},{7,6},{8,9},{9,8},{10,11... | collective-permute-start | bytes 1572872 | tf_op jit(solution)/shard_map/ppermute | solution.py:18
  101.7 1.9 collective-permute-start.14
  119.5 30.3 %all-to-all-start.1 = ((bf16[4,256,1024]{2,1,0:T(8,128)(2,1)}), bf16[4,256,1024]{2,1,0:T(8,128)(2,1)}, u32[]{:S(2)}, u32[]{:S(2)}) async-start(bf16[4,256,1024]{2,1,0:T(8,128)(2,1)} %bitcast.64), calls=%async_computation.1 | async-start | bytes 4194304 | tf_op jit(solution)/shard_map/all_to_all | solution.py:161
  126.5 2.0 collective-permute-start.16
  127.4 3.0 collective-permute-start.15
  129.3 14.0 %collective-permute-start.17 = (bf16[1024,256]{1,0:T(8,128)(2,1)S(1)}, bf16[1024,256]{1,0:T(8,128)(2,1)S(1)}, u32[]{:S(2)}, u32[]{:S(2)}) collective-permute-start(bf16[1024,256]{1,0:T(8,128)(2,1)S(1)} %convert_add_fusion.6), channel_id=1, source_target_pairs={{0,2},{1,3},{2,0},{3,1},{4,6},{5,7},{6,4},{7,5},{8,10},{9,11},{10,... | collective-permute-start | bytes 1572872 | tf_op jit(solution)/shard_map/ppermute | solution.py:18
  149.8 31.4 %all-to-all-start.2 = ((bf16[4,256,1024]{2,1,0:T(8,128)(2,1)}), bf16[4,256,1024]{2,1,0:T(8,128)(2,1)}, u32[]{:S(2)}, u32[]{:S(2)}) async-start(bf16[4,256,1024]{2,1,0:T(8,128)(2,1)} %bitcast.63), calls=%async_computation.2 | async-start | bytes 4194304 | tf_op jit(solution)/shard_map/all_to_all | solution.py:161
  154.4 1.9 collective-permute-start.18
  154.4 3.9 %collective-permute-start.19 = (f32[2,1024]{1,0:T(2,128)}, f32[2,1024]{1,0:T(2,128)S(1)}, u32[]{:S(2)}, u32[]{:S(2)}) collective-permute-start(f32[2,1024]{1,0:T(2,128)} %pad_maximum_fusion.16), channel_id=1, source_target_pairs={{0,2},{1,3},{2,0},{3,1},{4,6},{5,7},{6,4},{7,5},{8,10},{9,11},{10,... | collective-permute-start | bytes 24584 | tf_op jit(solution)/shard_map/ppermute | solution.py:18
  155.6 3.3 collective-permute-start.20
  164.1 2.2 collective-permute-start.22
  165.2 5.4 %collective-permute-start.21 = (bf16[1024,256]{1,0:T(8,128)(2,1)S(1)}, bf16[1024,256]{1,0:T(8,128)(2,1)S(1)}, u32[]{:S(2)}, u32[]{:S(2)}) collective-permute-start(bf16[1024,256]{1,0:T(8,128)(2,1)S(1)} %convolution_convert_fusion.1), channel_id=1, source_target_pairs={{0,1},{1,0},{2,3},{3,2},{4,5},{5,4},{6,7},{7,6},{8,9},{9,8},{10,11... | collective-permute-start | bytes 1572872 | tf_op jit(solution)/shard_map/ppermute | solution.py:18
  166.8 14.3 %collective-permute-start.23 = (bf16[1024,256]{1,0:T(8,128)(2,1)S(1)}, bf16[1024,256]{1,0:T(8,128)(2,1)S(1)}, u32[]{:S(2)}, u32[]{:S(2)}) collective-permute-start(bf16[1024,256]{1,0:T(8,128)(2,1)S(1)} %fusion.96), channel_id=1, source_target_pairs={{0,2},{1,3},{2,0},{3,1},{4,6},{5,7},{6,4},{7,5},{8,10},{9,11},{10,... | collective-permute-start | bytes 1572872 | tf_op jit(solution)/shard_map/ppermute | solution.py:18
  181.2 30.6 %all-to-all-start.3 = ((bf16[4,256,512]{2,1,0:T(8,128)(2,1)}), bf16[4,256,512]{2,1,0:T(8,128)(2,1)S(1)}, u32[]{:S(2)}, u32[]{:S(2)}) async-start(bf16[4,256,512]{2,1,0:T(8,128)(2,1)} %bitcast.65), calls=%async_computation.3 | async-start | bytes 2097152 | tf_op jit(solution)/shard_map/all_to_all | solution.py:161
  191.6 25.5 %collective-permute-start.24 = (bf16[256,1024]{1,0:T(8,128)(2,1)}, bf16[256,1024]{1,0:T(8,128)(2,1)S(1)}, u32[]{:S(2)}, u32[]{:S(2)}) collective-permute-start(bf16[256,1024]{1,0:T(8,128)(2,1)} %get-tuple-element.74.refs_1_), channel_id=1, source_target_pairs={{0,16},{4,20},{8,24},{12,28},{16,0},{20,4},{24,8},{28,12},{1,17},{... | collective-permute-start | bytes 1572872 | tf_op jit(solution)/shard_map/ppermute | solution.py:18
  221.5 3.8 %collective-permute-start.25 = (f32[2,1024]{1,0:T(2,128)S(1)}, f32[2,1024]{1,0:T(2,128)S(1)}, u32[]{:S(2)}, u32[]{:S(2)}) collective-permute-start(f32[2,1024]{1,0:T(2,128)S(1)} %pad_maximum_fusion.17), channel_id=1, source_target_pairs={{0,1},{1,0},{2,3},{3,2},{4,5},{5,4},{6,7},{7,6},{8,9},{9,8},{10,11... | collective-permute-start | bytes 24584 | tf_op jit(solution)/shard_map/ppermute | solution.py:18
  221.6 7.9 %collective-permute-start.26 = (f32[2,1024]{1,0:T(2,128)S(1)}, f32[2,1024]{1,0:T(2,128)S(1)}, u32[]{:S(2)}, u32[]{:S(2)}) collective-permute-start(f32[2,1024]{1,0:T(2,128)S(1)} %pad_maximum_fusion.17), channel_id=1, source_target_pairs={{0,2},{1,3},{2,0},{3,1},{4,6},{5,7},{6,4},{7,5},{8,10},{9,11},{10,... | collective-permute-start | bytes 24584 | tf_op jit(solution)/shard_map/ppermute | solution.py:18
  222.5 7.0 %collective-permute-start.27 = (f32[2,1024]{1,0:T(2,128)S(1)}, f32[2,1024]{1,0:T(2,128)S(1)}, u32[]{:S(2)}, u32[]{:S(2)}) collective-permute-start(f32[2,1024]{1,0:T(2,128)S(1)} %pad_maximum_fusion.17), channel_id=1, source_target_pairs={{0,3},{1,2},{2,1},{3,0},{4,7},{5,6},{6,5},{7,4},{8,11},{9,10},{10,... | collective-permute-start | bytes 24584 | tf_op jit(solution)/shard_map/ppermute | solution.py:18
  223.4 40.1 %collective-permute-start.28 = (bf16[256,1024]{1,0:T(8,128)(2,1)S(1)}, bf16[256,1024]{1,0:T(8,128)(2,1)S(1)}, u32[]{:S(2)}, u32[]{:S(2)}) collective-permute-start(bf16[256,1024]{1,0:T(8,128)(2,1)S(1)} %copy-done.23), channel_id=1, source_target_pairs={{0,16},{4,20},{8,24},{12,28},{16,0},{20,4},{24,8},{28,12},{1,17},{... | collective-permute-start | bytes 1572872 | tf_op jit(solution)/shard_map/ppermute | solution.py:18
  223.4 40.1 %collective-permute-start.30 = (bf16[256,1024]{1,0:T(8,128)(2,1)S(1)}, bf16[256,1024]{1,0:T(8,128)(2,1)S(1)}, u32[]{:S(2)}, u32[]{:S(2)}) collective-permute-start(bf16[256,1024]{1,0:T(8,128)(2,1)S(1)} %copy-done.23), channel_id=1, source_target_pairs={{0,4},{4,0},{8,12},{12,8},{16,20},{20,16},{24,28},{28,24},{1,5},{5... | collective-permute-start | bytes 1572872 | tf_op jit(solution)/shard_map/ppermute | solution.py:18
  225.3 38.2 %collective-permute-start.31 = (bf16[256,1024]{1,0:T(8,128)(2,1)S(1)}, bf16[256,1024]{1,0:T(8,128)(2,1)S(1)}, u32[]{:S(2)}, u32[]{:S(2)}) collective-permute-start(bf16[256,1024]{1,0:T(8,128)(2,1)S(1)} %copy-done.23), channel_id=1, source_target_pairs={{0,8},{4,12},{8,0},{12,4},{16,24},{20,28},{24,16},{28,20},{1,9},{5... | collective-permute-start | bytes 1572872 | tf_op jit(solution)/shard_map/ppermute | solution.py:18
  229.5 39.0 %collective-permute-start.32 = (bf16[256,1024]{1,0:T(8,128)(2,1)S(1)}, bf16[256,1024]{1,0:T(8,128)(2,1)S(1)}, u32[]{:S(2)}, u32[]{:S(2)}) collective-permute-start(bf16[256,1024]{1,0:T(8,128)(2,1)S(1)} %copy-done.23), channel_id=1, source_target_pairs={{0,12},{4,8},{8,4},{12,0},{16,28},{20,24},{24,20},{28,16},{1,13},{... | collective-permute-start | bytes 1572872 | tf_op jit(solution)/shard_map/ppermute | solution.py:18
  229.6 34.0 %collective-permute-start.29 = (bf16[256,512]{1,0:T(8,128)(2,1)S(1)}, bf16[256,512]{1,0:T(8,128)(2,1)S(1)}, u32[]{:S(2)}, u32[]{:S(2)}) collective-permute-start(bf16[256,512]{1,0:T(8,128)(2,1)S(1)} %copy-done.54), channel_id=1, source_target_pairs={{0,16},{4,20},{8,24},{12,28},{16,0},{20,4},{24,8},{28,12},{1,17},{... | collective-permute-start | bytes 786440 | tf_op jit(solution)/shard_map/ppermute | solution.py:18
  273.4 4.3 %collective-permute-start.34 = (bf16[1024,256]{1,0:T(8,128)(2,1)S(1)}, bf16[1024,256]{1,0:T(8,128)(2,1)S(1)}, u32[]{:S(2)}, u32[]{:S(2)}) collective-permute-start(bf16[1024,256]{1,0:T(8,128)(2,1)S(1)} %convolution_convert_fusion.2), channel_id=1, source_target_pairs={{0,1},{1,0},{2,3},{3,2},{4,5},{5,4},{6,7},{7,6},{8,9},{9,8},{10,11... | collective-permute-start | bytes 1572872 | tf_op jit(solution)/shard_map/ppermute | solution.py:18
  273.5 22.5 %collective-permute-start.37 = (bf16[256,1536]{1,0:T(8,128)(2,1)}, bf16[256,1536]{1,0:T(8,128)(2,1)S(1)}, u32[]{:S(2)}, u32[]{:S(2)}) collective-permute-start(bf16[256,1536]{1,0:T(8,128)(2,1)} %join_sum.1.refs_0_.refs_4_), channel_id=1, source_target_pairs={{0,8},{4,12},{8,0},{12,4},{16,24},{20,28},{24,16},{28,20},{1,9},{5... | collective-permute-start | bytes 2359304 | tf_op jit(solution)/shard_map/ppermute | solution.py:18
  274.7 22.7 %collective-permute-start.36 = (bf16[256,1536]{1,0:T(8,128)(2,1)}, bf16[256,1536]{1,0:T(8,128)(2,1)S(1)}, u32[]{:S(2)}, u32[]{:S(2)}) collective-permute-start(bf16[256,1536]{1,0:T(8,128)(2,1)} %join_sum.1.refs_0_.refs_4_), channel_id=1, source_target_pairs={{0,4},{4,0},{8,12},{12,8},{16,20},{20,16},{24,28},{28,24},{1,5},{5... | collective-permute-start | bytes 2359304 | tf_op jit(solution)/shard_map/ppermute | solution.py:18
  277.6 28.7 %collective-permute-start.33 = (bf16[1024,256]{1,0:T(8,128)(2,1)}, bf16[1024,256]{1,0:T(8,128)(2,1)}, u32[]{:S(2)}, u32[]{:S(2)}) collective-permute-start(bf16[1024,256]{1,0:T(8,128)(2,1)} %convolution_convert_fusion.3), channel_id=1, source_target_pairs={{0,1},{1,0},{2,3},{3,2},{4,5},{5,4},{6,7},{7,6},{8,9},{9,8},{10,11... | collective-permute-start | bytes 1572872 | tf_op jit(solution)/shard_map/ppermute | solution.py:18
  279.2 27.2 %collective-permute-start.35 = (bf16[1024,256]{1,0:T(8,128)(2,1)}, bf16[1024,256]{1,0:T(8,128)(2,1)}, u32[]{:S(2)}, u32[]{:S(2)}) collective-permute-start(bf16[1024,256]{1,0:T(8,128)(2,1)} %fusion.44), channel_id=1, source_target_pairs={{0,2},{1,3},{2,0},{3,1},{4,6},{5,7},{6,4},{7,5},{8,10},{9,11},{10,... | collective-permute-start | bytes 1572872 | tf_op jit(solution)/shard_map/ppermute | solution.py:18
  280.1 18.4 %all-to-all-start.4 = ((bf16[8,112,128]{2,1,0:T(8,128)(2,1)}), bf16[8,112,128]{2,1,0:T(8,128)(2,1)S(1)}, u32[]{:S(2)}, u32[]{:S(2)}) async-start(bf16[8,112,128]{2,1,0:T(8,128)(2,1)} %pack_small.1.refs_0_), calls=%async_computation.4 | async-start | bytes 458752 | tf_op jit(solution)/shard_map/all_to_all | solution.py:59
  296.8 13.1 %collective-permute-start.38 = (bf16[128,1536]{1,0:T(8,128)(2,1)}, bf16[128,1536]{1,0:T(8,128)(2,1)}, u32[]{:S(2)}, u32[]{:S(2)}) collective-permute-start(bf16[128,1536]{1,0:T(8,128)(2,1)} %slice.134), channel_id=1, source_target_pairs={{0,4},{4,0},{8,12},{12,8},{16,20},{20,16},{24,28},{28,24},{1,5},{5... | collective-permute-start | bytes 1179656 | tf_op jit(solution)/shard_map/ppermute | solution.py:18
  298.2 12.8 %collective-permute-start.39 = (bf16[128,1536]{1,0:T(8,128)(2,1)}, bf16[128,1536]{1,0:T(8,128)(2,1)}, u32[]{:S(2)}, u32[]{:S(2)}) collective-permute-start(bf16[128,1536]{1,0:T(8,128)(2,1)} %slice.135), channel_id=1, source_target_pairs={{0,8},{4,12},{8,0},{12,4},{16,24},{20,28},{24,16},{28,20},{1,9},{5... | collective-permute-start | bytes 1179656 | tf_op jit(solution)/shard_map/ppermute | solution.py:18
  300.9 13.5 %all-to-all-start.5 = ((bf16[8,112,128]{2,1,0:T(8,128)(2,1)}), bf16[8,112,128]{2,1,0:T(8,128)(2,1)S(1)}, u32[]{:S(2)}, u32[]{:S(2)}) async-start(bf16[8,112,128]{2,1,0:T(8,128)(2,1)} %sum_small.1), calls=%async_computation.5 | async-start | bytes 458752 | tf_op jit(solution)/shard_map/all_to_all | solution.py:59
  317.3 28.0 %all-to-all-start.6 = ((bf16[8,128,512]{2,1,0:T(8,128)(2,1)}), bf16[8,128,512]{2,1,0:T(8,128)(2,1)S(1)}, u32[]{:S(2)}, u32[]{:S(2)}) async-start(bf16[8,128,512]{2,1,0:T(8,128)(2,1)} %bitcast.62), calls=%async_computation.6 | async-start | bytes 2097152 | tf_op jit(solution)/shard_map/all_to_all | solution.py:867
  (79 other events, 447.0 us)

commit v4 on v3

--- a/solution.py
+++ b/solution.py
@@ -171,15 +171,13 @@
     def accept(self, task, outs):
         if task == "deal":
             self.parts = [outs[0], swap(outs[1], "seq", self.masks[0])]
-        elif task == "whole":
-            self.parts = [outs[0], swap(outs[0], "seq", self.masks[0])]
-        else:
-            total = outs[0]
-            for mask in self.masks[1:]:
-                total = (total.astype(FULL) + swap(total, "seq", mask).astype(FULL)).astype(LOW)
-            self.parts = [total]
-            if self.halves:
-                self.parts.append(swap(total, "seq", self.masks[0]))
+            return
+        total = outs[0]
+        for mask in self.masks[1:]:
+            total = (total.astype(FULL) + swap(total, "seq", mask).astype(FULL)).astype(LOW)
+        self.parts = [total]
+        if task == "whole" or self.halves:
+            self.parts.append(swap(total, "seq", self.masks[0]))
 
 
 def gather(part):
@@ -857,7 +855,7 @@
     assert seqs % batch == 0
     runs = seqs // batch
     total_width = width * chans
-    assert chans == 4
+    assert chans == 4 and batch == 8 and block == 2 * a_decay.shape[0]
     seq_me = lax.axis_index("seq")
     chan_me = lax.axis_index("chan")
     groups = None if runs == 1 else [[r * batch + j for j in range(batch)] for r in range(runs)]
@@ -897,7 +895,7 @@
         end = add(cmul(carry, split(s[:, -1])), cmul(const_factor(BBAR), split(p[:, -1])))
         ends = lax.all_gather(pair(*end), "seq", axis_index_groups=peers)
         hop = carry
-        for _ in range(3):
+        for _ in range(batch.bit_length() - 1):
             hop = cmul(hop, hop)
         for r in range(runs - 1):
             moved = add(cmul(hop, split(init)), split(ends[r]))

time: 354 us -> 354 us (level)
  no operation moved by 1% of the time
where the time goes in v4:
time: 354 us; the launch traced here: 347 us
  Pallas kernels  115 us (32%)
  waiting for transfers between devices  85 us (24%)
  starting transfers between devices  63.6 us (18%)
  matrix products  45.1 us (13%)
  other arithmetic  21 us (6%)
  local copies, waits for them, and re-layouts  15.1 us (4%)
    ppermute x40, waiting for transfers between devices, swap(): lax.ppermute(x, axis, [(i, i ^ distance) for i in range(lax.axis_size(axi...  71.7 us
    ppermute x40, starting transfers between devices, swap(): lax.ppermute(x, axis, [(i, i ^ distance) for i in range(lax.axis_size(axi...  29.7 us
    pallas_call x1, Pallas kernels, s4_sums(): pl.pallas_call(lambda *refs: sums_kernel(block, *refs), grid=(steps,), in...  25.4 us
    pallas_call x1, Pallas kernels, s4_tables(): pl.pallas_call(tables_kernel, grid=(steps,), in_specs=[pl.BlockSpec((8, C...  20 us
    pallas_call x1, Pallas kernels, s4_forward(): pl.pallas_call(forward_kernel, grid=(width // CHANNELS,), in_specs=[whole...  18.8 us
    dot_general x12, matrix products, dot_t(): lax.dot_general(a, b, (((1,), (1,)), ((), ())), preferred_element_type=FULL)  18.4 us
    pallas_call x1, Pallas kernels, s4_backward(): pl.pallas_call(backward_kernel, grid=(width // CHANNELS,), in_specs=[whol...  17.6 us
    dot_general x12, matrix products, dot(): lax.dot_general(a, b, (((1,), (0,)), ((), ())), preferred_element_type=FULL)  15.6 us
  transfers between devices with their start and end apart: 47, of which 19 were waited for; matrix products, arithmetic and copies ran while one was open for 16% of the time, Pallas kernels for 31%

profile of v4, /device:TPU:0, one launch (start us, length us, event | category | flops | bytes accessed | tf_op | source)
XLA Modules:
  0.0 346.7 jit_solution(449571684828399462)
XLA Ops:
  0.7 2.4 pad_maximum_fusion
  3.1 7.3 %all-to-all-start = ((bf16[8,128,512]{2,1,0:T(8,128)(2,1)}), bf16[8,128,512]{2,1,0:T(8,128)(2,1)S(1)}, u32[]{:S(2)}, u32[]{:S(2)}) async-start(bf16[8,128,512]{2,1,0:T(8,128)(2,1)} %pad_maximum_fusion), calls=%async_computation | async-start | bytes 2097152 | tf_op jit(solution)/shard_map/all_to_all | solution.py:865
  10.9 5.1 %s4_consts.1 = (f32[30,256,128]{2,1,0:T(8,128)}, f32[8,256,128]{2,1,0:T(8,128)}) custom-call(f32[64,256]{1,0:T(8,128)} %refs_0_.1, f32[64,256]{1,0:T(8,128)} %refs_1_.1, f32[2,64,256]{2,1,0:T(8,128)} %refs_2_.1, f32[2,64,256]{2,1,0:T(8,128)} %refs_3_.1, f32[1,256]{1,0:T(1,128)} %bitcast.101), custom_call_target="tpu_custom_call" | custom-call | bytes 600000 | tf_op jit(solution)/shard_map/s4_consts/pallas_call | solution.py:419
  16.1 20.0 %s4_tables.1 = (bf16[256,256,128]{2,1,0:T(8,128)(2,1)}, bf16[256,128,128]{2,1,0:T(8,128)(2,1)}) custom-call(f32[8,256,128]{2,1,0:T(8,128)} %get-tuple-element.58.base, f32[30,256,128]{2,1,0:T(8,128)} %get-tuple-element.59.consts.refs_9_), custom_call_target="tpu_custom_call" | custom-call | bytes 2400000 | tf_op jit(solution)/shard_map/s4_tables/pallas_call | solution.py:487
  36.1 2.1 constant_dynamic-slice_fusion
  43.9 1.9 fusion.56.signal
  46.5 18.8 %s4_forward.1 = (bf16[1024,256]{1,0:T(8,128)(2,1)}, f32[1024,256]{1,0:T(8,128)}, f32[256,8,128]{2,1,0:T(8,128)}, f32[256,8,128]{2,1,0:T(8,128)}, f32[256,8,128]{2,1,0:T(8,128)}, /*index=5*/f32[256,8,128]{2,1,0:T(8,128)}) custom-call(bf16[1024,256]{1,0:T(8,128)(2,1)} %fusion.56.signal, f32[1,256]{1,0:T(1,128)} %bitcast.100, ...), custom_call_target="tpu_custom_call" | custom-call | bytes 1800000 | tf_op jit(solution)/shard_map/s4_forward/pallas_call | solution.py:602
  67.3 12.3 %collective-permute-done.5 = bf16[1024,256]{1,0:T(8,128)(2,1)S(1)} collective-permute-done((bf16[1024,256]{1,0:T(8,128)(2,1)}, bf16[1024,256]{1,0:T(8,128)(2,1)S(1)}, u32[]{:S(2)}, u32[]{:S(2)}) %collective-permute-start.5) | collective-permute-done | bytes 524320 | tf_op jit(solution)/shard_map/ppermute | solution.py:18
  88.8 1.8 fusion.91
  91.5 10.2 %collective-permute-done.13 = bf16[1024,256]{1,0:T(8,128)(2,1)S(1)} collective-permute-done((bf16[1024,256]{1,0:T(8,128)(2,1)S(1)}, bf16[1024,256]{1,0:T(8,128)(2,1)S(1)}, u32[]{:S(2)}, u32[]{:S(2)}) %collective-permute-start.13) | collective-permute-done | bytes 524320 | tf_op jit(solution)/shard_map/ppermute | solution.py:18
  103.6 3.2 multiply_convert_fusion
  106.9 7.5 %convert_reduce_fusion = (f32[1024]{0:T(1024)}, bf16[1024,1024]{1,0:T(8,128)(2,1)}) fusion(f32[1024,1024]{1,0:T(8,128)S(1)} %get-tuple-element.146, bf16[1024,256]{1,0:T(8,128)(2,1)} %collective-permute-done.11, bf16[1024,1024]{1,0:T(8,128)(2,1)} %param.39, s32[]{:T(128)S(6)} %select_n.63, f32[1024,1024]{1,0:T(8,128)S(1)} %fusion.88, ...), kind=kOutput, calls=%fused_computation.9 | convolution fusion | flops 563084288 | bytes 19927044 | tf_op jit(solution)/shard_map/dot_general | solution.py:445
  114.4 5.1 %fusion.34 = bf16[1024,1024]{1,0:T(8,128)(2,1)} fusion(bf16[1024,1024]{1,0:T(8,128)(2,1)S(1)} %get-tuple-element.88, bf16[1024,256]{1,0:T(8,128)(2,1)} %collective-permute-done.11, bf16[1024,256]{1,0:T(8,128)(2,1)} %collective-permute-done.3, bf16[1024,256]{1,0:T(8,128)(2,1)} %collective-permute-done.10, bf16[1024,256]{1,0:T(8,128)(2,1)S(1)} %slice.95), kind=kOutput, calls=%fused_computation.38 | convolution fusion | flops 2156920832 | bytes 6291456 | tf_op jit(solution)/shard_map/dot_general | solution.py:806
  119.5 4.5 %all-to-all-start.1 = ((bf16[4,256,1024]{2,1,0:T(8,128)(2,1)}), bf16[4,256,1024]{2,1,0:T(8,128)(2,1)}, u32[]{:S(2)}, u32[]{:S(2)}) async-start(bf16[4,256,1024]{2,1,0:T(8,128)(2,1)} %bitcast.64), calls=%async_computation.1 | async-start | bytes 4194304 | tf_op jit(solution)/shard_map/all_to_all | solution.py:161
  124.0 2.5 convolution_convert_fusion.4
  131.2 3.7 %fusion.31 = bf16[1024,1024]{1,0:T(8,128)(2,1)} fusion(bf16[1024,1024]{1,0:T(8,128)(2,1)S(1)} %copy-done.79, bf16[1024,256]{1,0:T(8,128)(2,1)S(1)} %copy-done.36, bf16[1024,256]{1,0:T(8,128)(2,1)S(1)} %copy-done.26, bf16[1024,256]{1,0:T(8,128)(2,1)S(1)} %copy-done.28, bf16[1024,256]{1,0:T(8,128)(2,1)S(1)} %copy-done.20), kind=kOutput, calls=%fused_computation.37 | convolution fusion | flops 2156920832 | bytes 6291456 | tf_op jit(solution)/shard_map/dot_general | solution.py:806
  134.9 8.3 %collective-permute-done.17 = bf16[1024,256]{1,0:T(8,128)(2,1)S(1)} collective-permute-done((bf16[1024,256]{1,0:T(8,128)(2,1)S(1)}, bf16[1024,256]{1,0:T(8,128)(2,1)S(1)}, u32[]{:S(2)}, u32[]{:S(2)}) %collective-permute-start.17) | collective-permute-done | bytes 524320 | tf_op jit(solution)/shard_map/ppermute | solution.py:18
  145.8 4.0 %all-to-all-done.1.refs_0_ = bf16[4,256,1024]{2,1,0:T(8,128)(2,1)} async-done(((bf16[4,256,1024]{2,1,0:T(8,128)(2,1)}), bf16[4,256,1024]{2,1,0:T(8,128)(2,1)}, u32[]{:S(2)}, u32[]{:S(2)}) %all-to-all-start.1) | async-done | bytes 2097184 | tf_op jit(solution)/shard_map/all_to_all | solution.py:161
  149.8 4.6 %all-to-all-start.2 = ((bf16[4,256,1024]{2,1,0:T(8,128)(2,1)}), bf16[4,256,1024]{2,1,0:T(8,128)(2,1)}, u32[]{:S(2)}, u32[]{:S(2)}) async-start(bf16[4,256,1024]{2,1,0:T(8,128)(2,1)} %bitcast.63), calls=%async_computation.2 | async-start | bytes 4194304 | tf_op jit(solution)/shard_map/all_to_all | solution.py:161
  156.3 2.1 collective-permute-done.19
  159.7 3.0 convert_reduce_fusion.3
  168.3 2.3 fusion.37
  170.6 10.5 %collective-permute-done.23 = bf16[1024,256]{1,0:T(8,128)(2,1)S(1)} collective-permute-done((bf16[1024,256]{1,0:T(8,128)(2,1)S(1)}, bf16[1024,256]{1,0:T(8,128)(2,1)S(1)}, u32[]{:S(2)}, u32[]{:S(2)}) %collective-permute-start.23) | collective-permute-done | bytes 524320 | tf_op jit(solution)/shard_map/ppermute | solution.py:18
  181.2 4.2 %all-to-all-start.3 = ((bf16[4,256,512]{2,1,0:T(8,128)(2,1)}), bf16[4,256,512]{2,1,0:T(8,128)(2,1)S(1)}, u32[]{:S(2)}, u32[]{:S(2)}) async-start(bf16[4,256,512]{2,1,0:T(8,128)(2,1)} %bitcast.65), calls=%async_computation.3 | async-start | bytes 2097152 | tf_op jit(solution)/shard_map/all_to_all | solution.py:161
  185.5 2.4 fusion.47
  187.9 3.6 %advance.2 = (bf16[256,1024]{1,0:T(8,128)(2,1)}, bf16[256,1024]{1,0:T(8,128)(2,1)}) custom-call(s32[1]{0:T(128)} %bitcast.16.high, bf16[4,256,1024]{2,1,0:T(8,128)(2,1)} %all-to-all-done.1.refs_0_, bf16[4,256,1024]{2,1,0:T(8,128)(2,1)} %all-to-all-done.2.refs_1_, bf16[1024,256]{1,0:T(8,128)(2,1)} %get-tuple-element.115.refs_2_.grads), custom_call_target="tpu_custom_call" | custom-call | bytes 200000 | tf_op jit(solution)/shard_map/advance/pallas_call | solution.py:250
  191.6 2.6 collective-permute-start.24
  194.2 17.6 %s4_backward.1 = (f32[1024,256]{1,0:T(8,128)}, f32[256,8,128]{2,1,0:T(8,128)}, f32[256,8,128]{2,1,0:T(8,128)}, f32[256,8,128]{2,1,0:T(8,128)}, f32[256,8,128]{2,1,0:T(8,128)}) custom-call(bf16[1024,256]{1,0:T(8,128)(2,1)} %get-tuple-element.115.refs_2_.grads, f32[30,256,128]{2,1,0:T(8,128)} %get-tuple-element.59.consts.refs_9_, ...), custom_call_target="tpu_custom_call" | custom-call | bytes 1800000 | tf_op jit(solution)/shard_map/s4_backward/pallas_call | solution.py:678
  211.9 5.2 %collective-permute-done.24.refs_1_ = bf16[256,1024]{1,0:T(8,128)(2,1)S(1)} collective-permute-done((bf16[256,1024]{1,0:T(8,128)(2,1)}, bf16[256,1024]{1,0:T(8,128)(2,1)S(1)}, u32[]{:S(2)}, u32[]{:S(2)}) %collective-permute-start.24) | collective-permute-done | bytes 524320 | tf_op jit(solution)/shard_map/ppermute | solution.py:18
  217.9 2.5 advance.3
  225.3 4.2 %collective-permute-start.31 = (bf16[256,1024]{1,0:T(8,128)(2,1)S(1)}, bf16[256,1024]{1,0:T(8,128)(2,1)S(1)}, u32[]{:S(2)}, u32[]{:S(2)}) collective-permute-start(bf16[256,1024]{1,0:T(8,128)(2,1)S(1)} %copy-done.23), channel_id=1, source_target_pairs={{0,8},{4,12},{8,0},{12,4},{16,24},{20,28},{24,16},{28,20},{1,9},{5... | collective-permute-start | bytes 1572872 | tf_op jit(solution)/shard_map/ppermute | solution.py:18
  232.2 25.4 %s4_sums.1.refs_0_ = f32[4,256,128]{2,1,0:T(8,128)} custom-call(f32[256,8,128]{2,1,0:T(8,128)} %get-tuple-element.80.refs_0_, f32[256,8,128]{2,1,0:T(8,128)} %get-tuple-element.81.refs_1_, f32[256,8,128]{2,1,0:T(8,128)} %get-tuple-element.82.refs_2_, f32[256,8,128]{2,1,0:T(8,128)} %get-tuple-element.83.refs_3_, f32[256,8,128]{2,1,0:T(8,128)} %get-tuple-element.84.refs_4_, ...), custom_call_target="tpu_custom_call" | custom-call | bytes 1800000 | tf_op jit(solution)/shard_map/s4_sums/pallas_call | solution.py:783
  259.3 1.9 pack_small.1.refs_0_
  261.2 2.3 collective-permute-done.29.received
  263.6 4.9 %collective-permute-done.32.refs_3_ = bf16[256,1024]{1,0:T(8,128)(2,1)S(1)} collective-permute-done((bf16[256,1024]{1,0:T(8,128)(2,1)S(1)}, bf16[256,1024]{1,0:T(8,128)(2,1)S(1)}, u32[]{:S(2)}, u32[]{:S(2)}) %collective-permute-start.32) | collective-permute-done | bytes 524320 | tf_op jit(solution)/shard_map/ppermute | solution.py:18
  269.3 2.2 join_sum.1.refs_0_.refs_4_
  271.5 1.9 convolution_convert_fusion.2
  280.1 3.4 all-to-all-start.4
  283.5 12.4 %collective-permute-done.37.refs_2_.refs_4_.refs_6_ = bf16[256,1536]{1,0:T(8,128)(2,1)S(1)} collective-permute-done((bf16[256,1536]{1,0:T(8,128)(2,1)}, bf16[256,1536]{1,0:T(8,128)(2,1)S(1)}, u32[]{:S(2)}, u32[]{:S(2)}) %collective-permute-start.37) | collective-permute-done | bytes 786464 | tf_op jit(solution)/shard_map/ppermute | solution.py:18
  300.9 5.5 %all-to-all-start.5 = ((bf16[8,112,128]{2,1,0:T(8,128)(2,1)}), bf16[8,112,128]{2,1,0:T(8,128)(2,1)S(1)}, u32[]{:S(2)}, u32[]{:S(2)}) async-start(bf16[8,112,128]{2,1,0:T(8,128)(2,1)} %sum_small.1), calls=%async_computation.5 | async-start | bytes 458752 | tf_op jit(solution)/shard_map/all_to_all | solution.py:59
  306.4 3.5 %fusion.43.refs_1_ = bf16[1024,256]{1,0:T(8,128)(2,1)} fusion(f32[1024,256]{1,0:T(8,128)S(1)} %copy-done.8, bf16[1024,1024]{1,0:T(8,128)(2,1)} %copy-done.21, bf16[1024,256]{1,0:T(8,128)(2,1)} %collective-permute-done.35, bf16[1024,256]{1,0:T(8,128)(2,1)} %collective-permute-done.33, f32[256]{0:T(256)S(1)} %copy-done.77, bf16[1024,1024]{1,0:T(8,128)(2,1)} %param.39, ...), kind=kOutput, calls=%fused_computation.53 | convolution fusion | flops 538705920 | bytes 5243908 | tf_op jit(solution)/shard_map/dot_general | solution.py:441
  312.0 2.3 all-to-all-done.5.refs_2_.refs_0_
  315.0 2.2 beside.1
  317.3 4.5 %all-to-all-start.6 = ((bf16[8,128,512]{2,1,0:T(8,128)(2,1)}), bf16[8,128,512]{2,1,0:T(8,128)(2,1)S(1)}, u32[]{:S(2)}, u32[]{:S(2)}) async-start(bf16[8,128,512]{2,1,0:T(8,128)(2,1)} %bitcast.62), calls=%async_computation.6 | async-start | bytes 2097152 | tf_op jit(solution)/shard_map/all_to_all | solution.py:865
  323.0 4.1 %finish.4 = f32[1024,1024]{1,0:T(8,128)} custom-call(s32[4]{0:T(128)} %add_add_fusion.6.scalars, bf16[256,1024]{1,0:T(8,128)(2,1)} %get-tuple-element.77.refs_0_, bf16[256,1024]{1,0:T(8,128)(2,1)} %copy-done.14, bf16[256,1024]{1,0:T(8,128)(2,1)} %copy-done.15, bf16[256,1024]{1,0:T(8,128)(2,1)} %copy-done.16, bf16[256,1536]{1,0:T(8,128)(2,1)} %join_sum.1.refs_0_.refs_4_, ...), custom_call_target="tpu_custom_call" | custom-call | bytes 300000 | tf_op jit(solution)/shard_map/finish/pallas_call | solution.py:296
  327.1 3.4 finish.3
  330.5 4.3 %finish.5 = f32[1024,1024]{1,0:T(8,128)} custom-call(s32[4]{0:T(128)} %add_add_fusion.7.scalars, bf16[256,1024]{1,0:T(8,128)(2,1)} %get-tuple-element.77.refs_0_, bf16[256,1024]{1,0:T(8,128)(2,1)} %copy-done.14, bf16[256,1024]{1,0:T(8,128)(2,1)} %copy-done.15, bf16[256,1024]{1,0:T(8,128)(2,1)} %copy-done.16, bf16[256,1536]{1,0:T(8,128)(2,1)} %join_sum.1.refs_0_.refs_4_, ...), custom_call_target="tpu_custom_call" | custom-call | bytes 300000 | tf_op jit(solution)/shard_map/finish/pallas_call | solution.py:296
  338.5 6.8 %all-to-all-done.6 = bf16[8,128,512]{2,1,0:T(8,128)(2,1)S(1)} async-done(((bf16[8,128,512]{2,1,0:T(8,128)(2,1)}), bf16[8,128,512]{2,1,0:T(8,128)(2,1)S(1)}, u32[]{:S(2)}, u32[]{:S(2)}) %all-to-all-start.6) | async-done | bytes 1048608 | tf_op jit(solution)/shard_map/all_to_all | solution.py:865
  (306 shorter events, 67.7 us)
Async XLA Ops:
  0.7 90.1 %copy-start = (bf16[1024,1024]{1,0:T(8,128)(2,1)S(1)}, bf16[1024,1024]{1,0:T(8,128)(2,1)}, u32[]{:S(2)}) copy-start(bf16[1024,1024]{1,0:T(8,128)(2,1)} %param.37) | copy-start | bytes 6291460
  3.1 35.1 %all-to-all-start = ((bf16[8,128,512]{2,1,0:T(8,128)(2,1)}), bf16[8,128,512]{2,1,0:T(8,128)(2,1)S(1)}, u32[]{:S(2)}, u32[]{:S(2)}) async-start(bf16[8,128,512]{2,1,0:T(8,128)(2,1)} %pad_maximum_fusion), calls=%async_computation | async-start | bytes 2097152 | tf_op jit(solution)/shard_map/all_to_all | solution.py:865
  39.1 4.3 %collective-permute-start = (f32[2,1024]{1,0:T(2,128)S(1)}, f32[2,1024]{1,0:T(2,128)S(1)}, u32[]{:S(2)}, u32[]{:S(2)}) collective-permute-start(f32[2,1024]{1,0:T(2,128)S(1)} %pad_maximum_fusion.14), channel_id=1, source_target_pairs={{0,1},{1,0},{2,3},{3,2},{4,5},{5,4},{6,7},{7,6},{8,9},{9,8},{10,11... | collective-permute-start | bytes 24584 | tf_op jit(solution)/shard_map/ppermute | solution.py:18
  39.2 4.2 %collective-permute-start.1 = (f32[2,1024]{1,0:T(2,128)S(1)}, f32[2,1024]{1,0:T(2,128)S(1)}, u32[]{:S(2)}, u32[]{:S(2)}) collective-permute-start(f32[2,1024]{1,0:T(2,128)S(1)} %pad_maximum_fusion.14), channel_id=1, source_target_pairs={{0,2},{1,3},{2,0},{3,1},{4,6},{5,7},{6,4},{7,5},{8,10},{9,11},{10,... | collective-permute-start | bytes 24584 | tf_op jit(solution)/shard_map/ppermute | solution.py:18
  40.7 3.1 collective-permute-start.2
  41.7 23.6 %collective-permute-start.3 = (bf16[1024,256]{1,0:T(8,128)(2,1)S(1)}, bf16[1024,256]{1,0:T(8,128)(2,1)}, u32[]{:S(2)}, u32[]{:S(2)}) collective-permute-start(bf16[1024,256]{1,0:T(8,128)(2,1)S(1)} %slice.95), channel_id=1, source_target_pairs={{0,2},{1,3},{2,0},{3,1},{4,6},{5,7},{6,4},{7,5},{8,10},{9,11},{10,... | collective-permute-start | bytes 1572872 | tf_op jit(solution)/shard_map/ppermute | solution.py:18
  43.3 45.5 %collective-permute-start.10 = (bf16[1024,256]{1,0:T(8,128)(2,1)S(1)}, bf16[1024,256]{1,0:T(8,128)(2,1)}, u32[]{:S(2)}, u32[]{:S(2)}) collective-permute-start(bf16[1024,256]{1,0:T(8,128)(2,1)S(1)} %slice.95), channel_id=1, source_target_pairs={{0,1},{1,0},{2,3},{3,2},{4,5},{5,4},{6,7},{7,6},{8,9},{9,8},{10,11... | collective-permute-start | bytes 1572872 | tf_op jit(solution)/shard_map/ppermute | solution.py:18
  65.4 14.3 %collective-permute-start.5 = (bf16[1024,256]{1,0:T(8,128)(2,1)}, bf16[1024,256]{1,0:T(8,128)(2,1)S(1)}, u32[]{:S(2)}, u32[]{:S(2)}) collective-permute-start(bf16[1024,256]{1,0:T(8,128)(2,1)} %get-tuple-element.64), channel_id=1, source_target_pairs={{0,2},{1,3},{2,0},{3,1},{4,6},{5,7},{6,4},{7,5},{8,10},{9,11},{10,... | collective-permute-start | bytes 1572872 | tf_op jit(solution)/shard_map/ppermute | solution.py:18
  66.8 13.3 %collective-permute-start.4 = (bf16[1024,256]{1,0:T(8,128)(2,1)S(1)}, bf16[1024,256]{1,0:T(8,128)(2,1)S(1)}, u32[]{:S(2)}, u32[]{:S(2)}) collective-permute-start(bf16[1024,256]{1,0:T(8,128)(2,1)S(1)} %copy-done.47), channel_id=1, source_target_pairs={{0,1},{1,0},{2,3},{3,2},{4,5},{5,4},{6,7},{7,6},{8,9},{9,8},{10,11... | collective-permute-start | bytes 1572872 | tf_op jit(solution)/shard_map/ppermute | solution.py:18
  79.6 1.9 collective-permute-start.6
  83.0 4.2 %collective-permute-start.7 = (f32[2,1024]{1,0:T(2,128)S(1)}, f32[2,1024]{1,0:T(2,128)S(1)}, u32[]{:S(2)}, u32[]{:S(2)}) collective-permute-start(f32[2,1024]{1,0:T(2,128)S(1)} %pad_maximum_fusion.15), channel_id=1, source_target_pairs={{0,1},{1,0},{2,3},{3,2},{4,5},{5,4},{6,7},{7,6},{8,9},{9,8},{10,11... | collective-permute-start | bytes 24584 | tf_op jit(solution)/shard_map/ppermute | solution.py:18
  83.2 4.0 %collective-permute-start.8 = (f32[2,1024]{1,0:T(2,128)S(1)}, f32[2,1024]{1,0:T(2,128)S(1)}, u32[]{:S(2)}, u32[]{:S(2)}) collective-permute-start(f32[2,1024]{1,0:T(2,128)S(1)} %pad_maximum_fusion.15), channel_id=1, source_target_pairs={{0,2},{1,3},{2,0},{3,1},{4,6},{5,7},{6,4},{7,5},{8,10},{9,11},{10,... | collective-permute-start | bytes 24584 | tf_op jit(solution)/shard_map/ppermute | solution.py:18
  83.8 3.5 %collective-permute-start.9 = (f32[2,1024]{1,0:T(2,128)S(1)}, f32[2,1024]{1,0:T(2,128)S(1)}, u32[]{:S(2)}, u32[]{:S(2)}) collective-permute-start(f32[2,1024]{1,0:T(2,128)S(1)} %pad_maximum_fusion.15), channel_id=1, source_target_pairs={{0,3},{1,2},{2,1},{3,0},{4,7},{5,6},{6,5},{7,4},{8,11},{9,10},{10,... | collective-permute-start | bytes 24584 | tf_op jit(solution)/shard_map/ppermute | solution.py:18
  86.7 20.1 %collective-permute-start.11 = (bf16[1024,256]{1,0:T(8,128)(2,1)}, bf16[1024,256]{1,0:T(8,128)(2,1)}, u32[]{:S(2)}, u32[]{:S(2)}) collective-permute-start(bf16[1024,256]{1,0:T(8,128)(2,1)} %collective-permute-done.3), channel_id=1, source_target_pairs={{0,1},{1,0},{2,3},{3,2},{4,5},{5,4},{6,7},{7,6},{8,9},{9,8},{10,11... | collective-permute-start | bytes 1572872 | tf_op jit(solution)/shard_map/ppermute | solution.py:18
  87.7 14.0 %collective-permute-start.13 = (bf16[1024,256]{1,0:T(8,128)(2,1)S(1)}, bf16[1024,256]{1,0:T(8,128)(2,1)S(1)}, u32[]{:S(2)}, u32[]{:S(2)}) collective-permute-start(bf16[1024,256]{1,0:T(8,128)(2,1)S(1)} %add_convert_fusion), channel_id=1, source_target_pairs={{0,2},{1,3},{2,0},{3,1},{4,6},{5,7},{6,4},{7,5},{8,10},{9,11},{10,... | collective-permute-start | bytes 1572872 | tf_op jit(solution)/shard_map/ppermute | solution.py:18
  90.6 11.8 %collective-permute-start.12 = (bf16[1024,256]{1,0:T(8,128)(2,1)S(1)}, bf16[1024,256]{1,0:T(8,128)(2,1)S(1)}, u32[]{:S(2)}, u32[]{:S(2)}) collective-permute-start(bf16[1024,256]{1,0:T(8,128)(2,1)S(1)} %add_convert_fusion), channel_id=1, source_target_pairs={{0,1},{1,0},{2,3},{3,2},{4,5},{5,4},{6,7},{7,6},{8,9},{9,8},{10,11... | collective-permute-start | bytes 1572872 | tf_op jit(solution)/shard_map/ppermute | solution.py:18
  101.7 1.9 collective-permute-start.14
  119.5 30.3 %all-to-all-start.1 = ((bf16[4,256,1024]{2,1,0:T(8,128)(2,1)}), bf16[4,256,1024]{2,1,0:T(8,128)(2,1)}, u32[]{:S(2)}, u32[]{:S(2)}) async-start(bf16[4,256,1024]{2,1,0:T(8,128)(2,1)} %bitcast.64), calls=%async_computation.1 | async-start | bytes 4194304 | tf_op jit(solution)/shard_map/all_to_all | solution.py:161
  126.5 2.0 collective-permute-start.16
  127.4 3.0 collective-permute-start.15
  129.3 14.0 %collective-permute-start.17 = (bf16[1024,256]{1,0:T(8,128)(2,1)S(1)}, bf16[1024,256]{1,0:T(8,128)(2,1)S(1)}, u32[]{:S(2)}, u32[]{:S(2)}) collective-permute-start(bf16[1024,256]{1,0:T(8,128)(2,1)S(1)} %convert_add_fusion.6), channel_id=1, source_target_pairs={{0,2},{1,3},{2,0},{3,1},{4,6},{5,7},{6,4},{7,5},{8,10},{9,11},{10,... | collective-permute-start | bytes 1572872 | tf_op jit(solution)/shard_map/ppermute | solution.py:18
  149.8 31.4 %all-to-all-start.2 = ((bf16[4,256,1024]{2,1,0:T(8,128)(2,1)}), bf16[4,256,1024]{2,1,0:T(8,128)(2,1)}, u32[]{:S(2)}, u32[]{:S(2)}) async-start(bf16[4,256,1024]{2,1,0:T(8,128)(2,1)} %bitcast.63), calls=%async_computation.2 | async-start | bytes 4194304 | tf_op jit(solution)/shard_map/all_to_all | solution.py:161
  154.4 1.9 collective-permute-start.18
  154.4 3.9 %collective-permute-start.19 = (f32[2,1024]{1,0:T(2,128)}, f32[2,1024]{1,0:T(2,128)S(1)}, u32[]{:S(2)}, u32[]{:S(2)}) collective-permute-start(f32[2,1024]{1,0:T(2,128)} %pad_maximum_fusion.16), channel_id=1, source_target_pairs={{0,2},{1,3},{2,0},{3,1},{4,6},{5,7},{6,4},{7,5},{8,10},{9,11},{10,... | collective-permute-start | bytes 24584 | tf_op jit(solution)/shard_map/ppermute | solution.py:18
  155.6 3.3 collective-permute-start.20
  164.1 2.2 collective-permute-start.22
  165.2 5.4 %collective-permute-start.21 = (bf16[1024,256]{1,0:T(8,128)(2,1)S(1)}, bf16[1024,256]{1,0:T(8,128)(2,1)S(1)}, u32[]{:S(2)}, u32[]{:S(2)}) collective-permute-start(bf16[1024,256]{1,0:T(8,128)(2,1)S(1)} %convolution_convert_fusion.1), channel_id=1, source_target_pairs={{0,1},{1,0},{2,3},{3,2},{4,5},{5,4},{6,7},{7,6},{8,9},{9,8},{10,11... | collective-permute-start | bytes 1572872 | tf_op jit(solution)/shard_map/ppermute | solution.py:18
  166.8 14.3 %collective-permute-start.23 = (bf16[1024,256]{1,0:T(8,128)(2,1)S(1)}, bf16[1024,256]{1,0:T(8,128)(2,1)S(1)}, u32[]{:S(2)}, u32[]{:S(2)}) collective-permute-start(bf16[1024,256]{1,0:T(8,128)(2,1)S(1)} %fusion.96), channel_id=1, source_target_pairs={{0,2},{1,3},{2,0},{3,1},{4,6},{5,7},{6,4},{7,5},{8,10},{9,11},{10,... | collective-permute-start | bytes 1572872 | tf_op jit(solution)/shard_map/ppermute | solution.py:18
  181.2 30.6 %all-to-all-start.3 = ((bf16[4,256,512]{2,1,0:T(8,128)(2,1)}), bf16[4,256,512]{2,1,0:T(8,128)(2,1)S(1)}, u32[]{:S(2)}, u32[]{:S(2)}) async-start(bf16[4,256,512]{2,1,0:T(8,128)(2,1)} %bitcast.65), calls=%async_computation.3 | async-start | bytes 2097152 | tf_op jit(solution)/shard_map/all_to_all | solution.py:161
  191.6 25.5 %collective-permute-start.24 = (bf16[256,1024]{1,0:T(8,128)(2,1)}, bf16[256,1024]{1,0:T(8,128)(2,1)S(1)}, u32[]{:S(2)}, u32[]{:S(2)}) collective-permute-start(bf16[256,1024]{1,0:T(8,128)(2,1)} %get-tuple-element.74.refs_1_), channel_id=1, source_target_pairs={{0,16},{4,20},{8,24},{12,28},{16,0},{20,4},{24,8},{28,12},{1,17},{... | collective-permute-start | bytes 1572872 | tf_op jit(solution)/shard_map/ppermute | solution.py:18
  221.5 3.8 %collective-permute-start.25 = (f32[2,1024]{1,0:T(2,128)S(1)}, f32[2,1024]{1,0:T(2,128)S(1)}, u32[]{:S(2)}, u32[]{:S(2)}) collective-permute-start(f32[2,1024]{1,0:T(2,128)S(1)} %pad_maximum_fusion.17), channel_id=1, source_target_pairs={{0,1},{1,0},{2,3},{3,2},{4,5},{5,4},{6,7},{7,6},{8,9},{9,8},{10,11... | collective-permute-start | bytes 24584 | tf_op jit(solution)/shard_map/ppermute | solution.py:18
  221.6 7.9 %collective-permute-start.26 = (f32[2,1024]{1,0:T(2,128)S(1)}, f32[2,1024]{1,0:T(2,128)S(1)}, u32[]{:S(2)}, u32[]{:S(2)}) collective-permute-start(f32[2,1024]{1,0:T(2,128)S(1)} %pad_maximum_fusion.17), channel_id=1, source_target_pairs={{0,2},{1,3},{2,0},{3,1},{4,6},{5,7},{6,4},{7,5},{8,10},{9,11},{10,... | collective-permute-start | bytes 24584 | tf_op jit(solution)/shard_map/ppermute | solution.py:18
  222.5 7.0 %collective-permute-start.27 = (f32[2,1024]{1,0:T(2,128)S(1)}, f32[2,1024]{1,0:T(2,128)S(1)}, u32[]{:S(2)}, u32[]{:S(2)}) collective-permute-start(f32[2,1024]{1,0:T(2,128)S(1)} %pad_maximum_fusion.17), channel_id=1, source_target_pairs={{0,3},{1,2},{2,1},{3,0},{4,7},{5,6},{6,5},{7,4},{8,11},{9,10},{10,... | collective-permute-start | bytes 24584 | tf_op jit(solution)/shard_map/ppermute | solution.py:18
  223.4 40.1 %collective-permute-start.28 = (bf16[256,1024]{1,0:T(8,128)(2,1)S(1)}, bf16[256,1024]{1,0:T(8,128)(2,1)S(1)}, u32[]{:S(2)}, u32[]{:S(2)}) collective-permute-start(bf16[256,1024]{1,0:T(8,128)(2,1)S(1)} %copy-done.23), channel_id=1, source_target_pairs={{0,16},{4,20},{8,24},{12,28},{16,0},{20,4},{24,8},{28,12},{1,17},{... | collective-permute-start | bytes 1572872 | tf_op jit(solution)/shard_map/ppermute | solution.py:18
  223.4 40.1 %collective-permute-start.30 = (bf16[256,1024]{1,0:T(8,128)(2,1)S(1)}, bf16[256,1024]{1,0:T(8,128)(2,1)S(1)}, u32[]{:S(2)}, u32[]{:S(2)}) collective-permute-start(bf16[256,1024]{1,0:T(8,128)(2,1)S(1)} %copy-done.23), channel_id=1, source_target_pairs={{0,4},{4,0},{8,12},{12,8},{16,20},{20,16},{24,28},{28,24},{1,5},{5... | collective-permute-start | bytes 1572872 | tf_op jit(solution)/shard_map/ppermute | solution.py:18
  225.3 38.2 %collective-permute-start.31 = (bf16[256,1024]{1,0:T(8,128)(2,1)S(1)}, bf16[256,1024]{1,0:T(8,128)(2,1)S(1)}, u32[]{:S(2)}, u32[]{:S(2)}) collective-permute-start(bf16[256,1024]{1,0:T(8,128)(2,1)S(1)} %copy-done.23), channel_id=1, source_target_pairs={{0,8},{4,12},{8,0},{12,4},{16,24},{20,28},{24,16},{28,20},{1,9},{5... | collective-permute-start | bytes 1572872 | tf_op jit(solution)/shard_map/ppermute | solution.py:18
  229.5 39.0 %collective-permute-start.32 = (bf16[256,1024]{1,0:T(8,128)(2,1)S(1)}, bf16[256,1024]{1,0:T(8,128)(2,1)S(1)}, u32[]{:S(2)}, u32[]{:S(2)}) collective-permute-start(bf16[256,1024]{1,0:T(8,128)(2,1)S(1)} %copy-done.23), channel_id=1, source_target_pairs={{0,12},{4,8},{8,4},{12,0},{16,28},{20,24},{24,20},{28,16},{1,13},{... | collective-permute-start | bytes 1572872 | tf_op jit(solution)/shard_map/ppermute | solution.py:18
  229.6 34.0 %collective-permute-start.29 = (bf16[256,512]{1,0:T(8,128)(2,1)S(1)}, bf16[256,512]{1,0:T(8,128)(2,1)S(1)}, u32[]{:S(2)}, u32[]{:S(2)}) collective-permute-start(bf16[256,512]{1,0:T(8,128)(2,1)S(1)} %copy-done.54), channel_id=1, source_target_pairs={{0,16},{4,20},{8,24},{12,28},{16,0},{20,4},{24,8},{28,12},{1,17},{... | collective-permute-start | bytes 786440 | tf_op jit(solution)/shard_map/ppermute | solution.py:18
  273.4 4.3 %collective-permute-start.34 = (bf16[1024,256]{1,0:T(8,128)(2,1)S(1)}, bf16[1024,256]{1,0:T(8,128)(2,1)S(1)}, u32[]{:S(2)}, u32[]{:S(2)}) collective-permute-start(bf16[1024,256]{1,0:T(8,128)(2,1)S(1)} %convolution_convert_fusion.2), channel_id=1, source_target_pairs={{0,1},{1,0},{2,3},{3,2},{4,5},{5,4},{6,7},{7,6},{8,9},{9,8},{10,11... | collective-permute-start | bytes 1572872 | tf_op jit(solution)/shard_map/ppermute | solution.py:18
  273.5 22.5 %collective-permute-start.37 = (bf16[256,1536]{1,0:T(8,128)(2,1)}, bf16[256,1536]{1,0:T(8,128)(2,1)S(1)}, u32[]{:S(2)}, u32[]{:S(2)}) collective-permute-start(bf16[256,1536]{1,0:T(8,128)(2,1)} %join_sum.1.refs_0_.refs_4_), channel_id=1, source_target_pairs={{0,8},{4,12},{8,0},{12,4},{16,24},{20,28},{24,16},{28,20},{1,9},{5... | collective-permute-start | bytes 2359304 | tf_op jit(solution)/shard_map/ppermute | solution.py:18
  274.7 22.7 %collective-permute-start.36 = (bf16[256,1536]{1,0:T(8,128)(2,1)}, bf16[256,1536]{1,0:T(8,128)(2,1)S(1)}, u32[]{:S(2)}, u32[]{:S(2)}) collective-permute-start(bf16[256,1536]{1,0:T(8,128)(2,1)} %join_sum.1.refs_0_.refs_4_), channel_id=1, source_target_pairs={{0,4},{4,0},{8,12},{12,8},{16,20},{20,16},{24,28},{28,24},{1,5},{5... | collective-permute-start | bytes 2359304 | tf_op jit(solution)/shard_map/ppermute | solution.py:18
  277.6 28.7 %collective-permute-start.33 = (bf16[1024,256]{1,0:T(8,128)(2,1)}, bf16[1024,256]{1,0:T(8,128)(2,1)}, u32[]{:S(2)}, u32[]{:S(2)}) collective-permute-start(bf16[1024,256]{1,0:T(8,128)(2,1)} %convolution_convert_fusion.3), channel_id=1, source_target_pairs={{0,1},{1,0},{2,3},{3,2},{4,5},{5,4},{6,7},{7,6},{8,9},{9,8},{10,11... | collective-permute-start | bytes 1572872 | tf_op jit(solution)/shard_map/ppermute | solution.py:18
  279.2 27.2 %collective-permute-start.35 = (bf16[1024,256]{1,0:T(8,128)(2,1)}, bf16[1024,256]{1,0:T(8,128)(2,1)}, u32[]{:S(2)}, u32[]{:S(2)}) collective-permute-start(bf16[1024,256]{1,0:T(8,128)(2,1)} %fusion.44), channel_id=1, source_target_pairs={{0,2},{1,3},{2,0},{3,1},{4,6},{5,7},{6,4},{7,5},{8,10},{9,11},{10,... | collective-permute-start | bytes 1572872 | tf_op jit(solution)/shard_map/ppermute | solution.py:18
  280.1 18.4 %all-to-all-start.4 = ((bf16[8,112,128]{2,1,0:T(8,128)(2,1)}), bf16[8,112,128]{2,1,0:T(8,128)(2,1)S(1)}, u32[]{:S(2)}, u32[]{:S(2)}) async-start(bf16[8,112,128]{2,1,0:T(8,128)(2,1)} %pack_small.1.refs_0_), calls=%async_computation.4 | async-start | bytes 458752 | tf_op jit(solution)/shard_map/all_to_all | solution.py:59
  296.8 13.1 %collective-permute-start.38 = (bf16[128,1536]{1,0:T(8,128)(2,1)}, bf16[128,1536]{1,0:T(8,128)(2,1)}, u32[]{:S(2)}, u32[]{:S(2)}) collective-permute-start(bf16[128,1536]{1,0:T(8,128)(2,1)} %slice.134), channel_id=1, source_target_pairs={{0,4},{4,0},{8,12},{12,8},{16,20},{20,16},{24,28},{28,24},{1,5},{5... | collective-permute-start | bytes 1179656 | tf_op jit(solution)/shard_map/ppermute | solution.py:18
  298.2 12.8 %collective-permute-start.39 = (bf16[128,1536]{1,0:T(8,128)(2,1)}, bf16[128,1536]{1,0:T(8,128)(2,1)}, u32[]{:S(2)}, u32[]{:S(2)}) collective-permute-start(bf16[128,1536]{1,0:T(8,128)(2,1)} %slice.135), channel_id=1, source_target_pairs={{0,8},{4,12},{8,0},{12,4},{16,24},{20,28},{24,16},{28,20},{1,9},{5... | collective-permute-start | bytes 1179656 | tf_op jit(solution)/shard_map/ppermute | solution.py:18
  300.9 13.5 %all-to-all-start.5 = ((bf16[8,112,128]{2,1,0:T(8,128)(2,1)}), bf16[8,112,128]{2,1,0:T(8,128)(2,1)S(1)}, u32[]{:S(2)}, u32[]{:S(2)}) async-start(bf16[8,112,128]{2,1,0:T(8,128)(2,1)} %sum_small.1), calls=%async_computation.5 | async-start | bytes 458752 | tf_op jit(solution)/shard_map/all_to_all | solution.py:59
  317.3 28.0 %all-to-all-start.6 = ((bf16[8,128,512]{2,1,0:T(8,128)(2,1)}), bf16[8,128,512]{2,1,0:T(8,128)(2,1)S(1)}, u32[]{:S(2)}, u32[]{:S(2)}) async-start(bf16[8,128,512]{2,1,0:T(8,128)(2,1)} %bitcast.62), calls=%async_computation.6 | async-start | bytes 2097152 | tf_op jit(solution)/shard_map/all_to_all | solution.py:865
  (79 other events, 447.0 us)
